TPU v7x, 32 devices: a whole 2x2x4 slice. The times are simulated.
32 devices in a mesh: dp: 16 (over z, x, core), outer: 2 (over y).
Axes of the slice: x: 2, y: 2, z: 4, core: 2. Of those that a mesh axis runs over, the one named last changes fastest.
Arguments:
- patches: bfloat16 [128, 256, 768], P(('dp', 'outer')), may hold values from -6 to 6
- lengths: int32 [128], P(('dp', 'outer')), may hold values from 64 to 256, as said below
- leads: int32 [128], P(('dp', 'outer')), may hold values from 0 to 39
- counts: int32 [32], P(('dp', 'outer')), may hold values from 1 to 4, as said below
- cotangent: bfloat16 [128, 256, 768], P(('dp', 'outer')), may hold values from -6 to 6
- norm1_gain: float32 [768], replicated, may hold values from 0.5 to 1.5
- norm1_bias: float32 [768], replicated, may hold values from -1.75 to 1.75
- lead_table: float32 [40, 768], replicated, may hold values from -3 to 3
- w_qkv: bfloat16 [768, 2304], replicated, may hold values from -0.21875 to 0.21875
- bias_query: float32 [768], replicated, may hold values from -1.75 to 1.75
- bias_value: float32 [768], replicated, may hold values from -1.75 to 1.75
- w_out: bfloat16 [768, 768], replicated, may hold values from -0.625 to 0.625
- bias_out: float32 [768], replicated, may hold values from -1.75 to 1.75
- norm2_gain: float32 [768], replicated, may hold values from 0.5 to 1.5
- norm2_bias: float32 [768], replicated, may hold values from -1.75 to 1.75
- w_up: bfloat16 [768, 3072], replicated, may hold values from -0.21875 to 0.21875
- bias_up: float32 [3072], replicated, may hold values from -1.75 to 1.75
- w_down: bfloat16 [3072, 768], replicated, may hold values from -0.109375 to 0.109375
- bias_down: float32 [768], replicated, may hold values from -1.75 to 1.75
Outputs:
- block_out: bfloat16 [128, 256, 768], P(('dp', 'outer'))
- grad_patches: bfloat16 [128, 256, 768], P(('dp', 'outer'))
- grad_norm1_gain: float32 [768], replicated
- grad_norm1_bias: float32 [768], replicated
- grad_lead_table: float32 [40, 768], replicated
- grad_w_qkv: float32 [768, 2304], P('dp')
- grad_bias_query: float32 [768], replicated
- grad_bias_value: float32 [768], replicated
- grad_w_out: float32 [768, 768], P('dp')
- grad_bias_out: float32 [768], replicated
- grad_norm2_gain: float32 [768], replicated
- grad_norm2_bias: float32 [768], replicated
- grad_w_up: float32 [768, 3072], P('dp')
- grad_bias_up: float32 [3072], replicated
- grad_w_down: float32 [3072, 768], P('dp')
- grad_bias_down: float32 [768], replicated
Inputs may be any that keep to these rules, and one draw needn't show every extreme that they name: `lengths`: some window is full and some has 64 real patches. `counts`: a device's live windows are its first slots; some device has all 4 live and some one.
All inputs are finite; a program needn't handle non-finite values.
Results may differ from a plain program's by a relative error of at most 0.012.
The roundings to bfloat16 on the way count: a program that leaves them out, or rounds other values in their place, can miss the bound.
Values sent between devices are 32-bit elements; how exact they have to be, the bound alone decides.
No kernel may reach another device: no remote copies, remote signals or barrier semaphores. Data moves between devices by JAX's collectives and lax.ppermute only.
A program may use at most 192 MiB of HBM per device.

v0:
```python
import jax
import jax.numpy as jnp
from jax import lax
from jax.sharding import PartitionSpec as P

HEADS = 12


norm_epsilon = 1e-05
masked_score = -1e30


def layer_norm(values_in, norm_gain, norm_bias):
    centre = jnp.mean(values_in, axis=-1, keepdims=True)
    centred = values_in - centre
    spread = jnp.mean(centred * centred, axis=-1, keepdims=True)
    return centred * lax.rsqrt(spread + norm_epsilon) * norm_gain + norm_bias


def exact_gelu(pre_values):
    return jax.nn.gelu(pre_values, approximate=False)


def reduce_matrices(matrices):
    row_parts = lax.axis_size("dp")
    widths = [m.shape[0] * m.shape[1] // row_parts for m in matrices]
    buffer = jnp.concatenate([m.reshape(row_parts, -1) for m in matrices], axis=1)
    mine = lax.psum_scatter(buffer, "dp", scatter_dimension=0, tiled=True)
    share = lax.psum(mine, "outer")
    results = []
    offset = 0
    for matrix, width in zip(matrices, widths):
        piece = share[0, offset : offset + width]
        results.append(piece.reshape(matrix.shape[0] // row_parts, matrix.shape[1]))
        offset = offset + width
    return tuple(results)


def per_device(
    patches,
    lengths,
    leads,
    counts,
    cotangent,
    norm1_gain,
    norm1_bias,
    lead_table,
    w_qkv,
    bias_query,
    bias_value,
    w_out,
    bias_out,
    norm2_gain,
    norm2_bias,
    w_up,
    bias_up,
    w_down,
    bias_down,
):
    slot_count, window_len, model_width = patches.shape
    row_count = slot_count * window_len
    head_dim = model_width // HEADS
    lead_count = lead_table.shape[0]
    precise = lax.Precision.HIGHEST
    valid_keys = jnp.arange(window_len, dtype=jnp.int32)[None, :] < lengths[:, None]
    live_slots = jnp.arange(slot_count, dtype=jnp.int32) < counts[0]
    onehot = (leads[:, None] == jnp.arange(lead_count, dtype=jnp.int32)[None, :]).astype(
        jnp.float32
    )
    local_hist = jnp.sum(onehot * live_slots[:, None].astype(jnp.float32), axis=0)
    lead_totals = lax.psum(local_hist, ("dp", "outer"))
    window_total = jnp.sum(onehot * lead_totals[None, :], axis=1)
    window_scale = jnp.where(live_slots, 1.0 / jnp.maximum(window_total, 1.0), 0.0)
    lead_rows = jnp.dot(onehot, lead_table, precision=precise, preferred_element_type=jnp.float32)
    inputs = patches.astype(jnp.float32)

    def first_norm(inputs_in, norm_gain, norm_bias, lead_part):
        return layer_norm(inputs_in, norm_gain, norm_bias) + lead_part[:, None, :]

    normed, first_back = jax.vjp(first_norm, inputs, norm1_gain, norm1_bias, lead_rows)
    normed_low = normed.astype(jnp.bfloat16).reshape(row_count, model_width)
    projected = jnp.dot(normed_low, w_qkv, preferred_element_type=jnp.float32)
    shape_heads = (slot_count, window_len, HEADS, head_dim)
    queries = (projected[:, :model_width] + bias_query).astype(jnp.bfloat16).reshape(shape_heads)
    keys_low = projected[:, model_width : 2 * model_width].astype(jnp.bfloat16).reshape(shape_heads)
    values_low = (
        (projected[:, 2 * model_width :] + bias_value).astype(jnp.bfloat16).reshape(shape_heads)
    )
    key_mask = valid_keys[:, None, None, :]

    def compute_scores():
        raw_scores = jnp.einsum(
            "swhd,sthd->shwt", queries, keys_low, preferred_element_type=jnp.float32
        )
        return jnp.where(key_mask, raw_scores * 0.125, masked_score)

    scores = compute_scores()
    row_max = jnp.max(scores, axis=-1, keepdims=True)
    exponent = jnp.exp(scores - row_max)
    row_total = jnp.sum(exponent, axis=-1, keepdims=True)
    probs_low = (exponent / row_total).astype(jnp.bfloat16)
    log_total = row_max + jnp.log(row_total)
    attended = jnp.einsum(
        "shwt,sthd->swhd", probs_low, values_low, preferred_element_type=jnp.float32
    )
    attended_low = attended.astype(jnp.bfloat16).reshape(row_count, model_width)
    branch = jnp.dot(attended_low, w_out, preferred_element_type=jnp.float32) + bias_out
    residual = inputs.reshape(row_count, model_width) + branch

    def second_norm(residual_in, norm_gain, norm_bias):
        return layer_norm(residual_in, norm_gain, norm_bias)

    normed2, second_back = jax.vjp(second_norm, residual, norm2_gain, norm2_bias)
    normed2_low = normed2.astype(jnp.bfloat16)
    pre_up = jnp.dot(normed2_low, w_up, preferred_element_type=jnp.float32) + bias_up
    activated, gelu_back = jax.vjp(exact_gelu, pre_up)
    activated_low = activated.astype(jnp.bfloat16)
    final = (
        residual + jnp.dot(activated_low, w_down, preferred_element_type=jnp.float32) + bias_down
    )
    block_out = final.astype(jnp.bfloat16).reshape(slot_count, window_len, model_width)
    weighting = (window_scale[:, None] * valid_keys.astype(jnp.float32))[:, :, None]
    grad_out = (cotangent.astype(jnp.float32) * weighting).reshape(row_count, model_width)
    grad_down = grad_out.astype(jnp.bfloat16)
    grad_w_down = jnp.einsum(
        "rf,rd->fd", activated_low, grad_down, preferred_element_type=jnp.float32
    )
    grad_bias_down = jnp.sum(grad_down.astype(jnp.float32), axis=0)
    grad_act = jnp.einsum("rd,fd->rf", grad_down, w_down, preferred_element_type=jnp.float32)
    grad_pre_up = gelu_back(grad_act)[0]
    grad_up = grad_pre_up.astype(jnp.bfloat16)
    grad_w_up = jnp.einsum("rd,rf->df", normed2_low, grad_up, preferred_element_type=jnp.float32)
    grad_bias_up = jnp.sum(grad_up.astype(jnp.float32), axis=0)
    grad_normed2 = jnp.einsum("rf,df->rd", grad_up, w_up, preferred_element_type=jnp.float32)
    grad_resid_norm, grad_norm2_gain, grad_norm2_bias = second_back(grad_normed2)
    grad_residual = grad_out + grad_resid_norm
    grad_branch = grad_residual.astype(jnp.bfloat16)
    grad_w_out = jnp.einsum(
        "re,rd->ed", attended_low, grad_branch, preferred_element_type=jnp.float32
    )
    grad_bias_out = jnp.sum(grad_branch.astype(jnp.float32), axis=0)
    grad_attended = jnp.einsum("rd,ed->re", grad_branch, w_out, preferred_element_type=jnp.float32)
    grad_attended = grad_attended.astype(jnp.bfloat16).reshape(shape_heads)
    probs_again = jnp.exp(compute_scores() - log_total)
    probs_again_low = probs_again.astype(jnp.bfloat16)
    grad_probs = jnp.einsum(
        "swhd,sthd->shwt", grad_attended, values_low, preferred_element_type=jnp.float32
    )
    grad_values = jnp.einsum(
        "shwt,swhd->sthd", probs_again_low, grad_attended, preferred_element_type=jnp.float32
    )
    grad_scores = probs_again * (
        grad_probs - jnp.sum(grad_probs * probs_again, axis=-1, keepdims=True)
    )
    grad_scores_low = grad_scores.astype(jnp.bfloat16)
    grad_queries = (
        jnp.einsum("shwt,sthd->swhd", grad_scores_low, keys_low, preferred_element_type=jnp.float32)
        * 0.125
    )
    grad_keys = (
        jnp.einsum("shwt,swhd->sthd", grad_scores_low, queries, preferred_element_type=jnp.float32)
        * 0.125
    )
    grad_projected = jnp.concatenate(
        [
            grad_queries.reshape(row_count, model_width).astype(jnp.bfloat16),
            grad_keys.reshape(row_count, model_width).astype(jnp.bfloat16),
            grad_values.reshape(row_count, model_width).astype(jnp.bfloat16),
        ],
        axis=1,
    )
    grad_w_qkv = jnp.einsum(
        "rd,re->de", normed_low, grad_projected, preferred_element_type=jnp.float32
    )
    grad_bias_query = jnp.sum(grad_projected[:, :model_width].astype(jnp.float32), axis=0)
    grad_bias_value = jnp.sum(grad_projected[:, 2 * model_width :].astype(jnp.float32), axis=0)
    grad_normed = jnp.einsum("re,de->rd", grad_projected, w_qkv, preferred_element_type=jnp.float32)
    grad_normed = grad_normed.reshape(slot_count, window_len, model_width)
    grad_inputs_norm, grad_norm1_gain, grad_norm1_bias, grad_lead_rows = first_back(grad_normed)
    grad_lead_table = jnp.einsum("sl,sd->ld", onehot, grad_lead_rows, precision=precise)
    grad_patches = (
        grad_residual.reshape(slot_count, window_len, model_width) + grad_inputs_norm
    ).astype(jnp.bfloat16)
    small = lax.psum(
        (
            grad_norm1_gain,
            grad_norm1_bias,
            grad_lead_table,
            grad_bias_query,
            grad_bias_value,
            grad_bias_out,
            grad_norm2_gain,
            grad_norm2_bias,
            grad_bias_up,
            grad_bias_down,
        ),
        ("dp", "outer"),
    )
    sum_qkv, sum_out, sum_up, sum_down = reduce_matrices(
        (grad_w_qkv, grad_w_out, grad_w_up, grad_w_down)
    )
    return (
        block_out,
        grad_patches,
        small[0],
        small[1],
        small[2],
        sum_qkv,
        small[3],
        small[4],
        sum_out,
        small[5],
        small[6],
        small[7],
        sum_up,
        small[8],
        sum_down,
        small[9],
    )


def solution(mesh):
    placed = (
        P(("dp", "outer"), None, None),
        P(("dp", "outer")),
        P(("dp", "outer")),
        P(("dp", "outer")),
        P(("dp", "outer"), None, None),
        P(),
        P(),
        P(),
        P(),
        P(),
        P(),
        P(),
        P(),
        P(),
        P(),
        P(),
        P(),
        P(),
        P(),
    )
    return jax.shard_map(
        per_device,
        mesh=mesh,
        in_specs=placed,
        out_specs=(
            P(("dp", "outer"), None, None),
            P(("dp", "outer"), None, None),
            P(),
            P(),
            P(),
            P("dp", None),
            P(),
            P(),
            P("dp", None),
            P(),
            P(),
            P(),
            P("dp", None),
            P(),
            P("dp", None),
            P(),
        ),
        check_vma=False,
    )
```

profile of v0, /device:TPU:0, one launch (start us, length us, event | category | flops | bytes accessed | tf_op | source)
XLA Modules:
  0.0 994.3 jit_solution(7107486746560884115)
XLA Ops:
  8.9 42.0 %psum.84 = f32[40]{0:T(128)S(1)} all-reduce(f32[40]{0:T(128)S(1)} %select_reduce_fusion.1), channel_id=1, replica_groups=mesh['dp'=16,'outer'=2] {'dp','outer'}, use_global_device_ids=true, to_apply=%region_7.8 | all-reduce | flops 40 | bytes 320 | tf_op jit(solution)/shard_map/psum | solution.py:71
  53.4 1.7 convert_reduce_fusion.5
  55.1 2.0 multiply_reduce_fusion.6
  58.9 1.3 bitcast_convert_fusion
  60.2 1.2 copy-done.2
  61.4 1.0 add_convert_fusion.4
  62.5 3.8 fusion.51
  66.3 1.3 slice.47
  67.6 2.3 fusion.14
  69.9 2.6 copy.87
  72.5 3.8 reshape.237
  76.4 2.6 copy.89
  79.0 3.9 reshape.239
  82.8 2.6 copy.88
  85.4 3.8 reshape.238
  89.2 4.8 fusion.12
  94.1 4.1 fusion.6
  98.9 3.4 fusion.19
  102.3 1.2 copy.94
  104.0 1.7 fusion.49
  107.2 35.2 %multiply_convert_fusion.1 = (bf16[1024,3072]{1,0:T(8,128)(2,1)}, f32[1024,3072]{1,0:T(8,128)}, f32[1024,3072]{1,0:T(8,128)}) fusion(f32[3072]{0:T(1024)S(1)} %copy-done.46, bf16[768,3072]{1,0:T(8,128)(2,1)S(1)} %bitcast.94, f32[1024,768]{1,0:T(8,128)S(1)} %get-tuple-element.46, f32[768]{0:T(1024)S(1)} %copy-done.36, f32[768]{0:T(1024)S(1)} %copy-done.35, ...), kind=kOutput, calls=%fused_computation.8 | convolution fusion | flops 5043388416 | bytes 39348224 | tf_op jit(solution)/shard_map/dot_general | solution.py:115
  142.5 19.0 %convert_reduce_fusion = (f32[3072]{0:T(1024)}, bf16[1024,3072]{1,0:T(8,128)(2,1)}) fusion(f32[1024,3072]{1,0:T(8,128)} %get-tuple-element.38, bf16[1024,768]{1,0:T(8,128)(2,1)} %bitcast_convert_fusion, bf16[3072,768]{1,0:T(8,128)(2,1)} %param.36, f32[1024,3072]{1,0:T(8,128)} %get-tuple-element.47, f32[3072]{0:T(1024)S(1)} %copy-done.46), kind=kOutput, calls=%fused_computation.3 | convolution fusion | flops 4885312512 | bytes 37773312 | tf_op jit(solution)/shard_map/rd,fd->rf/dot_general | solution.py:129
  161.5 9.9 multiply_reduce_fusion.1
  171.4 8.4 fusion.45
  179.9 1.9 fusion.47
  181.8 1.0 convert_reduce_fusion.2
  183.2 2.8 fusion.38
  186.0 2.6 convolution_convert_fusion
  188.6 2.6 copy.95
  191.2 3.9 reshape.244
  195.1 10.1 %convert_reduce_fusion.3 = (f32[12,64]{1,0:T(8,128)}, bf16[4,12,64,256]{3,2,1,0:T(8,128)(2,1)}) fusion(f32[4,12,256]{2,1,0:T(8,128)} %log_add_fusion, f32[4,12,256,256]{2,3,1,0:T(8,128)} %copy-done.1, pred[4,256]{1,0:T(4,128)(4,1)S(1)} %copy-done.30, bf16[4,256,12,64]{1,0,3,2:T(4,128)(2,1)} %reshape.244), kind=kOutput, calls=%fused_computation.45 | convolution fusion | flops 417594624 | bytes 15781888 | tf_op jit(solution)/shard_map/shwt,swhd->sthd/dot_general | solution.py:149
  205.2 10.2 %multiply_reduce_fusion = (f32[4,12,256]{2,1,0:T(8,128)S(1)}, f32[4,12,256,256]{2,3,1,0:T(8,128)}) fusion(f32[4,12,256]{2,1,0:T(8,128)S(1)} %copy-done.24, f32[4,12,256,256]{2,3,1,0:T(8,128)} %copy-done.1, pred[4,256]{1,0:T(4,128)(4,1)S(1)} %copy-done.30, bf16[4,256,12,64]{1,0,3,2:T(4,128)(2,1)S(1)} %copy-done.13, bf16[4,256,12,64]{1,0,3,2:T(4,128)(2,1)S(1)} %copy-done.14), kind=kOutput, calls=%fused_computation.5 | convolution fusion | flops 418369536 | bytes 28410880 | tf_op jit(solution)/shard_map/swhd,sthd->shwt/dot_general | solution.py:146
  215.5 8.2 multiply_convert_fusion
  223.7 3.2 fusion.20
  226.9 3.0 convert_reduce_fusion.4
  229.8 10.1 %fusion.53 = f32[3072,768]{1,0:T(8,128)} fusion(bf16[1024,3072]{1,0:T(8,128)(2,1)} %get-tuple-element.37, bf16[1024,768]{1,0:T(8,128)(2,1)S(1)} %copy-done.23), kind=kOutput, calls=%fused_computation.120 | convolution fusion | flops 4831838208 | bytes 17301504 | tf_op jit(solution)/shard_map/rf,rd->fd/dot_general | solution.py:125
  239.9 10.7 %reshape.249 = f32[16,147456]{1,0:T(8,128)} reshape(f32[3072,768]{1,0:T(8,128)} %fusion.53) | data formatting | bytes 18874368 | tf_op jit(solution)/shard_map/reshape | solution.py:27
  250.6 10.7 %reshape.248 = f32[16,147456]{1,0:T(8,128)} reshape(f32[768,3072]{1,0:T(8,128)} %fusion.45) | data formatting | bytes 18874368 | tf_op jit(solution)/shard_map/reshape | solution.py:27
  261.3 3.0 reshape.247
  264.3 2.8 copy.106
  267.4 1.2 copy.100
  269.0 1.2 copy.103
  271.0 2.1 copy-done.25
  273.2 6.2 fusion.52
  279.4 5.5 reshape.246
  284.9 25.7 %pad_maximum_fusion = f32[16,442368]{1,0:T(8,128)} fusion(f32[16,147456]{1,0:T(8,128)} %reshape.249, f32[16,147456]{1,0:T(8,128)} %reshape.248, f32[16,36864]{1,0:T(8,128)} %reshape.247, f32[16,110592]{1,0:T(8,128)} %reshape.246), kind=kLoop, calls=%fused_computation | loop fusion | flops 21233664 | bytes 56623104 | tf_op jit(solution)/shard_map/concatenate | solution.py:27
  311.8 482.7 %all-reduce.10.cloned.1.call-done = f32[16,442368]{1,0:T(8,128)} async-done(((f32[16,442368]{1,0:T(8,128)}), f32[16,442368]{1,0:T(8,128)}) %all-reduce.10.cloned.1.call-update) | async-done | bytes 28311568
  794.5 7.5 constant_dynamic-slice_fusion
  802.1 6.5 fusion.50
  809.5 2.4 bitcast_reduce_fusion
  812.9 10.0 %add_convert_fusion.2 = bf16[1024,768]{1,0:T(8,128)(2,1)} fusion(f32[1024,768]{1,0:T(8,128)} %copy-done.6, bf16[1024,3072]{1,0:T(8,128)(2,1)} %get-tuple-element.37, bf16[3072,768]{1,0:T(8,128)(2,1)} %param.36, f32[768]{0:T(1024)} %param.37), kind=kOutput, calls=%fused_computation.54 | convolution fusion | flops 4834197504 | bytes 15731712 | tf_op jit(solution)/shard_map/dot_general | solution.py:119
  822.9 1.4 reduce_sum.256
  824.2 1.4 reduce_sum.254
  826.3 4.7 add_convert_fusion.1
  831.0 42.7 %all-reduce.1 = (f32[768]{0:T(1024)}, f32[768]{0:T(1024)}, f32[768]{0:T(1024)}, f32[768]{0:T(1024)}, f32[768]{0:T(1024)}, /*index=5*/f32[768]{0:T(1024)}, f32[768]{0:T(1024)}, f32[3072]{0:T(1024)}, f32[768]{0:T(1024)}) all-reduce(f32[768]{0:T(1024)} %get-tuple-element.20, ...), channel_id=1, replica_groups=mesh['dp'=16,'outer'=2] {'dp','outer'}, use_global_device_ids=true, to_apply=%region_15.16 | all-reduce | flops 9216 | bytes 73728 | tf_op jit(solution)/shard_map/psum | solution.py:184
  873.7 2.9 slice_reduce_fusion.2
  876.6 8.2 slice_reduce_fusion
  884.8 1.9 slice_reduce_fusion.3
  886.8 1.6 reshape_squeeze.13
  888.4 2.0 reshape_squeeze.15
  890.4 1.8 reshape_squeeze.12
  892.2 2.0 reshape_squeeze.14
  894.2 91.6 %all-reduce.6.cloned.1.call-done = f32[40,768]{1,0:T(8,128)} async-done(((f32[40,768]{1,0:T(8,128)}), f32[40,768]{1,0:T(8,128)}) %all-reduce.6.cloned.1.call-update) | async-done | bytes 122896 | tf_op jit(solution)/shard_map/psum | solution.py:184
  985.8 1.6 copy.149
  (143 shorter events, 13.5 us)
Async XLA Ops:
  7.2 55.3 %copy-start = (bf16[768,2304]{1,0:T(8,128)(2,1)S(1)}, bf16[768,2304]{1,0:T(8,128)(2,1)}, u32[]{:S(2)}) copy-start(bf16[768,2304]{1,0:T(8,128)(2,1)} %param.27) | copy-start | bytes 10616836
  7.2 50.5 %copy-start.42 = (s32[4]{0:T(128)S(1)}, s32[4]{0:T(128)}, u32[]{:S(2)}) copy-start(s32[4]{0:T(128)} %param.21) | copy-start | bytes 52
  7.2 787.3 %all-reduce.10.cloned.1.call-start = ((), (), s32[]{:S(2)}) async-start(), calls=%async_computation.2 | async-start | bytes 56623104
  50.9 6.7 copy-start.28
  50.9 6.9 copy-start.22
  52.6 46.2 %copy-start.29 = (pred[4,256]{1,0:T(4,128)(4,1)}, pred[4,256]{1,0:T(4,128)(4,1)S(1)}, u32[]{:S(2)}) copy-start(pred[4,256]{1,0:T(4,128)(4,1)S(1)} %iota_compare_fusion) | copy-start | bytes 3076
  55.1 5.1 copy-start.26
  57.1 0.6 copy-start.37
  57.7 2.5 copy-start.31
  58.9 3.6 copy-start.7
  58.9 2.5 copy-start.2
  58.9 2.5 copy-start.33
  58.9 2.5 copy-start.39
  62.4 3.9 copy-start.18
  66.3 1.3 copy-start.40
  66.3 1.3 copy-start.41
  94.1 4.8 copy-start.1
  94.1 4.8 copy-start.12
  102.3 1.7 copy-start.3
  102.3 1.7 copy-start.44
  102.3 1.7 copy-start.47
  103.9 1.8 copy-start.20
  103.9 2.8 slice-start.3
  104.0 3.1 slice-start.4
  105.7 74.1 %copy-start.6 = (f32[1024,768]{1,0:T(8,128)}, f32[1024,768]{1,0:T(8,128)S(1)}, u32[]{:S(2)}) copy-start(f32[1024,768]{1,0:T(8,128)S(1)} %get-tuple-element.46) | copy-start | bytes 9437188
  105.7 1.4 copy-start.35
  105.7 1.5 copy-start.36
  105.7 1.5 copy-start.46
  161.5 9.9 copy-start.16
  179.8 1.9 copy-start.8
  181.8 1.4 copy-start.21
  182.8 3.2 copy-start.11
  183.2 2.8 copy-start.45
  188.6 6.5 copy-start.30
  195.1 10.1 %copy-start.13 = (bf16[4,256,12,64]{1,0,3,2:T(4,128)(2,1)S(1)}, bf16[4,256,12,64]{1,0,3,2:T(4,128)(2,1)}, u32[]{:S(2)}) copy-start(bf16[4,256,12,64]{1,0,3,2:T(4,128)(2,1)} %reshape.237) | copy-start | bytes 4718596
  195.1 10.1 %copy-start.14 = (bf16[4,256,12,64]{1,0,3,2:T(4,128)(2,1)S(1)}, bf16[4,256,12,64]{1,0,3,2:T(4,128)(2,1)}, u32[]{:S(2)}) copy-start(bf16[4,256,12,64]{1,0,3,2:T(4,128)(2,1)} %reshape.244) | copy-start | bytes 4718596
  195.1 10.1 %copy-start.24 = (f32[4,12,256]{2,1,0:T(8,128)S(1)}, f32[4,12,256]{2,1,0:T(8,128)}, u32[]{:S(2)}) copy-start(f32[4,12,256]{2,1,0:T(8,128)} %log_add_fusion) | copy-start | bytes 147460
  195.1 20.3 %slice-start = ((s8[12582912]{0:T(1024)(128)(4,1)}), s8[4194304]{0:T(1024)(128)(4,1)S(1)}, s32[]{:S(2)}) async-start(s8[12582912]{0:T(1024)(128)(4,1)} %bitcast.75), calls=%async_computation.3 | async-start | bytes 8388608
  205.2 10.2 %slice-start.1 = ((s8[12582912]{0:T(1024)(128)(4,1)}), s8[4194304]{0:T(1024)(128)(4,1)S(1)}, s32[]{:S(2)}) async-start(s8[12582912]{0:T(1024)(128)(4,1)} %bitcast.75), calls=%async_computation.4 | async-start | bytes 8388608
  205.2 10.2 %slice-start.2 = ((s8[12582912]{0:T(1024)(128)(4,1)}), s8[4194304]{0:T(1024)(128)(4,1)S(1)}, s32[]{:S(2)}) async-start(s8[12582912]{0:T(1024)(128)(4,1)} %bitcast.75), calls=%async_computation.5 | async-start | bytes 8388608
  215.4 8.2 copy-start.9
  223.7 3.2 copy-start.10
  226.9 3.0 copy-start.23
  264.3 3.1 copy-start.17
  267.4 1.6 copy-start.15
  270.7 2.4 copy-start.19
  271.0 2.2 copy-start.25
  310.6 0.7 copy-start.48
  310.6 563.1 %all-reduce.8.cloned.1.call-start = ((), (), s32[]{:S(2)}) async-start(), calls=%async_computation.1 | async-start | bytes 3538944 | tf_op jit(solution)/shard_map/psum | solution.py:29
  802.0 6.6 copy-start.27
  802.0 6.6 copy-start.34
  802.1 183.8 %all-reduce.6.cloned.1.call-start = ((), (), s32[]{:S(2)}) async-start(), calls=%async_computation | async-start | bytes 245760 | tf_op jit(solution)/shard_map/psum | solution.py:184
  802.1 6.5 copy-start.4
  808.6 3.3 copy-start.5
  808.6 0.8 copy-start.38
  808.6 0.9 copy-start.32
  809.5 2.4 copy-start.43
Sparse Core Ops, SparseCore 0:
  310.7 483.7 all-reduce.9
  802.2 56.5 all-reduce.7
  864.9 120.9 all-reduce.5
where the time goes:
time: 1000 us; the launch traced here: 994 us
  waiting for transfers between devices  574 us (57%)
  matrix products  152 us (15%)
  local copies, waits for them, and re-layouts  104 us (10%)
  blocking collectives  84.6 us (8%)
  other arithmetic  63.3 us (6%)
  between operations  15.6 us (2%)
    unnamed x4, waiting for transfers between devices  483 us
    psum x1, waiting for transfers between devices, per_device(): lax.psum((grad_norm1_gain, grad_norm1_bias, grad_lead_table, grad_bias_qu...  91.6 us
    psum x1, blocking collectives, per_device(): lax.psum((grad_norm1_gain, grad_norm1_bias, grad_lead_table, grad_bias_qu...  42.7 us
    psum x1, blocking collectives, per_device(): lead_totals = lax.psum(local_hist, ('dp', 'outer'))  42 us
    dot_general x1, matrix products, per_device(): jnp.dot(normed2_low, w_up, preferred_element_type=jnp.float32) + bias_up  35.2 us
    reshape x4, local copies, waits for them, and re-layouts, reduce_matrices(): m.reshape(row_parts, -1)  29.9 us
    concatenate x1, other arithmetic, reduce_matrices(): jnp.concatenate([m.reshape(row_parts, -1) for m in matrices], axis=1)  25.7 us
  transfers between devices with their start and end apart: 3, of which 2 were waited for; matrix products, arithmetic and copies ran while one was open for 5% of the time, Pallas kernels for 0%

commit v1 on v0

--- a/solution.py
+++ b/solution.py
@@ -21,19 +21,63 @@
     return jax.nn.gelu(pre_values, approximate=False)
 
 
-def reduce_matrices(matrices):
-    row_parts = lax.axis_size("dp")
-    widths = [m.shape[0] * m.shape[1] // row_parts for m in matrices]
-    buffer = jnp.concatenate([m.reshape(row_parts, -1) for m in matrices], axis=1)
-    mine = lax.psum_scatter(buffer, "dp", scatter_dimension=0, tiled=True)
-    share = lax.psum(mine, "outer")
-    results = []
-    offset = 0
-    for matrix, width in zip(matrices, widths):
-        piece = share[0, offset : offset + width]
-        results.append(piece.reshape(matrix.shape[0] // row_parts, matrix.shape[1]))
-        offset = offset + width
-    return tuple(results)
+def swap(values, axis, bit):
+    size = lax.axis_size(axis)
+    return lax.ppermute(values, axis, [(i, i ^ (1 << bit)) for i in range(size)])
+
+
+def bit_of(axis, bit):
+    return lax.rem(lax.div(lax.axis_index(axis), 1 << bit), 2)
+
+
+def dp_bits():
+    return lax.axis_size("dp").bit_length() - 1
+
+
+def sum_small(values):
+    for bit in range(dp_bits()):
+        values = values + swap(values, "dp", bit)
+    return values + swap(values, "outer", 0)
+
+
+def part_orders(bit_count):
+    rest = list(range(3, bit_count))
+    return (
+        [("dp", 1), ("outer", 0), ("dp", 2)] + [("dp", b) for b in rest],
+        [("outer", 0), ("dp", 2), ("dp", 1)] + [("dp", b) for b in rest],
+        [("dp", 2), ("dp", 1), ("outer", 0)] + [("dp", b) for b in rest],
+    )
+
+
+def halve(values, dims, step):
+    axis, bit = step
+    place = dims.index(step)
+    mine = bit_of(axis, bit)
+    keep = lax.dynamic_index_in_dim(values, mine, place, keepdims=False)
+    send = lax.dynamic_index_in_dim(values, 1 - mine, place, keepdims=False)
+    left = dims[:place] + dims[place + 1 :]
+    return keep + swap(send, axis, bit), left
+
+
+def scatter_sum(matrix):
+    bit_count = dp_bits()
+    rows, columns = matrix.shape
+    share = rows // lax.axis_size("dp")
+    dims = [("dp", b) for b in range(bit_count - 1, -1, -1)] + [("outer", 0)]
+    values = matrix.reshape((2,) * bit_count + (2, share // 2, columns))
+    values, dims = halve(values, dims, ("dp", 0))
+    third = columns // 3
+    pieces = []
+    for index, order in enumerate(part_orders(bit_count)):
+        part = lax.slice_in_dim(values, index * third, (index + 1) * third, axis=values.ndim - 1)
+        left = dims
+        for step in order:
+            part, left = halve(part, left, step)
+        pieces.append(part)
+    mine = jnp.concatenate(pieces, axis=1)
+    other = swap(mine, "outer", 0)
+    first = lax.axis_index("outer") == 0
+    return jnp.concatenate([jnp.where(first, mine, other), jnp.where(first, other, mine)], axis=0)
 
 
 def per_device(
@@ -68,7 +112,7 @@
         jnp.float32
     )
     local_hist = jnp.sum(onehot * live_slots[:, None].astype(jnp.float32), axis=0)
-    lead_totals = lax.psum(local_hist, ("dp", "outer"))
+    lead_totals = sum_small(local_hist)
     window_total = jnp.sum(onehot * lead_totals[None, :], axis=1)
     window_scale = jnp.where(live_slots, 1.0 / jnp.maximum(window_total, 1.0), 0.0)
     lead_rows = jnp.dot(onehot, lead_table, precision=precise, preferred_element_type=jnp.float32)
@@ -181,41 +225,41 @@
     grad_patches = (
         grad_residual.reshape(slot_count, window_len, model_width) + grad_inputs_norm
     ).astype(jnp.bfloat16)
-    small = lax.psum(
-        (
-            grad_norm1_gain,
-            grad_norm1_bias,
-            grad_lead_table,
-            grad_bias_query,
-            grad_bias_value,
-            grad_bias_out,
-            grad_norm2_gain,
-            grad_norm2_bias,
-            grad_bias_up,
-            grad_bias_down,
-        ),
-        ("dp", "outer"),
-    )
-    sum_qkv, sum_out, sum_up, sum_down = reduce_matrices(
-        (grad_w_qkv, grad_w_out, grad_w_up, grad_w_down)
-    )
+    vectors = (
+        grad_norm1_gain,
+        grad_norm1_bias,
+        grad_bias_query,
+        grad_bias_value,
+        grad_bias_out,
+        grad_norm2_gain,
+        grad_norm2_bias,
+        grad_bias_down,
+    )
+    stacked = jnp.concatenate(
+        [jnp.stack(vectors), grad_bias_up.reshape(-1, model_width), grad_lead_table], axis=0
+    )
+    small = sum_small(stacked)
+    up_rows = grad_bias_up.shape[0] // model_width
+    sum_down = scatter_sum(grad_w_down)
+    sum_up = scatter_sum(grad_w_up)
+    sum_last = scatter_sum(jnp.concatenate([grad_w_out, grad_w_qkv], axis=1))
     return (
         block_out,
         grad_patches,
         small[0],
         small[1],
+        small[8 + up_rows :],
+        sum_last[:, model_width:],
         small[2],
-        sum_qkv,
         small[3],
+        sum_last[:, :model_width],
         small[4],
-        sum_out,
         small[5],
         small[6],
+        sum_up,
+        small[8 : 8 + up_rows].reshape(-1),
+        sum_down,
         small[7],
-        sum_up,
-        small[8],
-        sum_down,
-        small[9],
     )
 
 

time: 1000 us -> 501 us (0.50)
  waiting for transfers between devices: 574 us -> 101 us
  blocking collectives: 84.6 us -> 0 us
  starting transfers between devices: 0.12 us -> 51.5 us
  other arithmetic: 63.3 us -> 101 us
  local copies, waits for them, and re-layouts: 104 us -> 90.2 us
  between operations: 15.6 us -> 3.34 us
    unnamed x4 -> x0, waiting for transfers between devices: 483 us -> none
    ppermute x0 -> x52, waiting for transfers between devices: none -> 101 us  [swap(): return lax.ppermute(values, axis, [(i, i ^ 1 << bit) for i in range(size)])]
    psum x2 -> x0, waiting for transfers between devices: 91.6 us -> none  [the longest x1 91.6 us: per_device(): lax.psum((grad_norm1_gain, grad_norm1_bias, grad_lead_table, grad_bias_qu...]
    psum x2 -> x0, blocking collectives: 84.6 us -> none  [the longest x1 42.7 us: per_device(): lax.psum((grad_norm1_gain, grad_norm1_bias, grad_lead_table, grad_bias_qu...]
    ppermute x0 -> x52, starting transfers between devices: none -> 51.5 us  [swap(): return lax.ppermute(values, axis, [(i, i ^ 1 << bit) for i in range(size)])]
    convert_element_type x0 -> x1, other arithmetic: none -> 28.7 us  [per_device(): activated_low = activated.astype(jnp.bfloat16)]
    reshape x4, local copies, waits for them, and re-layouts: 29.9 us -> 3.77 us  [the longest x2 1.85 us: layer_norm(): return centred * lax.rsqrt(spread + norm_epsilon) * norm_gain + norm_bias]
    add x0 -> x49, other arithmetic: none -> 19.4 us  [the longest x39 12.3 us: halve(): return (keep + swap(send, axis, bit), left)]
  transfers between devices with their start and end apart: 3 -> 52, of which waited for: 2 -> 30; matrix products, arithmetic and copies ran while one was open for 5% -> 40% of each run, Pallas kernels for 0% -> 0%
where the time goes in v1:
time: 501 us; the launch traced here: 495 us
  matrix products  148 us (30%)
  other arithmetic  101 us (20%)
  waiting for transfers between devices  101 us (20%)
  local copies, waits for them, and re-layouts  90.2 us (18%)
  starting transfers between devices  51.5 us (10%)
    ppermute x52, waiting for transfers between devices, swap(): return lax.ppermute(values, axis, [(i, i ^ 1 << bit) for i in range(size)])  101 us
    ppermute x52, starting transfers between devices, swap(): return lax.ppermute(values, axis, [(i, i ^ 1 << bit) for i in range(size)])  51.5 us
    dot_general x1, matrix products, per_device(): jnp.dot(normed2_low, w_up, preferred_element_type=jnp.float32) + bias_up  33.6 us
    convert_element_type x1, other arithmetic, per_device(): activated_low = activated.astype(jnp.bfloat16)  28.7 us
    dot_general x1, matrix products, per_device(): jnp.einsum('rd,fd->rf', grad_down, w_down, preferred_element_type=jnp.flo...  19.1 us
    unnamed x128, local copies, waits for them, and re-layouts  14.4 us
    dot_general x1, matrix products, per_device(): jnp.dot(activated_low, w_down, preferred_element_type=jnp.float32)  13.1 us
    add x39, other arithmetic, halve(): return (keep + swap(send, axis, bit), left)  12.3 us
  transfers between devices with their start and end apart: 52, of which 30 were waited for; matrix products, arithmetic and copies ran while one was open for 40% of the time, Pallas kernels for 0%

profile of v1, /device:TPU:0, one launch (start us, length us, event | category | flops | bytes accessed | tf_op | source)
XLA Modules:
  0.0 495.4 jit_solution(11136240521346925501)
XLA Ops:
  9.5 2.4 add_convert_fusion.4
  12.0 3.8 fusion.77
  17.1 2.3 fusion.34
  19.4 3.1 copy.89
  22.5 3.9 reshape.248
  26.4 2.6 copy.91
  28.9 3.9 reshape.250
  32.8 2.6 copy.90
  35.4 3.9 reshape.249
  39.3 4.8 fusion.32
  44.1 3.9 fusion.23
  48.9 3.4 fusion.39
  57.3 33.6 %fusion = (f32[1024,3072]{1,0:T(8,128)}, f32[1024,3072]{1,0:T(8,128)S(1)}) fusion(f32[3072]{0:T(1024)S(1)} %copy-done.40, bf16[768,3072]{1,0:T(8,128)(2,1)S(1)} %bitcast.339, f32[1024,768]{1,0:T(8,128)S(1)} %get-tuple-element.75, f32[768]{0:T(1024)S(1)} %copy-done.35, f32[768]{0:T(1024)S(1)} %copy-done.34, f32[1024]{0:T(1024)S(1)} %fusion.54, ...), kind=kOutput, calls=%fused_computation.2 | convolution fusion | flops 5033951232 | bytes 33056768 | tf_op jit(solution)/shard_map/dot_general | solution.py:159
  90.9 4.5 copy-done.13
  95.5 28.7 %fusion.3 = bf16[3072,1024]{0,1:T(8,128)(2,1)} fusion(f32[1024,3072]{1,0:T(8,128)S(1)} %get-tuple-element.77, f32[3072]{0:T(1024)S(1)} %copy-done.40), kind=kLoop, calls=%fused_computation.5 | loop fusion | flops 207618048 | bytes 18886656 | tf_op jit(solution)/shard_map/convert_element_type | solution.py:161
  125.4 2.5 collective-permute-start.1
  130.8 2.1 collective-permute-start.2
  135.8 3.0 collective-permute-start.3
  143.6 8.6 %copy.122 = bf16[3072,1024]{1,0:T(8,128)(2,1)} copy(bf16[3072,1024]{0,1:T(8,128)(2,1)} %fusion.3) | data formatting | bytes 12582912 | tf_op jit(solution)/shard_map/convert_element_type | solution.py:161
  154.5 3.6 convert_reduce_fusion.1
  160.2 19.1 %convert_reduce_fusion = (f32[3072]{0:T(1024)}, bf16[1024,3072]{1,0:T(8,128)(2,1)}) fusion(f32[1024,3072]{1,0:T(8,128)} %get-tuple-element.76, bf16[1024,768]{1,0:T(8,128)(2,1)} %bitcast_convert_fusion, bf16[3072,768]{1,0:T(8,128)(2,1)} %param.36, f32[1024,3072]{1,0:T(8,128)} %copy-done.13, f32[3072]{0:T(1024)S(1)} %copy-done.41), kind=kOutput, calls=%fused_computation.23 | convolution fusion | flops 4885312512 | bytes 37773312 | tf_op jit(solution)/shard_map/rd,fd->rf/dot_general | solution.py:173
  179.3 9.9 %multiply_reduce_fusion.1 = (f32[768]{0:T(1024)}, f32[1024]{0:T(1024)S(1)}, f32[768]{0:T(1024)}, f32[1024,768]{1,0:T(8,128)S(1)}) fusion(f32[1024,768]{1,0:T(8,128)S(1)} %copy-done.6, f32[1024]{0:T(1024)S(1)} %fusion.54, f32[1024]{0:T(1024)S(1)} %broadcast_multiply_fusion, f32[768]{0:T(1024)S(1)} %copy-done.34, bf16[1024,3072]{1,0:T(8,128)(2,1)} %get-tuple-element.88, ...), kind=kOutput, calls=%fused_computation.75 | convolution fusion | flops 4838126592 | bytes 17323008 | tf_op jit(solution)/shard_map/rf,df->rd/dot_general | solution.py:178
  189.2 8.5 %fusion.68 = f32[768,3072]{1,0:T(8,128)} fusion(bf16[1024,3072]{1,0:T(8,128)(2,1)S(1)} %copy-done.19, f32[1024,768]{1,0:T(8,128)S(1)} %copy-done.6, f32[768]{0:T(1024)S(1)} %copy-done.35, f32[768]{0:T(1024)S(1)} %copy-done.34, f32[1024]{0:T(1024)S(1)} %fusion.54, f32[1024]{0:T(1024)S(1)} %broadcast_multiply_fusion), kind=kOutput, calls=%fused_computation.255 | convolution fusion | flops 4835770368 | bytes 18888704 | tf_op jit(solution)/shard_map/rd,rf->df/dot_general | solution.py:176
  201.2 2.8 fusion.60
  204.0 2.6 convolution_convert_fusion
  206.7 2.6 copy.97
  209.3 3.9 reshape.255
  213.1 8.4 %convert_reduce_fusion.3 = (f32[12,64]{1,0:T(8,128)S(1)}, bf16[4,12,64,256]{3,2,1,0:T(8,128)(2,1)S(1)}) fusion(f32[4,12,256]{2,1,0:T(8,128)} %log_add_fusion, f32[4,12,256,256]{2,3,1,0:T(8,128)} %copy-done.1, pred[4,256]{1,0:T(4,128)(4,1)S(1)} %copy-done.30, bf16[4,256,12,64]{1,0,3,2:T(4,128)(2,1)} %reshape.255), kind=kOutput, calls=%fused_computation.77 | convolution fusion | flops 417594624 | bytes 15781888 | tf_op jit(solution)/shard_map/shwt,swhd->sthd/dot_general | solution.py:193
  221.6 10.2 %multiply_reduce_fusion = (f32[4,12,256]{2,1,0:T(8,128)S(1)}, f32[4,12,256,256]{2,3,1,0:T(8,128)}) fusion(f32[4,12,256]{2,1,0:T(8,128)S(1)} %copy-done.24, f32[4,12,256,256]{2,3,1,0:T(8,128)} %copy-done.1, pred[4,256]{1,0:T(4,128)(4,1)S(1)} %copy-done.30, bf16[4,256,12,64]{1,0,3,2:T(4,128)(2,1)S(1)} %copy-done.16, bf16[4,256,12,64]{1,0,3,2:T(4,128)(2,1)S(1)} %copy-done.17), kind=kOutput, calls=%fused_computation.25 | convolution fusion | flops 418369536 | bytes 28410880 | tf_op jit(solution)/shard_map/swhd,sthd->shwt/dot_general | solution.py:190
  231.8 8.2 %multiply_convert_fusion = bf16[4,12,256,256]{2,3,1,0:T(8,128)(2,1)S(1)} fusion(f32[4,12,256,256]{2,3,1,0:T(8,128)} %get-tuple-element.80, f32[4,12,256]{2,1,0:T(8,128)S(1)} %get-tuple-element.79, f32[4,12,256]{2,1,0:T(8,128)S(1)} %copy-done.24, f32[4,12,256,256]{2,3,1,0:T(8,128)S(1)} %bitcast.306, pred[4,256]{1,0:T(4,128)(4,1)S(1)} %copy-done.30), kind=kLoop, calls=%fused_computation.24 | loop fusion | flops 18874368 | bytes 31556608 | tf_op jit(solution)/shard_map/convert_element_type | solution.py:199
  249.1 6.2 %fusion.76 = (f32[768]{0:T(1024)}, f32[1024,768]{1,0:T(8,128)}) fusion(bf16[1024,2304]{0,1:T(8,128)(2,1)S(1)} %constant_dynamic-update-slice_fusion, bf16[768,2304]{1,0:T(8,128)(2,1)S(1)} %copy-done), kind=kOutput, calls=%fused_computation.262 | convolution fusion | flops 3624664320 | bytes 11406336 | tf_op jit(solution)/shard_map/re,de->rd/dot_general | solution.py:221
  255.3 6.2 %fusion.78 = f32[768,2304]{1,0:T(8,128)} fusion(bf16[1024,768]{1,0:T(8,128)(2,1)S(1)} %bitcast.326, bf16[1024,2304]{0,1:T(8,128)(2,1)S(1)} %constant_dynamic-update-slice_fusion), kind=kOutput, calls=%fused_computation.264 | convolution fusion | flops 3623878656 | bytes 13369344 | tf_op jit(solution)/shard_map/rd,re->de/dot_general | solution.py:216
  266.5 7.6 %fusion.79 = f32[2,2,2,2,2,96,768]{6,5,4,3,2,1,0:T(8,128)S(1)} fusion(bf16[2,2,2,2,2,96,1024]{6,5,4,3,2,1,0:T(8,128)(2,1)} %bitcast.316, bf16[1024,768,1,1,1,1,1]{1,0,6,5,4,3,2:T(8,128)(2,1)} %bitcast.330), kind=kOutput, calls=%fused_computation.265 | convolution fusion | flops 4831838208 | bytes 17301504 | tf_op jit(solution)/shard_map/rf,rd->fd/dot_general | solution.py:169
  274.2 2.9 dynamic-slice_bitcast_fusion
  281.1 3.4 multiply_reduce_fusion.3
  285.3 2.4 bitcast_reduce_fusion
  289.2 4.4 concatenate.28
  294.1 4.5 pad_maximum_fusion
  300.2 7.6 %constant_dynamic-slice_fusion.11 = (f32[2,2,2,1,2,24,3072]{6,5,4,3,2,1,0:T(8,128)}, f32[2,2,2,1,2,24,3072]{6,5,4,3,2,1,0:T(8,128)S(1)}, f32[2,2,2,1,2,24,3072]{6,5,4,3,2,1,0:T(8,128)}, f32[2,2,2,1,2,24,3072]{6,5,4,3,2,1,0:T(8,128)}) fusion(f32[2,2,2,2,2,24,3072]{6,5,4,3,2,1,0:T(8,128)} %bitcast.309, s32[]{:T(128)S(6)} %select_n.162, s32[]{:T(128)S(6)} %select_n.163, ...), kind=kLoop, calls=%fused_computation.208 | loop fusion | bytes 37748744 | tf_op jit(solution)/shard_map/jit(dynamic_index_in_dim)/dynamic_slice | solution.py:56
  307.8 2.7 copy.185
  311.8 2.7 copy.186
  317.3 13.1 %add_convert_fusion.2 = bf16[1024,768]{1,0:T(8,128)(2,1)} fusion(f32[1024,768]{1,0:T(8,128)S(1)} %copy-done.7, bf16[3072,768]{1,0:T(8,128)(2,1)} %param.36, f32[1024,3072]{1,0:T(8,128)} %get-tuple-element.76, f32[1024,3072]{1,0:T(8,128)} %copy-done.13, f32[3072]{0:T(1024)S(1)} %copy-done.42, f32[768]{0:T(1024)S(1)} %copy-done.51), kind=kOutput, calls=%fused_computation.86 | convolution fusion | flops 4846780416 | bytes 34618368 | tf_op jit(solution)/shard_map/dot_general | solution.py:163
  331.4 2.6 collective-permute-start.8
  334.7 7.2 %collective-permute-done.8 = f32[52,768]{1,0:T(8,128)S(1)} collective-permute-done((f32[52,768]{1,0:T(8,128)S(1)}, f32[52,768]{1,0:T(8,128)S(1)}, u32[]{:S(2)}, u32[]{:S(2)}) %collective-permute-start.8) | collective-permute-done | bytes 159776 | tf_op jit(solution)/shard_map/ppermute | solution.py:26
  342.5 5.0 %add_convert_fusion.1 = bf16[4,256,768]{2,1,0:T(8,128)(2,1)} fusion(f32[4,256,768]{2,1,0:T(8,128)} %bitcast.315, f32[4,256]{1,0:T(4,128)S(1)} %negate_multiply_fusion.1, f32[4,256]{1,0:T(4,128)S(1)} %multiply_multiply_fusion.5, f32[4,256]{1,0:T(4,128)S(1)} %copy-done.28, bf16[4,256,768]{2,1,0:T(8,128)(2,1)} %param.19, f32[4,256]{1,0:T(4,128)S(1)} %copy-done.32, ...), kind=kLoop, calls=%fused_computation.80 | loop fusion | flops 7864320 | bytes 9456640 | tf_op jit(solution)/shard_map/convert_element_type | solution.py:227
  352.0 4.4 bitcast_add_fusion
  359.4 3.1 bitcast_add_fusion.2
  365.8 3.1 bitcast_add_fusion.1
  370.2 7.4 %collective-permute-done.39 = f32[2,2,2,96,256]{4,3,1,0,2:T(8,128)S(1)} collective-permute-done((f32[2,2,2,96,256]{4,3,1,0,2:T(8,128)S(1)}, f32[2,2,2,96,256]{4,3,1,0,2:T(8,128)S(1)}, u32[]{:S(2)}, u32[]{:S(2)}) %collective-permute-start.39) | collective-permute-done | bytes 786464 | tf_op jit(solution)/shard_map/ppermute | solution.py:26
  381.1 13.3 %collective-permute-done.11 = f32[2,2,2,24,1024]{4,3,2,1,0:T(8,128)S(1)} collective-permute-done((f32[2,2,2,24,1024]{4,3,2,1,0:T(8,128)S(1)}, f32[2,2,2,24,1024]{4,3,2,1,0:T(8,128)S(1)}, u32[]{:S(2)}, u32[]{:S(2)}) %collective-permute-start.11) | collective-permute-done | bytes 786464 | tf_op jit(solution)/shard_map/ppermute | solution.py:26
  396.3 13.1 %collective-permute-done.25 = f32[2,2,2,24,1024]{4,3,2,1,0:T(8,128)S(1)} collective-permute-done((f32[2,2,2,24,1024]{4,3,2,1,0:T(8,128)S(1)}, f32[2,2,2,24,1024]{4,3,2,1,0:T(8,128)S(1)}, u32[]{:S(2)}, u32[]{:S(2)}) %collective-permute-start.25) | collective-permute-done | bytes 786464 | tf_op jit(solution)/shard_map/ppermute | solution.py:26
  414.1 6.5 %collective-permute-done.40 = f32[2,2,96,256]{3,2,1,0:T(8,128)S(1)} collective-permute-done((f32[2,2,96,256]{3,2,1,0:T(8,128)S(1)}, f32[2,2,96,256]{3,2,1,0:T(8,128)S(1)}, u32[]{:S(2)}, u32[]{:S(2)}) %collective-permute-start.40) | collective-permute-done | bytes 393248 | tf_op jit(solution)/shard_map/ppermute | solution.py:26
  423.8 5.3 %collective-permute-done.12 = f32[2,2,24,1024]{3,2,1,0:T(8,128)S(1)} collective-permute-done((f32[2,2,24,1024]{3,2,1,0:T(8,128)S(1)}, f32[2,2,24,1024]{3,2,1,0:T(8,128)S(1)}, u32[]{:S(2)}, u32[]{:S(2)}) %collective-permute-start.12) | collective-permute-done | bytes 393248 | tf_op jit(solution)/shard_map/ppermute | solution.py:26
  431.7 3.7 collective-permute-done.26
  448.1 2.9 collective-permute-start.42
  451.4 2.8 collective-permute-start.50
  454.5 2.8 collective-permute-start.18
  457.4 6.7 %collective-permute-done.42 = f32[96,256]{1,0:T(8,128)S(1)} collective-permute-done((f32[96,256]{1,0:T(8,128)S(1)}, f32[96,256]{1,0:T(8,128)S(1)}, u32[]{:S(2)}, u32[]{:S(2)}) %collective-permute-start.42) | collective-permute-done | bytes 98336 | tf_op jit(solution)/shard_map/ppermute | solution.py:26
  464.1 3.1 collective-permute-done.46
  467.3 5.2 %collective-permute-done.50 = f32[96,256]{1,0:T(8,128)S(1)} collective-permute-done((f32[96,256]{1,0:T(8,128)S(1)}, f32[96,256]{1,0:T(8,128)S(1)}, u32[]{:S(2)}, u32[]{:S(2)}) %collective-permute-start.50) | collective-permute-done | bytes 98336 | tf_op jit(solution)/shard_map/ppermute | solution.py:26
  472.5 2.1 collective-permute-done.14
  475.6 2.2 collective-permute-done.18
  487.3 2.5 collective-permute-done.23
  491.3 2.8 collective-permute-done.37
  (361 shorter events, 117.3 us)
Async XLA Ops:
  0.6 11.3 %copy-start = (bf16[768,2304]{1,0:T(8,128)(2,1)S(1)}, bf16[768,2304]{1,0:T(8,128)(2,1)}, u32[]{:S(2)}) copy-start(bf16[768,2304]{1,0:T(8,128)(2,1)} %param.27) | copy-start | bytes 10616836
  2.9 121.3 %collective-permute-start = (f32[40]{0:T(128)}, f32[40]{0:T(128)}, u32[]{:S(2)}, u32[]{:S(2)}) collective-permute-start(f32[40]{0:T(128)} %select_reduce_fusion.1), channel_id=1, source_target_pairs={{0,2},{2,0},{4,6},{6,4},{8,10},{10,8},{12,14},{14,12},{16,18},{18,... | collective-permute-start | bytes 488 | tf_op jit(solution)/shard_map/ppermute | solution.py:26
  4.1 44.8 %copy-start.29 = (pred[4,256]{1,0:T(4,128)(4,1)}, pred[4,256]{1,0:T(4,128)(4,1)S(1)}, u32[]{:S(2)}) copy-start(pred[4,256]{1,0:T(4,128)(4,1)S(1)} %iota_compare_fusion) | copy-start | bytes 3076
  55.8 35.1 %copy-start.5 = (f32[1024,768]{1,0:T(8,128)}, f32[1024,768]{1,0:T(8,128)S(1)}, u32[]{:S(2)}) copy-start(f32[1024,768]{1,0:T(8,128)S(1)} %get-tuple-element.75) | copy-start | bytes 9437188
  125.4 4.2 collective-permute-start.1
  130.8 3.9 collective-permute-start.2
  135.8 4.8 collective-permute-start.3
  141.8 10.5 %collective-permute-start.4 = (f32[40]{0:T(128)}, f32[40]{0:T(128)}, u32[]{:S(2)}, u32[]{:S(2)}) collective-permute-start(f32[40]{0:T(128)} %add.403), channel_id=1, source_target_pairs={{0,1},{1,0},{2,3},{3,2},{4,5},{5,4},{6,7},{7,6},{8,9},{9,8},{10,11... | collective-permute-start | bytes 488 | tf_op jit(solution)/shard_map/ppermute | solution.py:26
  160.2 19.1 %copy-start.6 = (f32[1024,768]{1,0:T(8,128)S(1)}, f32[1024,768]{1,0:T(8,128)}, u32[]{:S(2)}) copy-start(f32[1024,768]{1,0:T(8,128)} %copy-done.5) | copy-start | bytes 9437188
  179.3 9.9 %copy-start.19 = (bf16[1024,3072]{1,0:T(8,128)(2,1)S(1)}, bf16[1024,3072]{1,0:T(8,128)(2,1)}, u32[]{:S(2)}) copy-start(bf16[1024,3072]{1,0:T(8,128)(2,1)} %get-tuple-element.88) | copy-start | bytes 18874372
  189.2 8.5 %copy-start.38 = (f32[1024]{0:T(1024)S(1)}, f32[1024]{0:T(1024)}, u32[]{:S(2)}) copy-start(f32[1024]{0:T(1024)} %copy-done.37) | copy-start | bytes 12292
  213.1 8.4 %copy-start.17 = (bf16[4,256,12,64]{1,0,3,2:T(4,128)(2,1)S(1)}, bf16[4,256,12,64]{1,0,3,2:T(4,128)(2,1)}, u32[]{:S(2)}) copy-start(bf16[4,256,12,64]{1,0,3,2:T(4,128)(2,1)} %reshape.255) | copy-start | bytes 4718596
  213.1 8.4 %copy-start.24 = (f32[4,12,256]{2,1,0:T(8,128)S(1)}, f32[4,12,256]{2,1,0:T(8,128)}, u32[]{:S(2)}) copy-start(f32[4,12,256]{2,1,0:T(8,128)} %log_add_fusion) | copy-start | bytes 147460
  213.1 18.6 %slice-start = ((s8[12582912]{0:T(1024)(128)(4,1)}), s8[4194304]{0:T(1024)(128)(4,1)S(1)}, s32[]{:S(2)}) async-start(s8[12582912]{0:T(1024)(128)(4,1)} %bitcast.305), calls=%async_computation | async-start | bytes 8388608
  221.5 10.2 %slice-start.1 = ((s8[12582912]{0:T(1024)(128)(4,1)}), s8[4194304]{0:T(1024)(128)(4,1)S(1)}, s32[]{:S(2)}) async-start(s8[12582912]{0:T(1024)(128)(4,1)} %bitcast.305), calls=%async_computation.1 | async-start | bytes 8388608
  221.5 10.2 %slice-start.2 = ((s8[12582912]{0:T(1024)(128)(4,1)}), s8[4194304]{0:T(1024)(128)(4,1)S(1)}, s32[]{:S(2)}) async-start(s8[12582912]{0:T(1024)(128)(4,1)} %bitcast.305), calls=%async_computation.2 | async-start | bytes 8388608
  255.3 10.0 %copy-start.45 = (f32[768]{0:T(1024)S(1)}, f32[768]{0:T(1024)}, u32[]{:S(2)}) copy-start(f32[768]{0:T(1024)} %get-tuple-element.20) | copy-start | bytes 9220
  279.2 72.8 %collective-permute-start.38 = (f32[2,2,2,2,96,768]{5,4,3,2,1,0:T(8,128)}, f32[2,2,2,2,96,768]{5,4,3,2,1,0:T(8,128)}, u32[]{:S(2)}, u32[]{:S(2)}) collective-permute-start(f32[2,2,2,2,96,768]{5,4,3,2,1,0:T(8,128)} %dynamic-slice_bitcast_fusion), channel_id=1, source_target_pairs={{0,2},{2,0},{4,6},{6,4},{8,10},{10,8},{12,14},{14,12},{16,18},{18,... | collective-permute-start | bytes 14155784 | tf_op jit(solution)/shard_map/ppermute | solution.py:26
  293.6 5.0 %collective-permute-start.5 = (f32[52,768]{1,0:T(8,128)}, f32[52,768]{1,0:T(8,128)S(1)}, u32[]{:S(2)}, u32[]{:S(2)}) collective-permute-start(f32[52,768]{1,0:T(8,128)} %concatenate.28), channel_id=1, source_target_pairs={{0,2},{2,0},{4,6},{6,4},{8,10},{10,8},{12,14},{14,12},{16,18},{18,... | collective-permute-start | bytes 479240 | tf_op jit(solution)/shard_map/ppermute | solution.py:26
  298.6 16.4 %collective-permute-start.6 = (f32[52,768]{1,0:T(8,128)S(1)}, f32[52,768]{1,0:T(8,128)S(1)}, u32[]{:S(2)}, u32[]{:S(2)}) collective-permute-start(f32[52,768]{1,0:T(8,128)S(1)} %add.408), channel_id=1, source_target_pairs={{0,4},{2,6},{4,0},{6,2},{8,12},{10,14},{12,8},{14,10},{16,20},{18,... | collective-permute-start | bytes 479240 | tf_op jit(solution)/shard_map/ppermute | solution.py:26
  314.5 44.3 %collective-permute-start.10 = (f32[2,2,2,2,24,3072]{5,4,3,1,0,2:T(8,128)}, f32[2,2,2,2,24,3072]{5,4,3,1,0,2:T(8,128)}, u32[]{:S(2)}, u32[]{:S(2)}) collective-permute-start(f32[2,2,2,2,24,3072]{5,4,3,1,0,2:T(8,128)} %bitcast.295), channel_id=1, source_target_pairs={{0,2},{2,0},{4,6},{6,4},{8,10},{10,8},{12,14},{14,12},{16,18},{18,... | collective-permute-start | bytes 14155784 | tf_op jit(solution)/shard_map/ppermute | solution.py:26
  314.5 50.0 %collective-permute-start.24 = (f32[2,2,2,2,24,3072]{5,4,3,1,0,2:T(8,128)}, f32[2,2,2,2,24,3072]{5,4,3,1,0,2:T(8,128)}, u32[]{:S(2)}, u32[]{:S(2)}) collective-permute-start(f32[2,2,2,2,24,3072]{5,4,3,1,0,2:T(8,128)} %bitcast.294), channel_id=1, source_target_pairs={{0,2},{2,0},{4,6},{6,4},{8,10},{10,8},{12,14},{14,12},{16,18},{18,... | collective-permute-start | bytes 14155784 | tf_op jit(solution)/shard_map/ppermute | solution.py:26
  315.7 14.7 %collective-permute-start.7 = (f32[52,768]{1,0:T(8,128)}, f32[52,768]{1,0:T(8,128)}, u32[]{:S(2)}, u32[]{:S(2)}) collective-permute-start(f32[52,768]{1,0:T(8,128)} %add.409), channel_id=1, source_target_pairs={{0,8},{2,10},{4,12},{6,14},{8,0},{10,2},{12,4},{14,6},{16,24},{18,... | collective-permute-start | bytes 479240 | tf_op jit(solution)/shard_map/ppermute | solution.py:26
  331.4 10.5 %collective-permute-start.8 = (f32[52,768]{1,0:T(8,128)S(1)}, f32[52,768]{1,0:T(8,128)S(1)}, u32[]{:S(2)}, u32[]{:S(2)}) collective-permute-start(f32[52,768]{1,0:T(8,128)S(1)} %add.410), channel_id=1, source_target_pairs={{0,16},{2,18},{4,20},{6,22},{8,24},{10,26},{12,28},{14,30},{16,0},... | collective-permute-start | bytes 479240 | tf_op jit(solution)/shard_map/ppermute | solution.py:26
  342.0 6.4 %collective-permute-start.9 = (f32[52,768]{1,0:T(8,128)S(1)}, f32[52,768]{1,0:T(8,128)S(1)}, u32[]{:S(2)}, u32[]{:S(2)}) collective-permute-start(f32[52,768]{1,0:T(8,128)S(1)} %add.411), channel_id=1, source_target_pairs={{0,1},{1,0},{2,3},{3,2},{4,5},{5,4},{6,7},{7,6},{8,9},{9,8},{10,11... | collective-permute-start | bytes 479240 | tf_op jit(solution)/shard_map/ppermute | solution.py:26
  357.0 20.5 %collective-permute-start.39 = (f32[2,2,2,96,256]{4,3,1,0,2:T(8,128)S(1)}, f32[2,2,2,96,256]{4,3,1,0,2:T(8,128)S(1)}, u32[]{:S(2)}, u32[]{:S(2)}) collective-permute-start(f32[2,2,2,96,256]{4,3,1,0,2:T(8,128)S(1)} %bitcast.335), channel_id=1, source_target_pairs={{0,4},{2,6},{4,0},{6,2},{8,12},{10,14},{12,8},{14,10},{16,20},{18,... | collective-permute-start | bytes 2359304 | tf_op jit(solution)/shard_map/ppermute | solution.py:26
  358.0 20.5 %collective-permute-start.43 = (f32[2,2,2,96,256]{4,3,2,0,1:T(8,128)S(1)}, f32[2,2,2,96,256]{4,3,2,0,1:T(8,128)S(1)}, u32[]{:S(2)}, u32[]{:S(2)}) collective-permute-start(f32[2,2,2,96,256]{4,3,2,0,1:T(8,128)S(1)} %bitcast.336), channel_id=1, source_target_pairs={{0,1},{1,0},{2,3},{3,2},{4,5},{5,4},{6,7},{7,6},{8,9},{9,8},{10,11... | collective-permute-start | bytes 2359304 | tf_op jit(solution)/shard_map/ppermute | solution.py:26
  358.8 21.4 %collective-permute-start.47 = (f32[2,2,2,96,256]{4,3,2,0,1:T(8,128)S(1)}, f32[2,2,2,96,256]{4,3,2,0,1:T(8,128)S(1)}, u32[]{:S(2)}, u32[]{:S(2)}) collective-permute-start(f32[2,2,2,96,256]{4,3,2,0,1:T(8,128)S(1)} %bitcast.333), channel_id=1, source_target_pairs={{0,8},{2,10},{4,12},{6,14},{8,0},{10,2},{12,4},{14,6},{16,24},{18,... | collective-permute-start | bytes 2359304 | tf_op jit(solution)/shard_map/ppermute | solution.py:26
  363.2 31.2 %collective-permute-start.11 = (f32[2,2,2,24,1024]{4,3,2,1,0:T(8,128)S(1)}, f32[2,2,2,24,1024]{4,3,2,1,0:T(8,128)S(1)}, u32[]{:S(2)}, u32[]{:S(2)}) collective-permute-start(f32[2,2,2,24,1024]{4,3,2,1,0:T(8,128)S(1)} %dynamic-slice_bitcast_fusion.2), channel_id=1, source_target_pairs={{0,4},{2,6},{4,0},{6,2},{8,12},{10,14},{12,8},{14,10},{16,20},{18,... | collective-permute-start | bytes 2359304 | tf_op jit(solution)/shard_map/ppermute | solution.py:26
  364.5 30.9 %collective-permute-start.15 = (f32[2,2,2,24,1024]{4,3,2,1,0:T(8,128)S(1)}, f32[2,2,2,24,1024]{4,3,2,1,0:T(8,128)S(1)}, u32[]{:S(2)}, u32[]{:S(2)}) collective-permute-start(f32[2,2,2,24,1024]{4,3,2,1,0:T(8,128)S(1)} %bitcast.337), channel_id=1, source_target_pairs={{0,1},{1,0},{2,3},{3,2},{4,5},{5,4},{6,7},{7,6},{8,9},{9,8},{10,11... | collective-permute-start | bytes 2359304 | tf_op jit(solution)/shard_map/ppermute | solution.py:26
  377.6 32.0 %collective-permute-start.19 = (f32[2,2,2,24,1024]{4,3,2,1,0:T(8,128)S(1)}, f32[2,2,2,24,1024]{4,3,2,1,0:T(8,128)S(1)}, u32[]{:S(2)}, u32[]{:S(2)}) collective-permute-start(f32[2,2,2,24,1024]{4,3,2,1,0:T(8,128)S(1)} %bitcast.331), channel_id=1, source_target_pairs={{0,8},{2,10},{4,12},{6,14},{8,0},{10,2},{12,4},{14,6},{16,24},{18,... | collective-permute-start | bytes 2359304 | tf_op jit(solution)/shard_map/ppermute | solution.py:26
  378.5 30.9 %collective-permute-start.25 = (f32[2,2,2,24,1024]{4,3,2,1,0:T(8,128)S(1)}, f32[2,2,2,24,1024]{4,3,2,1,0:T(8,128)S(1)}, u32[]{:S(2)}, u32[]{:S(2)}) collective-permute-start(f32[2,2,2,24,1024]{4,3,2,1,0:T(8,128)S(1)} %dynamic-slice_bitcast_fusion.1), channel_id=1, source_target_pairs={{0,4},{2,6},{4,0},{6,2},{8,12},{10,14},{12,8},{14,10},{16,20},{18,... | collective-permute-start | bytes 2359304 | tf_op jit(solution)/shard_map/ppermute | solution.py:26
  380.2 32.1 %collective-permute-start.29 = (f32[2,2,2,24,1024]{4,3,2,1,0:T(8,128)S(1)}, f32[2,2,2,24,1024]{4,3,2,1,0:T(8,128)S(1)}, u32[]{:S(2)}, u32[]{:S(2)}) collective-permute-start(f32[2,2,2,24,1024]{4,3,2,1,0:T(8,128)S(1)} %bitcast.334), channel_id=1, source_target_pairs={{0,1},{1,0},{2,3},{3,2},{4,5},{5,4},{6,7},{7,6},{8,9},{9,8},{10,11... | collective-permute-start | bytes 2359304 | tf_op jit(solution)/shard_map/ppermute | solution.py:26
  394.4 18.6 %collective-permute-start.33 = (f32[2,2,2,24,1024]{4,3,2,1,0:T(8,128)S(1)}, f32[2,2,2,24,1024]{4,3,2,1,0:T(8,128)S(1)}, u32[]{:S(2)}, u32[]{:S(2)}) collective-permute-start(f32[2,2,2,24,1024]{4,3,2,1,0:T(8,128)S(1)} %bitcast.332), channel_id=1, source_target_pairs={{0,8},{2,10},{4,12},{6,14},{8,0},{10,2},{12,4},{14,6},{16,24},{18,... | collective-permute-start | bytes 2359304 | tf_op jit(solution)/shard_map/ppermute | solution.py:26
  395.4 25.3 %collective-permute-start.40 = (f32[2,2,96,256]{3,2,1,0:T(8,128)S(1)}, f32[2,2,96,256]{3,2,1,0:T(8,128)S(1)}, u32[]{:S(2)}, u32[]{:S(2)}) collective-permute-start(f32[2,2,96,256]{3,2,1,0:T(8,128)S(1)} %dynamic-slice_bitcast_fusion.5), channel_id=1, source_target_pairs={{0,1},{1,0},{2,3},{3,2},{4,5},{5,4},{6,7},{7,6},{8,9},{9,8},{10,11... | collective-permute-start | bytes 1179656 | tf_op jit(solution)/shard_map/ppermute | solution.py:26
  409.4 12.8 %collective-permute-start.44 = (f32[2,2,96,256]{3,2,1,0:T(8,128)S(1)}, f32[2,2,96,256]{3,2,1,0:T(8,128)S(1)}, u32[]{:S(2)}, u32[]{:S(2)}) collective-permute-start(f32[2,2,96,256]{3,2,1,0:T(8,128)S(1)} %dynamic-slice_bitcast_fusion.4), channel_id=1, source_target_pairs={{0,8},{2,10},{4,12},{6,14},{8,0},{10,2},{12,4},{14,6},{16,24},{18,... | collective-permute-start | bytes 1179656 | tf_op jit(solution)/shard_map/ppermute | solution.py:26
  409.6 13.5 %collective-permute-start.48 = (f32[2,2,96,256]{3,2,1,0:T(8,128)S(1)}, f32[2,2,96,256]{3,2,1,0:T(8,128)S(1)}, u32[]{:S(2)}, u32[]{:S(2)}) collective-permute-start(f32[2,2,96,256]{3,2,1,0:T(8,128)S(1)} %dynamic-slice_bitcast_fusion.3), channel_id=1, source_target_pairs={{0,4},{2,6},{4,0},{6,2},{8,12},{10,14},{12,8},{14,10},{16,20},{18,... | collective-permute-start | bytes 1179656 | tf_op jit(solution)/shard_map/ppermute | solution.py:26
  412.2 16.9 %collective-permute-start.12 = (f32[2,2,24,1024]{3,2,1,0:T(8,128)S(1)}, f32[2,2,24,1024]{3,2,1,0:T(8,128)S(1)}, u32[]{:S(2)}, u32[]{:S(2)}) collective-permute-start(f32[2,2,24,1024]{3,2,1,0:T(8,128)S(1)} %dynamic-slice_bitcast_fusion.11), channel_id=1, source_target_pairs={{0,1},{1,0},{2,3},{3,2},{4,5},{5,4},{6,7},{7,6},{8,9},{9,8},{10,11... | collective-permute-start | bytes 1179656 | tf_op jit(solution)/shard_map/ppermute | solution.py:26
  413.1 17.6 %collective-permute-start.16 = (f32[2,2,24,1024]{3,2,1,0:T(8,128)S(1)}, f32[2,2,24,1024]{3,2,1,0:T(8,128)S(1)}, u32[]{:S(2)}, u32[]{:S(2)}) collective-permute-start(f32[2,2,24,1024]{3,2,1,0:T(8,128)S(1)} %dynamic-slice_bitcast_fusion.10), channel_id=1, source_target_pairs={{0,8},{2,10},{4,12},{6,14},{8,0},{10,2},{12,4},{14,6},{16,24},{18,... | collective-permute-start | bytes 1179656 | tf_op jit(solution)/shard_map/ppermute | solution.py:26
  420.7 10.2 %collective-permute-start.20 = (f32[2,2,24,1024]{3,2,1,0:T(8,128)S(1)}, f32[2,2,24,1024]{3,2,1,0:T(8,128)S(1)}, u32[]{:S(2)}, u32[]{:S(2)}) collective-permute-start(f32[2,2,24,1024]{3,2,1,0:T(8,128)S(1)} %dynamic-slice_bitcast_fusion.9), channel_id=1, source_target_pairs={{0,4},{2,6},{4,0},{6,2},{8,12},{10,14},{12,8},{14,10},{16,20},{18,... | collective-permute-start | bytes 1179656 | tf_op jit(solution)/shard_map/ppermute | solution.py:26
  422.2 13.2 %collective-permute-start.26 = (f32[2,2,24,1024]{3,2,1,0:T(8,128)S(1)}, f32[2,2,24,1024]{3,2,1,0:T(8,128)S(1)}, u32[]{:S(2)}, u32[]{:S(2)}) collective-permute-start(f32[2,2,24,1024]{3,2,1,0:T(8,128)S(1)} %dynamic-slice_bitcast_fusion.8), channel_id=1, source_target_pairs={{0,1},{1,0},{2,3},{3,2},{4,5},{5,4},{6,7},{7,6},{8,9},{9,8},{10,11... | collective-permute-start | bytes 1179656 | tf_op jit(solution)/shard_map/ppermute | solution.py:26
  423.1 15.2 %collective-permute-start.30 = (f32[2,2,24,1024]{3,2,1,0:T(8,128)S(1)}, f32[2,2,24,1024]{3,2,1,0:T(8,128)S(1)}, u32[]{:S(2)}, u32[]{:S(2)}) collective-permute-start(f32[2,2,24,1024]{3,2,1,0:T(8,128)S(1)} %dynamic-slice_bitcast_fusion.7), channel_id=1, source_target_pairs={{0,8},{2,10},{4,12},{6,14},{8,0},{10,2},{12,4},{14,6},{16,24},{18,... | collective-permute-start | bytes 1179656 | tf_op jit(solution)/shard_map/ppermute | solution.py:26
  429.1 10.9 %collective-permute-start.34 = (f32[2,2,24,1024]{3,2,1,0:T(8,128)S(1)}, f32[2,2,24,1024]{3,2,1,0:T(8,128)S(1)}, u32[]{:S(2)}, u32[]{:S(2)}) collective-permute-start(f32[2,2,24,1024]{3,2,1,0:T(8,128)S(1)} %dynamic-slice_bitcast_fusion.6), channel_id=1, source_target_pairs={{0,4},{2,6},{4,0},{6,2},{8,12},{10,14},{12,8},{14,10},{16,20},{18,... | collective-permute-start | bytes 1179656 | tf_op jit(solution)/shard_map/ppermute | solution.py:26
  430.7 11.9 %collective-permute-start.41 = (f32[2,96,256]{2,1,0:T(8,128)S(1)}, f32[2,96,256]{2,1,0:T(8,128)S(1)}, u32[]{:S(2)}, u32[]{:S(2)}) collective-permute-start(f32[2,96,256]{2,1,0:T(8,128)S(1)} %dynamic-slice_bitcast_fusion.14), channel_id=1, source_target_pairs={{0,8},{2,10},{4,12},{6,14},{8,0},{10,2},{12,4},{14,6},{16,24},{18,... | collective-permute-start | bytes 589832 | tf_op jit(solution)/shard_map/ppermute | solution.py:26
  430.9 13.0 %collective-permute-start.45 = (f32[2,96,256]{2,1,0:T(8,128)S(1)}, f32[2,96,256]{2,1,0:T(8,128)S(1)}, u32[]{:S(2)}, u32[]{:S(2)}) collective-permute-start(f32[2,96,256]{2,1,0:T(8,128)S(1)} %dynamic-slice_bitcast_fusion.13), channel_id=1, source_target_pairs={{0,4},{2,6},{4,0},{6,2},{8,12},{10,14},{12,8},{14,10},{16,20},{18,... | collective-permute-start | bytes 589832 | tf_op jit(solution)/shard_map/ppermute | solution.py:26
  435.4 8.7 %collective-permute-start.49 = (f32[2,96,256]{2,1,0:T(8,128)S(1)}, f32[2,96,256]{2,1,0:T(8,128)S(1)}, u32[]{:S(2)}, u32[]{:S(2)}) collective-permute-start(f32[2,96,256]{2,1,0:T(8,128)S(1)} %dynamic-slice_bitcast_fusion.12), channel_id=1, source_target_pairs={{0,1},{1,0},{2,3},{3,2},{4,5},{5,4},{6,7},{7,6},{8,9},{9,8},{10,11... | collective-permute-start | bytes 589832 | tf_op jit(solution)/shard_map/ppermute | solution.py:26
  438.3 8.4 %collective-permute-start.13 = (f32[2,24,1024]{2,1,0:T(8,128)S(1)}, f32[2,24,1024]{2,1,0:T(8,128)S(1)}, u32[]{:S(2)}, u32[]{:S(2)}) collective-permute-start(f32[2,24,1024]{2,1,0:T(8,128)S(1)} %dynamic-slice_bitcast_fusion.20), channel_id=1, source_target_pairs={{0,8},{2,10},{4,12},{6,14},{8,0},{10,2},{12,4},{14,6},{16,24},{18,... | collective-permute-start | bytes 589832 | tf_op jit(solution)/shard_map/ppermute | solution.py:26
  440.0 8.1 %collective-permute-start.17 = (f32[2,24,1024]{2,1,0:T(8,128)S(1)}, f32[2,24,1024]{2,1,0:T(8,128)S(1)}, u32[]{:S(2)}, u32[]{:S(2)}) collective-permute-start(f32[2,24,1024]{2,1,0:T(8,128)S(1)} %dynamic-slice_bitcast_fusion.19), channel_id=1, source_target_pairs={{0,4},{2,6},{4,0},{6,2},{8,12},{10,14},{12,8},{14,10},{16,20},{18,... | collective-permute-start | bytes 589832 | tf_op jit(solution)/shard_map/ppermute | solution.py:26
  442.6 8.5 %collective-permute-start.21 = (f32[2,24,1024]{2,1,0:T(8,128)S(1)}, f32[2,24,1024]{2,1,0:T(8,128)S(1)}, u32[]{:S(2)}, u32[]{:S(2)}) collective-permute-start(f32[2,24,1024]{2,1,0:T(8,128)S(1)} %dynamic-slice_bitcast_fusion.18), channel_id=1, source_target_pairs={{0,1},{1,0},{2,3},{3,2},{4,5},{5,4},{6,7},{7,6},{8,9},{9,8},{10,11... | collective-permute-start | bytes 589832 | tf_op jit(solution)/shard_map/ppermute | solution.py:26
  443.9 7.5 %collective-permute-start.27 = (f32[2,24,1024]{2,1,0:T(8,128)S(1)}, f32[2,24,1024]{2,1,0:T(8,128)S(1)}, u32[]{:S(2)}, u32[]{:S(2)}) collective-permute-start(f32[2,24,1024]{2,1,0:T(8,128)S(1)} %dynamic-slice_bitcast_fusion.17), channel_id=1, source_target_pairs={{0,8},{2,10},{4,12},{6,14},{8,0},{10,2},{12,4},{14,6},{16,24},{18,... | collective-permute-start | bytes 589832 | tf_op jit(solution)/shard_map/ppermute | solution.py:26
  444.1 10.1 %collective-permute-start.31 = (f32[2,24,1024]{2,1,0:T(8,128)S(1)}, f32[2,24,1024]{2,1,0:T(8,128)S(1)}, u32[]{:S(2)}, u32[]{:S(2)}) collective-permute-start(f32[2,24,1024]{2,1,0:T(8,128)S(1)} %dynamic-slice_bitcast_fusion.16), channel_id=1, source_target_pairs={{0,4},{2,6},{4,0},{6,2},{8,12},{10,14},{12,8},{14,10},{16,20},{18,... | collective-permute-start | bytes 589832 | tf_op jit(solution)/shard_map/ppermute | solution.py:26
  446.8 7.8 %collective-permute-start.35 = (f32[2,24,1024]{2,1,0:T(8,128)S(1)}, f32[2,24,1024]{2,1,0:T(8,128)S(1)}, u32[]{:S(2)}, u32[]{:S(2)}) collective-permute-start(f32[2,24,1024]{2,1,0:T(8,128)S(1)} %dynamic-slice_bitcast_fusion.15), channel_id=1, source_target_pairs={{0,1},{1,0},{2,3},{3,2},{4,5},{5,4},{6,7},{7,6},{8,9},{9,8},{10,11... | collective-permute-start | bytes 589832 | tf_op jit(solution)/shard_map/ppermute | solution.py:26
  448.1 16.0 %collective-permute-start.42 = (f32[96,256]{1,0:T(8,128)S(1)}, f32[96,256]{1,0:T(8,128)S(1)}, u32[]{:S(2)}, u32[]{:S(2)}) collective-permute-start(f32[96,256]{1,0:T(8,128)S(1)} %dynamic-slice_bitcast_fusion.23), channel_id=1, source_target_pairs={{0,16},{2,18},{4,20},{6,22},{8,24},{10,26},{12,28},{14,30},{16,0},... | collective-permute-start | bytes 294920 | tf_op jit(solution)/shard_map/ppermute | solution.py:26
  451.0 16.2 %collective-permute-start.46 = (f32[96,256]{1,0:T(8,128)S(1)}, f32[96,256]{1,0:T(8,128)S(1)}, u32[]{:S(2)}, u32[]{:S(2)}) collective-permute-start(f32[96,256]{1,0:T(8,128)S(1)} %dynamic-slice_bitcast_fusion.22), channel_id=1, source_target_pairs={{0,16},{2,18},{4,20},{6,22},{8,24},{10,26},{12,28},{14,30},{16,0},... | collective-permute-start | bytes 294920 | tf_op jit(solution)/shard_map/ppermute | solution.py:26
  451.4 21.1 %collective-permute-start.50 = (f32[96,256]{1,0:T(8,128)S(1)}, f32[96,256]{1,0:T(8,128)S(1)}, u32[]{:S(2)}, u32[]{:S(2)}) collective-permute-start(f32[96,256]{1,0:T(8,128)S(1)} %dynamic-slice_bitcast_fusion.21), channel_id=1, source_target_pairs={{0,16},{2,18},{4,20},{6,22},{8,24},{10,26},{12,28},{14,30},{16,0},... | collective-permute-start | bytes 294920 | tf_op jit(solution)/shard_map/ppermute | solution.py:26
  454.2 20.4 %collective-permute-start.14 = (f32[24,1024]{1,0:T(8,128)S(1)}, f32[24,1024]{1,0:T(8,128)S(1)}, u32[]{:S(2)}, u32[]{:S(2)}) collective-permute-start(f32[24,1024]{1,0:T(8,128)S(1)} %dynamic-slice_bitcast_fusion.29), channel_id=1, source_target_pairs={{0,16},{2,18},{4,20},{6,22},{8,24},{10,26},{12,28},{14,30},{16,0},... | collective-permute-start | bytes 294920 | tf_op jit(solution)/shard_map/ppermute | solution.py:26
  454.5 23.2 %collective-permute-start.18 = (f32[24,1024]{1,0:T(8,128)S(1)}, f32[24,1024]{1,0:T(8,128)S(1)}, u32[]{:S(2)}, u32[]{:S(2)}) collective-permute-start(f32[24,1024]{1,0:T(8,128)S(1)} %dynamic-slice_bitcast_fusion.28), channel_id=1, source_target_pairs={{0,16},{2,18},{4,20},{6,22},{8,24},{10,26},{12,28},{14,30},{16,0},... | collective-permute-start | bytes 294920 | tf_op jit(solution)/shard_map/ppermute | solution.py:26
  464.1 16.9 %collective-permute-start.22 = (f32[24,1024]{1,0:T(8,128)S(1)}, f32[24,1024]{1,0:T(8,128)S(1)}, u32[]{:S(2)}, u32[]{:S(2)}) collective-permute-start(f32[24,1024]{1,0:T(8,128)S(1)} %dynamic-slice_bitcast_fusion.27), channel_id=1, source_target_pairs={{0,16},{2,18},{4,20},{6,22},{8,24},{10,26},{12,28},{14,30},{16,0},... | collective-permute-start | bytes 294920 | tf_op jit(solution)/shard_map/ppermute | solution.py:26
  467.2 15.7 %collective-permute-start.28 = (f32[24,1024]{1,0:T(8,128)S(1)}, f32[24,1024]{1,0:T(8,128)S(1)}, u32[]{:S(2)}, u32[]{:S(2)}) collective-permute-start(f32[24,1024]{1,0:T(8,128)S(1)} %dynamic-slice_bitcast_fusion.26), channel_id=1, source_target_pairs={{0,16},{2,18},{4,20},{6,22},{8,24},{10,26},{12,28},{14,30},{16,0},... | collective-permute-start | bytes 294920 | tf_op jit(solution)/shard_map/ppermute | solution.py:26
  472.5 11.5 %collective-permute-start.32 = (f32[24,1024]{1,0:T(8,128)S(1)}, f32[24,1024]{1,0:T(8,128)S(1)}, u32[]{:S(2)}, u32[]{:S(2)}) collective-permute-start(f32[24,1024]{1,0:T(8,128)S(1)} %dynamic-slice_bitcast_fusion.25), channel_id=1, source_target_pairs={{0,16},{2,18},{4,20},{6,22},{8,24},{10,26},{12,28},{14,30},{16,0},... | collective-permute-start | bytes 294920 | tf_op jit(solution)/shard_map/ppermute | solution.py:26
  474.6 10.5 %collective-permute-start.36 = (f32[24,1024]{1,0:T(8,128)S(1)}, f32[24,1024]{1,0:T(8,128)S(1)}, u32[]{:S(2)}, u32[]{:S(2)}) collective-permute-start(f32[24,1024]{1,0:T(8,128)S(1)} %dynamic-slice_bitcast_fusion.24), channel_id=1, source_target_pairs={{0,16},{2,18},{4,20},{6,22},{8,24},{10,26},{12,28},{14,30},{16,0},... | collective-permute-start | bytes 294920 | tf_op jit(solution)/shard_map/ppermute | solution.py:26
  477.8 8.6 %collective-permute-start.51 = (f32[96,768]{1,0:T(8,128)S(1)}, f32[96,768]{1,0:T(8,128)S(1)}, u32[]{:S(2)}, u32[]{:S(2)}) collective-permute-start(f32[96,768]{1,0:T(8,128)S(1)} %pad_maximum_fusion.5), channel_id=1, source_target_pairs={{0,1},{1,0},{2,3},{3,2},{4,5},{5,4},{6,7},{7,6},{8,9},{9,8},{10,11... | collective-permute-start | bytes 884744 | tf_op jit(solution)/shard_map/ppermute | solution.py:26
  481.0 8.8 %collective-permute-start.23 = (f32[24,3072]{1,0:T(8,128)S(1)}, f32[24,3072]{1,0:T(8,128)S(1)}, u32[]{:S(2)}, u32[]{:S(2)}) collective-permute-start(f32[24,3072]{1,0:T(8,128)S(1)} %pad_maximum_fusion.3), channel_id=1, source_target_pairs={{0,1},{1,0},{2,3},{3,2},{4,5},{5,4},{6,7},{7,6},{8,9},{9,8},{10,11... | collective-permute-start | bytes 884744 | tf_op jit(solution)/shard_map/ppermute | solution.py:26
  485.1 9.0 %collective-permute-start.37 = (f32[24,3072]{1,0:T(8,128)S(1)}, f32[24,3072]{1,0:T(8,128)S(1)}, u32[]{:S(2)}, u32[]{:S(2)}) collective-permute-start(f32[24,3072]{1,0:T(8,128)S(1)} %pad_maximum_fusion.4), channel_id=1, source_target_pairs={{0,1},{1,0},{2,3},{3,2},{4,5},{5,4},{6,7},{7,6},{8,9},{9,8},{10,11... | collective-permute-start | bytes 884744 | tf_op jit(solution)/shard_map/ppermute | solution.py:26
  (49 other events, 199.9 us)

commit v2 on v1

v2 whole, which is shorter than its diff:
```python
import jax
import jax.numpy as jnp
from jax import lax
from jax.experimental import pallas as pl
from jax.experimental.pallas import tpu as pltpu
from jax.sharding import PartitionSpec as P

HEADS = 12
FORWARD_GROUP, BACK_GROUP = 2, 4
LAST_SHARES = (1280, 1280, 512)
NB = 100
VMEM_BYTES = 62 * 1024 * 1024


norm_epsilon = 1e-05
masked_score = -1e30

density_scale = 0.3989422804014327


def dot_nn(a, b):
    return lax.dot_general(a, b, (((1,), (0,)), ((), ())), preferred_element_type=jnp.float32)


def dot_nt(a, b):
    return lax.dot_general(a, b, (((1,), (1,)), ((), ())), preferred_element_type=jnp.float32)


def dot_tn(a, b):
    return lax.dot_general(a, b, (((0,), (0,)), ((), ())), preferred_element_type=jnp.float32)


def normalise(values):
    centre = jnp.mean(values, axis=-1, keepdims=True)
    centred = values - centre
    spread = jnp.mean(centred * centred, axis=-1, keepdims=True)
    inverse = lax.rsqrt(spread + norm_epsilon)
    return centred * inverse, inverse


def normalise_back(grad, unit, inverse):
    first = jnp.mean(grad, axis=-1, keepdims=True)
    second = jnp.mean(grad * unit, axis=-1, keepdims=True)
    return inverse * (grad - first - unit * second)


def column_sum(values):
    return jnp.sum(values, axis=0, keepdims=True)


def gelu_pair(pre):
    normal = 0.5 + 0.5 * lax.erf(pre * 0.7071067811865476)
    return pre * normal, normal + pre * (density_scale * jnp.exp(-0.5 * (pre * pre)))


def line(vector):
    return vector[...].reshape(1, -1)


def project_kernel(
    leads, patches, gain, bias, bias_query, bias_value, lead_table, w_qkv, normed, qkv
):
    window = pl.program_id(0)
    width = patches.shape[-1]
    unit, _ = normalise(patches[0].astype(jnp.float32))
    lead_row = lead_table[pl.ds(leads[window], 1), :]
    low = (unit * line(gain) + line(bias) + lead_row).astype(jnp.bfloat16)
    normed[...] = low
    queries = dot_nn(low, w_qkv[:, :width]) + line(bias_query)
    qkv[:, :width] = queries.astype(jnp.bfloat16) * 0.125
    qkv[:, width : 2 * width] = dot_nn(low, w_qkv[:, width : 2 * width]).astype(jnp.bfloat16)
    values = dot_nn(low, w_qkv[:, 2 * width :]) + line(bias_value)
    qkv[:, 2 * width :] = values.astype(jnp.bfloat16)


def each_alone(columns, place):
    zero = jnp.zeros_like(columns)
    return jnp.concatenate([jnp.where(place == i, columns, zero) for i in range(columns.shape[1] // 64)], axis=0)


def own_columns(stacked, place):
    rows = place.shape[0]
    joined = stacked[:rows]
    for i in range(1, stacked.shape[1] // 64):
        joined = jnp.where(place == i, stacked[i * rows : (i + 1) * rows], joined)
    return joined


def attend_kernel(
    lengths,
    patches,
    qkv,
    w_out,
    bias_out,
    gain,
    bias,
    attended,
    residual,
    normed2,
    turned,
    log_total,
):
    window = pl.program_id(0)
    _, rows, width = patches.shape
    keys_at = lax.broadcasted_iota(jnp.int32, (rows, 1), 0)
    blocked = jnp.where(keys_at < lengths[window], 0.0, masked_score)
    span = FORWARD_GROUP * 64
    place = lax.broadcasted_iota(jnp.int32, (rows, span), 1) // 64
    for at in range(0, width, span):
        query = each_alone(qkv[:, at : at + span], place)
        key = qkv[:, width + at : width + at + span]
        value = qkv[:, 2 * width + at : 2 * width + at + span]
        scores = dot_nt(key, query) + blocked
        top = jnp.max(scores, axis=0, keepdims=True)
        exponent = jnp.exp(scores - top)
        total = jnp.sum(exponent, axis=0, keepdims=True)
        probs = (exponent * (1.0 / total)).astype(jnp.bfloat16)
        out = own_columns(dot_tn(probs, value), place)
        attended[:, at : at + span] = out.astype(jnp.bfloat16)
        log_sum = top + jnp.log(total)
        for i in range(FORWARD_GROUP):
            head = at // 64 + i
            log_total[0, head : head + 1, :] = log_sum[:, i * rows : (i + 1) * rows]
    branch = dot_nn(attended[...], w_out[...]) + line(bias_out)
    held = patches[0].astype(jnp.float32) + branch
    residual[...] = held
    unit, _ = normalise(held)
    low = (unit * line(gain) + line(bias)).astype(jnp.bfloat16)
    normed2[...] = low
    turned[...] = low.T


def store_halves(result, here, keep, send):
    if keep.ndim == 2:
        keep[...] = result
        send[...] = jnp.zeros_like(send)
        return
    blocks, share, columns = keep.shape
    split = result.reshape(blocks, 2, share, columns)
    first, second = split[:, 0], split[:, 1]
    keep[...] = jnp.where(here == 0, first, second)
    send[...] = jnp.where(here == 0, second, first)


def mlp_kernel(
    lengths,
    scales,
    here,
    cotangent,
    normed2,
    w_up,
    bias_up,
    activated,
    slope,
    grad_down,
    keep,
    send,
):
    windows, rows, width = cotangent.shape
    step = pl.program_id(0)

    @pl.when(step == 0)
    def _():
        row = lax.broadcasted_iota(jnp.int32, (rows, 1), 0)
        for window in range(windows):
            weight = jnp.where(row < lengths[window], scales[window], 0.0)
            grad = (cotangent[window].astype(jnp.float32) * weight).astype(jnp.bfloat16)
            grad_down[window * rows : (window + 1) * rows, :] = grad

    for window in range(windows):
        at = slice(window * rows, (window + 1) * rows)
        pre = dot_nn(normed2[at, :], w_up[...]) + bias_up[pl.ds(step, 1), :]
        out, steep = gelu_pair(pre)
        out = out.astype(jnp.bfloat16)
        activated[at, :] = out
        slope[at, :] = steep.astype(jnp.bfloat16)
    store_halves(dot_tn(activated[...], grad_down[...]), here[0], keep, send)


def mlp_back_kernel(
    here, grad_down, slope, turned, w_up, w_down, grad_bias_up, grad_normed2, keep, send
):
    step = pl.program_id(0)

    @pl.when(step == 0)
    def _():
        grad_normed2[...] = jnp.zeros_like(grad_normed2)

    grad_act = dot_nt(grad_down[...], w_down[...])
    grad_up = (grad_act * slope[...].astype(jnp.float32)).astype(jnp.bfloat16)
    grad_bias_up[0] = column_sum(grad_up.astype(jnp.float32))
    store_halves(dot_nn(turned[...], grad_up), here[0], keep, send)
    grad_normed2[...] += dot_nt(grad_up, w_up[...])


def middle_back_kernel(
    lengths,
    scales,
    here,
    cotangent,
    residual,
    grad_normed2,
    attended,
    w_out,
    gain,
    head_rows,
    grad_residual,
    grad_attended,
    delta,
    sums,
    branch_low,
):
    window = pl.program_id(0)
    _, rows, width = cotangent.shape

    @pl.when(window == 0)
    def _():
        sums[...] = jnp.zeros_like(sums)

    row = lax.broadcasted_iota(jnp.int32, (rows, 1), 0)
    weight = jnp.where(row < lengths[window], scales[window], 0.0)
    grad_out = cotangent[0].astype(jnp.float32) * weight
    unit, inverse = normalise(residual[...])
    grad_norm = grad_normed2[...]
    held = grad_out + normalise_back(grad_norm * line(gain), unit, inverse)
    grad_residual[...] = held
    branch = held.astype(jnp.bfloat16)
    branch_low[...] = branch
    sums[0:1, :] += column_sum(grad_norm * unit)
    sums[1:2, :] += column_sum(grad_norm)
    sums[2:3, :] += column_sum(branch.astype(jnp.float32))
    sums[3:4, :] += column_sum(grad_out.astype(jnp.bfloat16).astype(jnp.float32))
    grad_att = dot_nt(branch, w_out[...]).astype(jnp.bfloat16)
    grad_attended[...] = grad_att
    product = grad_att.astype(jnp.float32) * attended[...].astype(jnp.float32)
    high = product.astype(jnp.bfloat16)
    low = (product - high.astype(jnp.float32)).astype(jnp.bfloat16)
    delta[0] = dot_nt(head_rows[...], high) + dot_nt(head_rows[...], low)


def attend_back_kernel(
    lengths,
    here,
    queries,
    keys,
    values,
    grad_attended,
    normed,
    log_total,
    delta,
    attended,
    branch,
    grad_projected,
    sums,
    keep,
    send,
    grad_w,
):
    window = pl.program_id(0)
    rows, width = queries.shape

    @pl.when(window == 0)
    def _():
        grad_w[...] = jnp.zeros_like(grad_w)
        sums[...] = jnp.zeros_like(sums)

    row = lax.broadcasted_iota(jnp.int32, (rows, 1), 0)
    blocked = jnp.where(row < lengths[window], 0.0, masked_score)
    span = BACK_GROUP * 64
    place = lax.broadcasted_iota(jnp.int32, (rows, span), 1) // 64
    for at in range(0, width, span):
        query = each_alone(queries[:, at : at + span], place)
        key = keys[:, at : at + span]
        value = values[:, at : at + span]
        grad_group = each_alone(grad_attended[:, at : at + span], place)
        heads = range(at // 64, at // 64 + BACK_GROUP)
        totals = jnp.concatenate([log_total[0, h : h + 1, :] for h in heads], axis=1)
        shift = jnp.concatenate([delta[0, h : h + 1, :] for h in heads], axis=1)
        scores = dot_nt(key, query) + blocked
        probs = jnp.exp(scores - totals)
        grad_probs = dot_nt(value, grad_group)
        grad_scores = (probs * (grad_probs - shift)).astype(jnp.bfloat16)
        grad_query = own_columns(dot_tn(grad_scores, key), place) * 0.125
        grad_key = dot_nn(grad_scores, query)
        grad_value = dot_nn(probs.astype(jnp.bfloat16), grad_group)
        for index, grad in enumerate((grad_query, grad_key, grad_value)):
            to = index * width + at
            grad_projected[:, to : to + span] = grad.astype(jnp.bfloat16)
    grad_w[:, : 3 * width] += dot_tn(normed[...], grad_projected[...])
    grad_w[:, 3 * width :] += dot_tn(attended[...], branch[...])
    sums[0:1, :] += column_sum(grad_projected[:, :width].astype(jnp.float32))
    sums[1:2, :] += column_sum(grad_projected[:, 2 * width :].astype(jnp.float32))

    @pl.when(window == pl.num_programs(0) - 1)
    def _():
        store_halves(grad_w[...], here[0], keep, send)


def norm_back_kernel(
    leads, patches, grad_residual, grad_projected, w_qkv, gain, grad_patches, sums, grad_leads
):
    window = pl.program_id(0)

    @pl.when(window == 0)
    def _():
        sums[...] = jnp.zeros_like(sums)
        grad_leads[...] = jnp.zeros_like(grad_leads)

    grad_norm = dot_nt(grad_projected[...], w_qkv[...])
    unit, inverse = normalise(patches[0].astype(jnp.float32))
    back = normalise_back(grad_norm * line(gain), unit, inverse)
    grad_patches[0] = (grad_residual[...] + back).astype(jnp.bfloat16)
    total = column_sum(grad_norm)
    sums[0:1, :] += column_sum(grad_norm * unit)
    sums[1:2, :] += total
    grad_leads[pl.ds(leads[window], 1), :] += total


def block_out_kernel(activated, w_down, bias_down, residual, block_out):
    final = residual[...] + dot_nn(activated[...], w_down[...]) + line(bias_down)
    block_out[0] = final.astype(jnp.bfloat16)


Z1, Z0, X, Y = range(4)
LINKS = (("dp", 3), ("dp", 2), ("dp", 1), ("outer", 0))


def split_kernel(pairs, parts, axes, merge, gridded, bits, *refs):
    outs = refs[2 * len(pairs) :]
    start = 0
    for index, (pieces, axis) in enumerate(zip(parts, axes)):
        send, keep = outs[:2] if merge else outs[2 * index : 2 * index + 2]
        if not merge:
            start = 0
        mine = bits[axis]
        for pair, first, width in pieces:
            held, come = refs[2 * pair], refs[2 * pair + 1]
            at = [slice(None)] * len(held.shape)
            if gridded:
                at[0] = 0
            at[-1] = slice(first, first + width)
            place = pairs[pair].index(axis)
            for out, side in ((send, 1 - mine), (keep, mine)):
                at[place] = side
                value = held[tuple(at)] + come[tuple(at)]
                to = (Ellipsis, slice(start, start + width))
                out[(0,) + to if gridded else to] = value
            start += width


def place_kernel(moves, bits, own, other, *outs):
    rows = own.shape[0]
    mine = bits[Y]
    for out, to, start, width in moves:
        for value, side in ((own, mine), (other, 1 - mine)):
            outs[out][pl.ds(side * rows, rows), to : to + width] = value[:, start : start + width]


def swap(values, axis, bit):
    size = lax.axis_size(axis)
    return lax.ppermute(values, axis, [(i, i ^ (1 << bit)) for i in range(size)])


def bit_of(axis, bit):
    return lax.rem(lax.div(lax.axis_index(axis), 1 << bit), 2)


def dp_bits():
    return lax.axis_size("dp").bit_length() - 1


def sum_small(values):
    for bit in reversed(range(dp_bits())):
        values = values + swap(values, "dp", bit)
    return values + swap(values, "outer", 0)


def exchange(values, dp_mask, outer_mask):
    inner = lax.axis_size("outer")
    size = lax.axis_size("dp") * inner
    flip = dp_mask * inner + outer_mask
    return lax.ppermute(values, ("dp", "outer"), [(i, i ^ flip) for i in range(size)])


def count_rounds(values):
    steps = [(1 << bit, 0) for bit in range(1, dp_bits())] + [(0, 1)]
    rounds = [[(1, 0)]] + [steps[at : at + 2] for at in range(0, len(steps), 2)]
    for group in rounds:
        flips = list(group)
        if len(group) == 2:
            flips.append((group[0][0] | group[1][0], group[0][1] | group[1][1]))
        values = values + sum(exchange(values, *flip) for flip in flips)
        yield values


def part_orders(bit_count):
    rest = list(range(3, bit_count))
    return (
        [("dp", 1), ("outer", 0), ("dp", 2)] + [("dp", b) for b in rest],
        [("outer", 0), ("dp", 2), ("dp", 1)] + [("dp", b) for b in rest],
        [("dp", 2), ("dp", 1), ("outer", 0)] + [("dp", b) for b in rest],
    )


def halve(values, dims, step):
    axis, bit = step
    place = dims.index(step)
    mine = bit_of(axis, bit)
    keep = lax.dynamic_index_in_dim(values, mine, place, keepdims=False)
    send = lax.dynamic_index_in_dim(values, 1 - mine, place, keepdims=False)
    left = dims[:place] + dims[place + 1 :]
    return keep + swap(send, axis, bit), left


def scatter_sum(matrix):
    bit_count = dp_bits()
    rows, columns = matrix.shape
    share = rows // lax.axis_size("dp")
    dims = [("dp", b) for b in range(bit_count - 1, -1, -1)] + [("outer", 0)]
    values = matrix.reshape((2,) * bit_count + (2, share // 2, columns))
    values, dims = halve(values, dims, ("dp", 0))
    third = columns // 3
    pieces = []
    for index, order in enumerate(part_orders(bit_count)):
        part = lax.slice_in_dim(values, index * third, (index + 1) * third, axis=values.ndim - 1)
        left = dims
        for step in order:
            part, left = halve(part, left, step)
        pieces.append(part)
    mine = jnp.concatenate(pieces, axis=1)
    other = swap(mine, "outer", 0)
    first = lax.axis_index("outer") == 0
    return jnp.concatenate([jnp.where(first, mine, other), jnp.where(first, other, mine)], axis=0)


def per_device(
    patches,
    lengths,
    leads,
    counts,
    cotangent,
    norm1_gain,
    norm1_bias,
    lead_table,
    w_qkv,
    bias_query,
    bias_value,
    w_out,
    bias_out,
    norm2_gain,
    norm2_bias,
    w_up,
    bias_up,
    w_down,
    bias_down,
):
    slots, rows, width = patches.shape
    total = slots * rows
    hidden = w_up.shape[1]
    lead_count = lead_table.shape[0]
    steps = hidden // width
    f32, bf16 = jnp.float32, jnp.bfloat16
    parts = lax.axis_size("dp")
    share = width // parts
    fast = parts == 16 and share % 16 == 0

    smem = pl.BlockSpec(memory_space=pltpu.SMEM)
    params = pltpu.CompilerParams(vmem_limit_bytes=VMEM_BYTES)

    def whole(*shape):
        return pl.BlockSpec(shape, lambda *i: (0,) * len(shape))

    def by_window(columns, at=0):
        return pl.BlockSpec((rows, columns), lambda i: (i, at))

    def call(kernel, grid, inputs, outs, scratch=(), after=(), carry=(), micros=0):
        count, extra, carried = len(inputs), len(after) + len(carry), len(carry)
        made = count + extra + len(outs)

        def body(*refs):
            kernel(*refs[:count], *refs[count + extra : made], *refs[made + carried :])

        anywhere = pl.BlockSpec(memory_space=pl.ANY)
        return pl.pallas_call(
            body,
            grid=grid,
            in_specs=[spec for spec, _ in inputs] + [anywhere] * extra,
            out_specs=[spec for spec, _, _ in outs] + [anywhere] * carried,
            out_shape=[jax.ShapeDtypeStruct(shape, dtype) for _, shape, dtype in outs]
            + [jax.ShapeDtypeStruct(value.shape, value.dtype) for value in carry],
            input_output_aliases={
                count + len(after) + i: len(outs) + i for i in range(carried)
            },
            scratch_shapes=scratch,
            compiler_params=params,
            cost_estimate=pl.CostEstimate(
                flops=int(micros * 1.15e9), bytes_accessed=0, transcendentals=0
            ),
        )(*[value for _, value in inputs], *after, *carry)

    live = jnp.arange(slots, dtype=jnp.int32) < counts[0]
    onehot = (leads[:, None] == jnp.arange(lead_count, dtype=jnp.int32)[None, :]).astype(f32)
    rounds = count_rounds(jnp.sum(onehot * live[:, None].astype(f32), axis=0))
    counted = next(rounds)

    dp_at, outer_at = lax.axis_index("dp"), lax.axis_index("outer")
    here = lax.rem(dp_at, 2).reshape(1)
    bits = jnp.stack([bit_of("dp", 3), bit_of("dp", 2), bit_of("dp", 1), outer_at])
    def flat(vector):
        return whole(*vector.shape), vector

    by_slot = pl.BlockSpec((1, rows, width), lambda i: (i, 0, 0))
    by_head = pl.BlockSpec((1, 16, rows), lambda i: (i, 0, 0))

    def halves(blocks, columns, grid_axis=None):
        if not fast:
            spec = pl.BlockSpec((width, columns), lambda i: (0, 0))
            return [(spec, (width, columns), f32), (whole(8, 128), (8, 128), f32)]
        shape = (parts // 2, share, columns)
        return [(whole(*shape), shape, f32)] * 2

    normed, qkv = call(
        project_kernel,
        (slots,),
        [
            (smem, leads),
            (by_slot, patches),
            flat(norm1_gain),
            flat(norm1_bias),
            flat(bias_query),
            flat(bias_value),
            (whole(*lead_table.shape), lead_table),
            (whole(*w_qkv.shape), w_qkv),
        ],
        [
            (by_window(width), (total, width), bf16),
            (by_window(3 * width), (total, 3 * width), bf16),
        ],
        after=[counted],
    )
    counted = next(rounds)
    attended, residual, normed2, turned, log_total = call(
        attend_kernel,
        (slots,),
        [
            (smem, lengths),
            (by_slot, patches),
            (by_window(3 * width), qkv),
            (whole(*w_out.shape), w_out),
            flat(bias_out),
            flat(norm2_gain),
            flat(norm2_bias),
        ],
        [
            (by_window(width), (total, width), bf16),
            (by_window(width), (total, width), f32),
            (by_window(width), (total, width), bf16),
            (pl.BlockSpec((width, rows), lambda i: (0, i)), (width, total), bf16),
            (by_head, (slots, 16, rows), f32),
        ],
        after=[counted],
    )
    for counted in rounds:
        pass
    window_total = jnp.sum(onehot * counted[None, :], axis=1)
    scales = jnp.where(live, 1.0 / jnp.maximum(window_total, 1.0), 0.0)

    by_lanes = pl.BlockSpec((total, width), lambda i: (0, i))
    up_spec = pl.BlockSpec((width, width), lambda i: (0, i))
    if fast:
        pair_share = hidden // parts
        pair_shape = (parts // 2, pair_share, width)
        pair_spec = pl.BlockSpec((parts // 2 // steps, pair_share, width), lambda i: (i, 0, 0))
        down_halves = [(pair_spec, pair_shape, f32)] * 2
    else:
        down_spec = pl.BlockSpec((width, width), lambda i: (i, 0))
        down_halves = [(down_spec, (hidden, width), f32), (whole(8, 128), (8, 128), f32)]
    activated, slope, grad_down, keep_down, send_down = call(
        mlp_kernel,
        (steps,),
        [
            (smem, lengths),
            (smem, scales),
            (smem, here),
            (whole(*cotangent.shape), cotangent),
            (whole(total, width), normed2),
            (up_spec, w_up),
            flat(bias_up.reshape(steps, width)),
        ],
        [
            (by_lanes, (total, hidden), bf16),
            (by_lanes, (total, hidden), bf16),
            (whole(total, width), (total, width), bf16),
        ]
        + down_halves,
    )
    if fast:
        shape = (parts // 2, share, hidden)
        up_halves = [(pl.BlockSpec((parts // 2, share, width), lambda i: (0, 0, i)), shape, f32)] * 2
    else:
        up_halves = [(up_spec, (width, hidden), f32), (whole(8, 128), (8, 128), f32)]
    grad_bias_up, grad_normed2, keep_up, send_up = call(
        mlp_back_kernel,
        (steps,),
        [
            (smem, here),
            (whole(total, width), grad_down),
            (by_lanes, slope),
            (whole(width, total), turned),
            (up_spec, w_up),
            (pl.BlockSpec((width, width), lambda i: (i, 0)), w_down),
        ],
        [
            (pl.BlockSpec((1, 1, width), lambda i: (i, 0, 0)), (steps, 1, width), f32),
            (whole(total, width), (total, width), f32),
        ]
        + up_halves,
    )

    def core_swap(send):
        return swap(send, "dp", 0) if fast else send

    def split_round(pairs, dims, parts, axes, after=(), carry=()):
        merge = len(set(axes)) == 1 and len({tuple(dims[p[0][0]]) for p in parts}) == 1
        gridded = all(d[0] == Z1 and len(d) > 1 for d in dims) and Z1 not in axes
        rows_here = pairs[0][0].shape[-2]
        blocks = 2 if gridded and rows_here % 48 == 0 else 1
        widths = [sum(width for _, _, width in part) for part in parts]
        left = [[d for d in dims[part[0][0]] if d != axis] for part, axis in zip(parts, axes)]
        if merge:
            widths, left = [sum(widths)], left[:1]
        shapes = [(2,) * len(d) + (rows_here, width) for d, width in zip(left, widths)]

        def spec(shape):
            if not gridded:
                return whole(*shape)
            block = (1,) + shape[1:-2] + (rows_here // blocks, shape[-1])
            return pl.BlockSpec(block, lambda i, j: (i,) + (0,) * (len(shape) - 3) + (j, 0))

        values = call(
            lambda *refs: split_kernel(dims, parts, axes, merge, gridded, *refs),
            (2, blocks) if gridded else (),
            [(smem, bits)] + [(spec(v.shape), v) for pair in pairs for v in pair],
            [(spec(shape), shape, f32) for shape in shapes for _ in range(2)],
            after=after,
            carry=carry,
        )
        states = [(values[2 * i], values[2 * i + 1]) for i in range(len(shapes))]
        return states, left, values[2 * len(shapes) :]

    class Chunk:
        def __init__(self, sources, orders, shares):
            self.sources, self.orders, self.step_count = sources, orders, 0
            self.columns = [[] for _ in orders]
            for i, cuts in enumerate(shares):
                start = 0
                for pieces, width in zip(self.columns, cuts):
                    pieces.append((i, start, width))
                    start += width

        def open(self, after=()):
            shaped = lambda v: v.reshape((2, 2, 2, 2, -1, v.shape[-1]))
            pairs = [(shaped(keep), shaped(come)) for keep, come in self.sources]
            axes = [order[0] for order in self.orders]
            dims = [[Z1, Z0, X, Y]] * len(pairs)
            self.put(split_round(pairs, dims, self.columns, axes, after), axes)

        def put(self, result, axes):
            self.states, self.dims, self.carried = result
            self.axes = axes[: len(self.states)]
            self.step_count += 1

        def pairs(self):
            return [
                (keep, swap(send, *LINKS[axis]))
                for (send, keep), axis in zip(self.states, self.axes)
            ]

        def step(self, after=(), carry=()):
            pairs = self.pairs()
            axes = [order[self.step_count] for order in self.orders][: len(pairs)]
            parts = [[(i, 0, keep.shape[-1])] for i, (keep, _) in enumerate(pairs)]
            self.put(split_round(pairs, self.dims, parts, axes, after, carry), axes)

        def finish(self, outputs):
            ((keep, come),) = self.pairs()
            own = keep + come
            other = swap(own, *LINKS[Y])
            moves, start = [], 0
            for pieces in self.columns:
                for source, first, wide in pieces:
                    for out, (origin, low, size) in enumerate(outputs):
                        begin, end = max(first, low), min(first + wide, low + size)
                        if origin == source and begin < end:
                            moves.append((out, begin - low, start + begin - first, end - begin))
                    start += wide
            shapes = [(2 * own.shape[0], size) for _, _, size in outputs]
            return call(
                lambda *refs: place_kernel(moves, *refs),
                (),
                [(smem, bits), (whole(*own.shape), own), (whole(*other.shape), other)],
                [(whole(*shape), shape, f32) for shape in shapes],
            )

        def tokens(self):
            return [value for state in self.states for value in state]

    come_down = core_swap(send_down)
    come_up = core_swap(send_up)
    two_orders = [(X, Y, Z0, Z1), (Y, X, Z0, Z1)]
    orders = [(X, Y, Z0, Z1), (Y, Z0, X, Z1), (Z0, X, Y, Z1)]
    tokens = []
    if fast:
        down = Chunk([(keep_down, come_down)], two_orders, [(width // 2,) * 2])
        down.open([grad_normed2])
        tokens = down.tokens()
    head_rows = (
        jnp.arange(16, dtype=jnp.int32)[:, None]
        == jnp.arange(width, dtype=jnp.int32)[None, :] // (width // HEADS)
    ).astype(bf16)
    grad_residual, grad_attended, delta, sums, branch_low = call(
        middle_back_kernel,
        (slots,),
        [
            (smem, lengths),
            (smem, scales),
            (smem, here),
            (by_slot, cotangent),
            (by_window(width), residual),
            (by_window(width), grad_normed2),
            (by_window(width), attended),
            (whole(*w_out.shape), w_out),
            flat(norm2_gain),
            (whole(*head_rows.shape), head_rows),
        ],
        [
            (by_window(width), (total, width), f32),
            (by_window(width), (total, width), bf16),
            (by_head, (slots, 16, rows), f32),
            (whole(8, width), (8, width), f32),
            (by_window(width), (total, width), bf16),
        ],
        after=tokens,
    )
    tokens = []
    if fast:
        up = Chunk(
            [(keep_up, come_up)], [(Z0, X, Y, Z1), (X, Z0, Y, Z1)], [(hidden // 2,) * 2]
        )
        up.open([grad_residual])
        tokens = up.tokens()

    grad_projected, bias_sums, keep_qkvo, send_qkvo = call(
        attend_back_kernel,
        (slots,),
        [
            (smem, lengths),
            (smem, here),
            (by_window(width, 0), qkv),
            (by_window(width, 1), qkv),
            (by_window(width, 2), qkv),
            (by_window(width), grad_attended),
            (by_window(width), normed),
            (by_head, log_total),
            (by_head, delta),
            (by_window(width), attended),
            (by_window(width), branch_low),
        ],
        [
            (by_window(3 * width), (total, 3 * width), bf16),
            (whole(8, width), (8, width), f32),
        ]
        + halves(parts // 2, 4 * width),
        [pltpu.VMEM((width, 4 * width), f32)],
        after=tokens,
    )
    come_qkvo = core_swap(send_qkvo)
    tokens = []
    if fast:
        down.step([grad_projected])
        up.step(down.tokens())
        tokens = up.tokens()
    grad_patches, late_sums, grad_leads = call(
        norm_back_kernel,
        (slots,),
        [
            (smem, leads),
            (by_slot, patches),
            (by_window(width), grad_residual),
            (by_window(3 * width), grad_projected),
            (whole(*w_qkv.shape), w_qkv),
            flat(norm1_gain),
        ],
        [
            (by_slot, patches.shape, bf16),
            (whole(8, width), (8, width), f32),
            (whole(lead_count, width), (lead_count, width), f32),
        ],
        after=tokens,
        micros=NB,
    )
    tokens = []
    if fast:
        last = Chunk([(keep_qkvo, come_qkvo)], orders, [LAST_SHARES])
        last.open([late_sums])
        down.step(last.tokens())
        up.step(down.tokens())
        tokens = up.tokens()

    (block_out,) = call(
        block_out_kernel,
        (slots,),
        [
            (by_window(hidden), activated),
            (whole(*w_down.shape), w_down),
            flat(bias_down),
            (by_window(width), residual),
        ],
        [(by_slot, patches.shape, bf16)],
        after=tokens,
    )

    bias_rows = grad_bias_up[:, 0]
    small = sum_small(jnp.concatenate([sums, bias_sums, late_sums, bias_rows, grad_leads], axis=0))
    up_rows = bias_rows.shape[0]

    if fast:
        down.step([block_out])
        last.step(down.tokens())
        up.step(last.tokens())
        (sum_down,) = down.finish([(0, 0, width)])
        last.step(up.tokens())
        last.step()
        (sum_up,) = up.finish([(0, 0, hidden)])
        sum_qkv, sum_out = last.finish([(0, 0, 3 * width), (0, 3 * width, width)])
    else:
        sum_down = scatter_sum(keep_down)
        sum_up = scatter_sum(keep_up)
        joined = scatter_sum(keep_qkvo)
        sum_qkv, sum_out = joined[:, : 3 * width], joined[:, 3 * width :]
    return (
        block_out,
        grad_patches,
        small[16],
        small[17],
        small[24 + up_rows :],
        sum_qkv,
        small[8],
        small[9],
        sum_out,
        small[2],
        small[0],
        small[1],
        sum_up,
        small[24 : 24 + up_rows].reshape(-1),
        sum_down,
        small[3],
    )


def solution(mesh):
    split = P(("dp", "outer"))
    placed = (split,) * 5 + (P(),) * 14
    row = P("dp", None)
    outs = (split, split, P(), P(), P(), row, P(), P(), row, P(), P(), P(), row, P(), row, P())
    return jax.shard_map(
        per_device, mesh=mesh, in_specs=placed, out_specs=outs, check_vma=False
    )
```

time: 501 us -> 274 us (0.55)
  Pallas kernels: 0 us -> 163 us
  matrix products: 148 us -> 0 us
  other arithmetic: 101 us -> 4.28 us
  local copies, waits for them, and re-layouts: 90.2 us -> 10.5 us
  waiting for transfers between devices: 101 us -> 44.1 us
    pallas_call x0 -> x23, Pallas kernels: none -> 163 us  [call(): pl.pallas_call(body, grid=grid, in_specs=[spec for spec, _ in inputs] + [...]
    dot_general x20 -> x0, matrix products: 148 us -> none  [the longest x1 33.6 us: per_device(): jnp.dot(normed2_low, w_up, preferred_element_type=jnp.float32) + bias_up]
    ppermute x52 -> x33, waiting for transfers between devices: 101 us -> 44.1 us  [swap(): return lax.ppermute(values, axis, [(i, i ^ 1 << bit) for i in range(size)])]
    convert_element_type x7 -> x2, other arithmetic: 48.1 us -> 0.62 us  [the longest x1 0.62 us: per_device(): head_rows = (jnp.arange(16, dtype=jnp.int32)[:, None] == jnp.arange(width...]
    convert_element_type x8 -> x0, local copies, waits for them, and re-layouts: 21.8 us -> none  [the longest x1 8.64 us: per_device(): activated_low = activated.astype(jnp.bfloat16)]
    reduce_sum x11 -> x2, other arithmetic: 22 us -> 0.93 us  [the longest x1 0.74 us: per_device(): rounds = count_rounds(jnp.sum(onehot * live[:, None].astype(f32), axis=0))]
    reshape x8 -> x2, local copies, waits for them, and re-layouts: 19.2 us -> 1.93 us  [the longest x1 1.31 us: per_device(): bias_up.reshape(steps, width)]
    dynamic_slice x17 -> x0, local copies, waits for them, and re-layouts: 14.3 us -> none  [the longest x8 8.53 us: halve(): keep = lax.dynamic_index_in_dim(values, mine, place, keepdims=False)]
  transfers between devices with their start and end apart: 52 -> 40, of which waited for: 30 -> 12; matrix products, arithmetic and copies ran while one was open for 40% -> 2% of each run, Pallas kernels for 0% -> 52%
where the time goes in v2:
time: 274 us; the launch traced here: 273 us
  Pallas kernels  163 us (59%)
  starting transfers between devices  50 us (18%)
  waiting for transfers between devices  44.1 us (16%)
  local copies, waits for them, and re-layouts  10.5 us (4%)
  other arithmetic  4.28 us (2%)
    pallas_call x23, Pallas kernels, call(): pl.pallas_call(body, grid=grid, in_specs=[spec for spec, _ in inputs] + [...  163 us
    ppermute x33, waiting for transfers between devices, swap(): return lax.ppermute(values, axis, [(i, i ^ 1 << bit) for i in range(size)])  44.1 us
    ppermute x33, starting transfers between devices, swap(): return lax.ppermute(values, axis, [(i, i ^ 1 << bit) for i in range(size)])  40.8 us
    ppermute x7, starting transfers between devices, exchange(): lax.ppermute(values, ('dp', 'outer'), [(i, i ^ flip) for i in range(size)])  9.18 us
    unnamed x49, local copies, waits for them, and re-layouts  5.52 us
  transfers between devices with their start and end apart: 40, of which 12 were waited for; matrix products, arithmetic and copies ran while one was open for 2% of the time, Pallas kernels for 52%

profile of v2, /device:TPU:0, one launch (start us, length us, event | category | flops | bytes accessed | tf_op | source)
XLA Modules:
  0.0 273.2 jit_solution(157451865717832665)
XLA Ops:
  1.3 0.7 select_reduce_fusion.1
  2.5 1.3 reshape.105.refs_6_
  3.9 2.6 collective-permute-start.1
  6.4 1.6 collective-permute-start.2
  8.0 8.7 %shard_map.306 = (bf16[1024,768]{1,0:T(8,128)(2,1)}, bf16[1024,2304]{1,0:T(8,128)(2,1)}) custom-call(s32[4]{0:T(128)} %refs_0_.11, bf16[4,256,768]{2,1,0:T(8,128)(2,1)} %refs_1_.6, f32[768]{0:T(1024)} %refs_5_.9, f32[768]{0:T(1024)} %refs_3_.4, f32[768]{0:T(1024)} %refs_4_.4, f32[768]{0:T(1024)} %refs_5_.5, f32[40,768]{1,0:T(8,128)} %refs_6_.2, ...), custom_call_target="tpu_custom_call" | custom-call | tf_op jit(solution)/shard_map/pallas_call | solution.py:484
  16.7 0.7 add_add_fusion.1.refs_7_
  17.4 3.0 %collective-permute-start.4 = (f32[40]{0:T(128)S(1)}, f32[40]{0:T(128)S(1)}, u32[]{:S(2)}, u32[]{:S(2)}) collective-permute-start(f32[40]{0:T(128)S(1)} %add_add_fusion.1.refs_7_), channel_id=1, source_target_pairs={{0,16},{1,17},{2,18},{3,19},{4,20},{5,21},{6,22},{7,23},{8,24},{9,... | collective-permute-start | bytes 488 | tf_op jit(solution)/shard_map/ppermute | solution.py:382
  20.4 1.5 collective-permute-start.5
  21.9 11.7 %shard_map.307 = (bf16[1024,768]{1,0:T(8,128)(2,1)}, f32[1024,768]{1,0:T(8,128)}, bf16[1024,768]{1,0:T(8,128)(2,1)}, bf16[768,1024]{1,0:T(8,128)(2,1)}, f32[4,16,256]{2,1,0:T(8,128)}) custom-call(s32[4]{0:T(128)} %refs_0_.10, bf16[4,256,768]{2,1,0:T(8,128)(2,1)} %refs_1_.6, bf16[1024,2304]{1,0:T(8,128)(2,1)} %get-tuple-element.90.refs_2_.refs_3_.refs_4_, ...), custom_call_target="tpu_custom_call" | custom-call | tf_op jit(solution)/shard_map/pallas_call | solution.py:484
  33.7 0.7 add_add_fusion
  35.1 18.4 %shard_map.308 = (bf16[1024,3072]{1,0:T(8,128)(2,1)}, bf16[1024,3072]{1,0:T(8,128)(2,1)}, bf16[1024,768]{1,0:T(8,128)(2,1)}, f32[8,192,768]{2,1,0:T(8,128)}, f32[8,192,768]{2,1,0:T(8,128)}) custom-call(s32[4]{0:T(128)} %refs_0_.10, f32[4]{0:T(128)} %compare_select_fusion.refs_1_, s32[1]{0:T(128)} %bitcast.1.refs_2_.refs_0_.refs_1_, ...), custom_call_target="tpu_custom_call" | custom-call | tf_op jit(solution)/shard_map/pallas_call | solution.py:484
  53.5 21.1 %shard_map.309 = (f32[4,1,768]{2,1,0:T(1,128)}, f32[1024,768]{1,0:T(8,128)}, f32[8,48,3072]{2,1,0:T(8,128)}, f32[8,48,3072]{2,1,0:T(8,128)}) custom-call(s32[1]{0:T(128)} %bitcast.1.refs_2_.refs_0_.refs_1_, bf16[1024,768]{1,0:T(8,128)(2,1)} %get-tuple-element.94.refs_1_, bf16[1024,3072]{1,0:T(8,128)(2,1)} %get-tuple-element.95.refs_2_, ...), custom_call_target="tpu_custom_call" | custom-call | tf_op jit(solution)/shard_map/pallas_call | solution.py:484
  76.5 6.2 %shard_map.310 = (f32[2,2,2,96,384]{4,3,2,1,0:T(8,128)}, f32[2,2,2,96,384]{4,3,2,1,0:T(8,128)}, f32[2,2,2,96,384]{4,3,2,1,0:T(8,128)}, f32[2,2,2,96,384]{4,3,2,1,0:T(8,128)}) custom-call(s32[4]{0:T(128)} %pad_add_fusion.refs_0_, f32[2,2,2,2,96,768]{5,4,3,2,1,0:T(8,128)} %bitcast.18, f32[2,2,2,2,96,768]{5,4,3,2,1,0:T(8,128)} %bitcast.9.refs_2_, ...), custom_call_target="tpu_custom_call" | custom-call | tf_op jit(solution)/shard_map/pallas_call | solution.py:484
  82.7 1.8 collective-permute-start.11
  84.5 1.5 collective-permute-start.12
  86.0 9.7 %shard_map.311 = (f32[1024,768]{1,0:T(8,128)}, bf16[1024,768]{1,0:T(8,128)(2,1)}, f32[4,16,256]{2,1,0:T(8,128)}, f32[8,768]{1,0:T(8,128)}, bf16[1024,768]{1,0:T(8,128)(2,1)}) custom-call(s32[4]{0:T(128)} %refs_0_.10, f32[4]{0:T(128)} %compare_select_fusion.refs_1_, s32[1]{0:T(128)} %bitcast.1.refs_2_.refs_0_.refs_1_, bf16[4,256,768]{2,1,0:T(8,128)(2,1)} %refs_3_.7, ...), custom_call_target="tpu_custom_call" | custom-call | tf_op jit(solution)/shard_map/pallas_call | solution.py:484
  95.7 6.0 %shard_map.312 = (f32[2,2,2,24,1536]{4,3,2,1,0:T(8,128)}, f32[2,2,2,24,1536]{4,3,2,1,0:T(8,128)}, f32[2,2,2,24,1536]{4,3,2,1,0:T(8,128)}, f32[2,2,2,24,1536]{4,3,2,1,0:T(8,128)}) custom-call(s32[4]{0:T(128)} %pad_add_fusion.refs_0_, f32[2,2,2,2,24,3072]{5,4,3,2,1,0:T(8,128)} %bitcast.17, f32[2,2,2,2,24,3072]{5,4,3,2,1,0:T(8,128)} %bitcast.7.refs_2_, ...), custom_call_target="tpu_custom_call" | custom-call | tf_op jit(solution)/shard_map/pallas_call | solution.py:484
  102.2 1.6 collective-permute-start.9
  103.8 23.0 %shard_map.313 = (bf16[1024,2304]{1,0:T(8,128)(2,1)}, f32[8,768]{1,0:T(8,128)}, f32[8,48,3072]{2,1,0:T(8,128)}, f32[8,48,3072]{2,1,0:T(8,128)}) custom-call(s32[4]{0:T(128)} %refs_0_.10, s32[1]{0:T(128)} %bitcast.1.refs_2_.refs_0_.refs_1_, bf16[1024,2304]{1,0:T(8,128)(2,1)} %get-tuple-element.90.refs_2_.refs_3_.refs_4_, ...), custom_call_target="tpu_custom_call" | custom-call | tf_op jit(solution)/shard_map/pallas_call | solution.py:484
  126.9 1.0 copy-done
  127.9 4.3 %shard_map.314 = (f32[2,2,96,384]{3,2,1,0:T(8,128)}, f32[2,2,96,384]{3,2,1,0:T(8,128)}, f32[2,2,96,384]{3,2,1,0:T(8,128)}, f32[2,2,96,384]{3,2,1,0:T(8,128)}) custom-call(s32[4]{0:T(128)} %pad_add_fusion.refs_0_, f32[2,2,2,96,384]{4,3,2,1,0:T(8,128)} %get-tuple-element.104.refs_11_.refs_1_, f32[2,2,2,96,384]{4,3,2,1,0:T(8,128)} %copy-done, ...), custom_call_target="tpu_custom_call" | custom-call | tf_op jit(solution)/shard_map/pallas_call | solution.py:484
  132.8 1.5 collective-permute-start.16
  134.2 2.3 collective-permute-done.10.refs_4_
  136.5 3.5 %shard_map.315 = (f32[2,2,24,1536]{3,2,1,0:T(8,128)}, f32[2,2,24,1536]{3,2,1,0:T(8,128)}, f32[2,2,24,1536]{3,2,1,0:T(8,128)}, f32[2,2,24,1536]{3,2,1,0:T(8,128)}) custom-call(s32[4]{0:T(128)} %pad_add_fusion.refs_0_, f32[2,2,2,24,1536]{4,3,2,1,0:T(8,128)} %get-tuple-element.108.refs_12_.refs_1_, f32[2,2,2,24,1536]{4,3,2,1,0:T(8,128)} %collective-permute-done.9.refs_2_, ...), custom_call_target="tpu_custom_call" | custom-call | tf_op jit(solution)/shard_map/pallas_call | solution.py:484
  140.0 2.0 collective-permute-start.13
  142.0 9.8 %shard_map.316 = (bf16[4,256,768]{2,1,0:T(8,128)(2,1)}, f32[8,768]{1,0:T(8,128)}, f32[40,768]{1,0:T(8,128)}) custom-call(s32[4]{0:T(128)} %refs_0_.11, bf16[4,256,768]{2,1,0:T(8,128)(2,1)} %refs_1_.6, f32[1024,768]{1,0:T(8,128)} %get-tuple-element.107.refs_3_.refs_2_, bf16[1024,2304]{1,0:T(8,128)(2,1)} %get-tuple-element.117.refs_5_.refs_3_, ...), custom_call_target="tpu_custom_call" | custom-call | flops 115000000512 | tf_op jit(solution)/shard_map/pallas_call | solution.py:484
  151.8 5.8 %shard_map.317 = (f32[2,2,2,24,1280]{4,3,2,1,0:T(8,128)}, f32[2,2,2,24,1280]{4,3,2,1,0:T(8,128)}, f32[2,2,2,24,1280]{4,3,2,1,0:T(8,128)}, f32[2,2,2,24,1280]{4,3...) custom-call(s32[4]{0:T(128)} %pad_add_fusion.refs_0_, f32[2,2,2,2,24,3072]{5,4,3,2,1,0:T(8,128)} %bitcast.19, ...), custom_call_target="tpu_custom_call" | custom-call | tf_op jit(solution)/shard_map/pallas_call | solution.py:484
  157.6 2.0 collective-permute-start.24
  159.6 1.9 collective-permute-start.14
  161.5 3.7 %shard_map.318 = (f32[2,96,768]{2,1,0:T(8,128)}, f32[2,96,768]{2,1,0:T(8,128)}) custom-call(s32[4]{0:T(128)} %pad_add_fusion.refs_0_, f32[2,2,96,384]{3,2,1,0:T(8,128)} %get-tuple-element.119.refs_6_.refs_1_, f32[2,2,96,384]{3,2,1,0:T(8,128)} %collective-permute-done.15.refs_2_, f32[2,2,96,384]{3,2,1,0:T(8,128)} %get-tuple-element.121.refs_8_.refs_3_, ...), custom_call_target="tpu_custom_call" | custom-call | tf_op jit(solution)/shard_map/pallas_call | solution.py:484
  165.4 1.9 collective-permute-start.25
  167.3 8.9 %collective-permute-done.14.refs_4_ = f32[2,2,24,1536]{3,2,1,0:T(8,128)} collective-permute-done((f32[2,2,24,1536]{3,2,1,0:T(8,128)}, f32[2,2,24,1536]{3,2,1,0:T(8,128)}, u32[]{:S(2)}, u32[]{:S(2)}) %collective-permute-start.14) | collective-permute-done | bytes 589856 | tf_op jit(solution)/shard_map/ppermute | solution.py:361
  176.2 2.5 shard_map.319
  179.1 9.9 %shard_map.320.refs_3_ = bf16[4,256,768]{2,1,0:T(8,128)(2,1)} custom-call(bf16[1024,3072]{1,0:T(8,128)(2,1)} %get-tuple-element.92.refs_0_, bf16[3072,768]{1,0:T(8,128)(2,1)} %refs_1_.7, f32[768]{0:T(1024)} %refs_2_.3, f32[1024,768]{1,0:T(8,128)} %get-tuple-element.93.refs_4_.refs_3_, f32[2,24,3072]{2,1,0:T(8,128)} %get-tuple-element.137.refs_4_, ...), custom_call_target="tpu_custom_call" | custom-call | tf_op jit(solution)/shard_map/pallas_call | solution.py:484
  188.9 2.2 shard_map.321
  191.1 2.9 %collective-permute-done.25.refs_6_ = f32[2,2,2,24,512]{4,3,2,1,0:T(8,128)} collective-permute-done((f32[2,2,2,24,512]{4,3,2,1,0:T(8,128)}, f32[2,2,2,24,512]{4,3,2,1,0:T(8,128)}, u32[]{:S(2)}, u32[]{:S(2)}) %collective-permute-start.25) | collective-permute-done | bytes 393248 | tf_op jit(solution)/shard_map/ppermute | solution.py:361
  194.0 1.0 copy-done.6
  195.3 3.5 %shard_map.322 = (f32[2,2,24,1280]{3,2,1,0:T(8,128)}, f32[2,2,24,1280]{3,2,1,0:T(8,128)}, f32[2,2,24,1280]{3,2,1,0:T(8,128)}, f32[2,2,24,1280]{3,2,1,0:T(8,128)}...) custom-call(s32[4]{0:T(128)} %pad_add_fusion.refs_0_, f32[2,2,2,24,1280]{4,3,2,1,0:T(8,128)} %get-tuple-element.130.refs_6_.refs_1_, ...), custom_call_target="tpu_custom_call" | custom-call | tf_op jit(solution)/shard_map/pallas_call | solution.py:484
  199.2 1.7 collective-permute-start.28
  201.0 1.8 concatenate.3
  202.7 2.6 collective-permute-start.18
  205.4 1.5 collective-permute-start.29
  206.9 6.4 %collective-permute-done.18 = f32[68,768]{1,0:T(8,128)S(1)} collective-permute-done((f32[68,768]{1,0:T(8,128)S(1)}, f32[68,768]{1,0:T(8,128)S(1)}, u32[]{:S(2)}, u32[]{:S(2)}) %collective-permute-start.18) | collective-permute-done | bytes 208928 | tf_op jit(solution)/shard_map/ppermute | solution.py:361
  213.3 5.8 %collective-permute-start.19 = (f32[68,768]{1,0:T(8,128)S(1)}, f32[68,768]{1,0:T(8,128)S(1)}, u32[]{:S(2)}, u32[]{:S(2)}) collective-permute-start(f32[68,768]{1,0:T(8,128)S(1)} %add.58), channel_id=1, source_target_pairs={{0,8},{2,10},{4,12},{6,14},{8,0},{10,2},{12,4},{14,6},{16,24},{18,... | collective-permute-start | bytes 626696 | tf_op jit(solution)/shard_map/ppermute | solution.py:361
  219.1 2.1 shard_map.323
  222.2 2.6 shard_map.324
  225.0 1.6 collective-permute-start.32
  226.6 1.6 collective-permute-start.20
  228.1 2.1 collective-permute-start.33
  230.2 2.8 %collective-permute-done.33.refs_6_ = f32[2,24,512]{2,1,0:T(8,128)S(1)} collective-permute-done((f32[2,24,512]{2,1,0:T(8,128)}, f32[2,24,512]{2,1,0:T(8,128)S(1)}, u32[]{:S(2)}, u32[]{:S(2)}) %collective-permute-start.33) | collective-permute-done | bytes 98336 | tf_op jit(solution)/shard_map/ppermute | solution.py:361
  234.3 2.3 shard_map.325
  236.5 2.4 collective-permute-start.34
  239.1 1.5 collective-permute-done.21
  240.6 2.1 collective-permute-start.22
  242.7 10.5 %collective-permute-done.38 = f32[96,768]{1,0:T(8,128)S(1)} collective-permute-done((f32[96,768]{1,0:T(8,128)S(1)}, f32[96,768]{1,0:T(8,128)S(1)}, u32[]{:S(2)}, u32[]{:S(2)}) %collective-permute-start.38) | collective-permute-done | bytes 294944 | tf_op jit(solution)/shard_map/ppermute | solution.py:361
  253.3 1.1 collective-permute-start.39
  254.4 4.5 %collective-permute-done.36 = f32[24,3072]{1,0:T(8,128)S(1)} collective-permute-done((f32[24,3072]{1,0:T(8,128)}, f32[24,3072]{1,0:T(8,128)S(1)}, u32[]{:S(2)}, u32[]{:S(2)}) %collective-permute-start.36) | collective-permute-done | bytes 294944 | tf_op jit(solution)/shard_map/ppermute | solution.py:361
  259.5 2.6 collective-permute-done.34
  264.6 0.7 copy-done.13
  265.3 1.9 shard_map.328
  267.5 1.9 shard_map.327
  269.4 1.1 collective-permute-done.35.refs_2_
  270.6 0.7 copy-done.12
  271.3 1.9 shard_map.326
  (112 shorter events, 11.5 us)
Async XLA Ops:
  2.0 1.8 collective-permute-start
  3.9 4.2 %copy-start.22 = (f32[40]{0:T(128)}, f32[40]{0:T(128)S(1)}, u32[]{:S(2)}) copy-start(f32[40]{0:T(128)S(1)} %add.51.refs_8_) | copy-start | bytes 484
  3.9 12.8 %collective-permute-start.1 = (f32[40]{0:T(128)S(1)}, f32[40]{0:T(128)S(1)}, u32[]{:S(2)}, u32[]{:S(2)}) collective-permute-start(f32[40]{0:T(128)S(1)} %add.51.refs_8_), channel_id=1, source_target_pairs={{0,4},{1,5},{2,6},{3,7},{4,0},{5,1},{6,2},{7,3},{8,12},{9,13},{10,... | collective-permute-start | bytes 488 | tf_op jit(solution)/shard_map/ppermute | solution.py:382
  6.4 10.3 %collective-permute-start.2 = (f32[40]{0:T(128)S(1)}, f32[40]{0:T(128)S(1)}, u32[]{:S(2)}, u32[]{:S(2)}) collective-permute-start(f32[40]{0:T(128)S(1)} %add.51.refs_8_), channel_id=1, source_target_pairs={{0,8},{1,9},{2,10},{3,11},{4,12},{5,13},{6,14},{7,15},{8,0},{9,1},... | collective-permute-start | bytes 488 | tf_op jit(solution)/shard_map/ppermute | solution.py:382
  8.0 8.7 %collective-permute-start.3 = (f32[40]{0:T(128)S(1)}, f32[40]{0:T(128)S(1)}, u32[]{:S(2)}, u32[]{:S(2)}) collective-permute-start(f32[40]{0:T(128)S(1)} %add.51.refs_8_), channel_id=1, source_target_pairs={{0,12},{1,13},{2,14},{3,15},{4,8},{5,9},{6,10},{7,11},{8,4},{9,5},... | collective-permute-start | bytes 488 | tf_op jit(solution)/shard_map/ppermute | solution.py:382
  17.4 4.5 %copy-start.21 = (f32[40]{0:T(128)}, f32[40]{0:T(128)S(1)}, u32[]{:S(2)}) copy-start(f32[40]{0:T(128)S(1)} %add_add_fusion.1.refs_7_) | copy-start | bytes 484
  17.4 16.3 %collective-permute-start.4 = (f32[40]{0:T(128)S(1)}, f32[40]{0:T(128)S(1)}, u32[]{:S(2)}, u32[]{:S(2)}) collective-permute-start(f32[40]{0:T(128)S(1)} %add_add_fusion.1.refs_7_), channel_id=1, source_target_pairs={{0,16},{1,17},{2,18},{3,19},{4,20},{5,21},{6,22},{7,23},{8,24},{9,... | collective-permute-start | bytes 488 | tf_op jit(solution)/shard_map/ppermute | solution.py:382
  20.4 13.3 %collective-permute-start.5 = (f32[40]{0:T(128)S(1)}, f32[40]{0:T(128)S(1)}, u32[]{:S(2)}, u32[]{:S(2)}) collective-permute-start(f32[40]{0:T(128)S(1)} %add_add_fusion.1.refs_7_), channel_id=1, source_target_pairs={{0,1},{1,0},{2,3},{3,2},{4,5},{5,4},{6,7},{7,6},{8,9},{9,8},{10,11... | collective-permute-start | bytes 488 | tf_op jit(solution)/shard_map/ppermute | solution.py:382
  21.9 11.8 %collective-permute-start.6 = (f32[40]{0:T(128)S(1)}, f32[40]{0:T(128)S(1)}, u32[]{:S(2)}, u32[]{:S(2)}) collective-permute-start(f32[40]{0:T(128)S(1)} %add_add_fusion.1.refs_7_), channel_id=1, source_target_pairs={{0,17},{1,16},{2,19},{3,18},{4,21},{5,20},{6,23},{7,22},{8,25},{9,... | collective-permute-start | bytes 488 | tf_op jit(solution)/shard_map/ppermute | solution.py:382
  21.9 12.4 %copy-start.23 = (s32[4]{0:T(128)S(1)}, s32[4]{0:T(128)}, u32[]{:S(2)}) copy-start(s32[4]{0:T(128)} %refs_0_.11) | copy-start | bytes 52
  53.5 23.0 %collective-permute-start.8 = (f32[8,192,768]{2,1,0:T(8,128)}, f32[8,192,768]{2,1,0:T(8,128)}, u32[]{:S(2)}, u32[]{:S(2)}) collective-permute-start(f32[8,192,768]{2,1,0:T(8,128)} %get-tuple-element.102), channel_id=1, source_target_pairs={{0,2},{2,0},{4,6},{6,4},{8,10},{10,8},{12,14},{14,12},{16,18},{18,... | collective-permute-start | bytes 14155784 | tf_op jit(solution)/shard_map/ppermute | solution.py:361
  74.7 21.0 %collective-permute-start.7 = (f32[8,48,3072]{2,1,0:T(8,128)}, f32[8,48,3072]{2,1,0:T(8,128)}, u32[]{:S(2)}, u32[]{:S(2)}) collective-permute-start(f32[8,48,3072]{2,1,0:T(8,128)} %get-tuple-element.98), channel_id=1, source_target_pairs={{0,2},{2,0},{4,6},{6,4},{8,10},{10,8},{12,14},{14,12},{16,18},{18,... | collective-permute-start | bytes 14155784 | tf_op jit(solution)/shard_map/ppermute | solution.py:361
  82.7 44.2 %collective-permute-start.11 = (f32[2,2,2,96,384]{4,3,2,1,0:T(8,128)}, f32[2,2,2,96,384]{4,3,2,1,0:T(8,128)S(1)}, u32[]{:S(2)}, u32[]{:S(2)}) collective-permute-start(f32[2,2,2,96,384]{4,3,2,1,0:T(8,128)} %get-tuple-element.103.refs_10_), channel_id=1, source_target_pairs={{0,4},{2,6},{4,0},{6,2},{8,12},{10,14},{12,8},{14,10},{16,20},{18,... | collective-permute-start | bytes 3538952 | tf_op jit(solution)/shard_map/ppermute | solution.py:361
  84.5 42.5 %collective-permute-start.12 = (f32[2,2,2,96,384]{4,3,2,1,0:T(8,128)}, f32[2,2,2,96,384]{4,3,2,1,0:T(8,128)}, u32[]{:S(2)}, u32[]{:S(2)}) collective-permute-start(f32[2,2,2,96,384]{4,3,2,1,0:T(8,128)} %get-tuple-element.105.refs_12_), channel_id=1, source_target_pairs={{0,1},{1,0},{2,3},{3,2},{4,5},{5,4},{6,7},{7,6},{8,9},{9,8},{10,11... | collective-permute-start | bytes 3538952 | tf_op jit(solution)/shard_map/ppermute | solution.py:361
  101.7 34.8 %collective-permute-start.10 = (f32[2,2,2,24,1536]{4,3,2,1,0:T(8,128)}, f32[2,2,2,24,1536]{4,3,2,1,0:T(8,128)}, u32[]{:S(2)}, u32[]{:S(2)}) collective-permute-start(f32[2,2,2,24,1536]{4,3,2,1,0:T(8,128)} %get-tuple-element.111.refs_13_), channel_id=1, source_target_pairs={{0,4},{2,6},{4,0},{6,2},{8,12},{10,14},{12,8},{14,10},{16,20},{18,... | collective-permute-start | bytes 3538952 | tf_op jit(solution)/shard_map/ppermute | solution.py:361
  102.2 34.3 %collective-permute-start.9 = (f32[2,2,2,24,1536]{4,3,2,1,0:T(8,128)}, f32[2,2,2,24,1536]{4,3,2,1,0:T(8,128)}, u32[]{:S(2)}, u32[]{:S(2)}) collective-permute-start(f32[2,2,2,24,1536]{4,3,2,1,0:T(8,128)} %get-tuple-element.109.refs_11_), channel_id=1, source_target_pairs={{0,8},{2,10},{4,12},{6,14},{8,0},{10,2},{12,4},{14,6},{16,24},{18,... | collective-permute-start | bytes 3538952 | tf_op jit(solution)/shard_map/ppermute | solution.py:361
  126.8 24.9 %collective-permute-start.17 = (f32[8,48,3072]{2,1,0:T(8,128)}, f32[8,48,3072]{2,1,0:T(8,128)}, u32[]{:S(2)}, u32[]{:S(2)}) collective-permute-start(f32[8,48,3072]{2,1,0:T(8,128)} %get-tuple-element.127), channel_id=1, source_target_pairs={{0,2},{2,0},{4,6},{6,4},{8,10},{10,8},{12,14},{14,12},{16,18},{18,... | collective-permute-start | bytes 14155784 | tf_op jit(solution)/shard_map/ppermute | solution.py:361
  126.9 1.0 copy-start
  132.2 27.4 %collective-permute-start.15 = (f32[2,2,96,384]{3,2,1,0:T(8,128)}, f32[2,2,96,384]{3,2,1,0:T(8,128)}, u32[]{:S(2)}, u32[]{:S(2)}) collective-permute-start(f32[2,2,96,384]{3,2,1,0:T(8,128)} %get-tuple-element.118.refs_5_), channel_id=1, source_target_pairs={{0,1},{1,0},{2,3},{3,2},{4,5},{5,4},{6,7},{7,6},{8,9},{9,8},{10,11... | collective-permute-start | bytes 1769480 | tf_op jit(solution)/shard_map/ppermute | solution.py:361
  132.8 28.8 %collective-permute-start.16 = (f32[2,2,96,384]{3,2,1,0:T(8,128)}, f32[2,2,96,384]{3,2,1,0:T(8,128)}, u32[]{:S(2)}, u32[]{:S(2)}) collective-permute-start(f32[2,2,96,384]{3,2,1,0:T(8,128)} %get-tuple-element.120.refs_7_), channel_id=1, source_target_pairs={{0,4},{2,6},{4,0},{6,2},{8,12},{10,14},{12,8},{14,10},{16,20},{18,... | collective-permute-start | bytes 1769480 | tf_op jit(solution)/shard_map/ppermute | solution.py:361
  140.0 25.4 %collective-permute-start.13 = (f32[2,2,24,1536]{3,2,1,0:T(8,128)}, f32[2,2,24,1536]{3,2,1,0:T(8,128)}, u32[]{:S(2)}, u32[]{:S(2)}) collective-permute-start(f32[2,2,24,1536]{3,2,1,0:T(8,128)} %get-tuple-element.123.refs_6_), channel_id=1, source_target_pairs={{0,4},{2,6},{4,0},{6,2},{8,12},{10,14},{12,8},{14,10},{16,20},{18,... | collective-permute-start | bytes 1769480 | tf_op jit(solution)/shard_map/ppermute | solution.py:361
  157.5 36.5 %collective-permute-start.23 = (f32[2,2,2,24,1280]{4,3,2,1,0:T(8,128)}, f32[2,2,2,24,1280]{4,3,2,1,0:T(8,128)S(1)}, u32[]{:S(2)}, u32[]{:S(2)}) collective-permute-start(f32[2,2,2,24,1280]{4,3,2,1,0:T(8,128)} %get-tuple-element.129.refs_5_), channel_id=1, source_target_pairs={{0,4},{2,6},{4,0},{6,2},{8,12},{10,14},{12,8},{14,10},{16,20},{18,... | collective-permute-start | bytes 2949128 | tf_op jit(solution)/shard_map/ppermute | solution.py:361
  157.6 36.5 %collective-permute-start.24 = (f32[2,2,2,24,1280]{4,3,2,1,0:T(8,128)}, f32[2,2,2,24,1280]{4,3,2,1,0:T(8,128)S(1)}, u32[]{:S(2)}, u32[]{:S(2)}) collective-permute-start(f32[2,2,2,24,1280]{4,3,2,1,0:T(8,128)} %get-tuple-element.131.refs_7_), channel_id=1, source_target_pairs={{0,1},{1,0},{2,3},{3,2},{4,5},{5,4},{6,7},{7,6},{8,9},{9,8},{10,11... | collective-permute-start | bytes 2949128 | tf_op jit(solution)/shard_map/ppermute | solution.py:361
  159.6 16.6 %collective-permute-start.14 = (f32[2,2,24,1536]{3,2,1,0:T(8,128)}, f32[2,2,24,1536]{3,2,1,0:T(8,128)}, u32[]{:S(2)}, u32[]{:S(2)}) collective-permute-start(f32[2,2,24,1536]{3,2,1,0:T(8,128)} %get-tuple-element.125.refs_8_), channel_id=1, source_target_pairs={{0,8},{2,10},{4,12},{6,14},{8,0},{10,2},{12,4},{14,6},{16,24},{18,... | collective-permute-start | bytes 1769480 | tf_op jit(solution)/shard_map/ppermute | solution.py:361
  165.3 23.7 %collective-permute-start.26 = (f32[2,96,768]{2,1,0:T(8,128)}, f32[2,96,768]{2,1,0:T(8,128)}, u32[]{:S(2)}, u32[]{:S(2)}) collective-permute-start(f32[2,96,768]{2,1,0:T(8,128)} %get-tuple-element.135.refs_5_), channel_id=1, source_target_pairs={{0,8},{2,10},{4,12},{6,14},{8,0},{10,2},{12,4},{14,6},{16,24},{18,... | collective-permute-start | bytes 1769480 | tf_op jit(solution)/shard_map/ppermute | solution.py:361
  165.4 28.7 %collective-permute-start.25 = (f32[2,2,2,24,512]{4,3,2,1,0:T(8,128)}, f32[2,2,2,24,512]{4,3,2,1,0:T(8,128)}, u32[]{:S(2)}, u32[]{:S(2)}) collective-permute-start(f32[2,2,2,24,512]{4,3,2,1,0:T(8,128)} %get-tuple-element.133.refs_9_), channel_id=1, source_target_pairs={{0,8},{2,10},{4,12},{6,14},{8,0},{10,2},{12,4},{14,6},{16,24},{18,... | collective-permute-start | bytes 1179656 | tf_op jit(solution)/shard_map/ppermute | solution.py:361
  178.6 40.5 %collective-permute-start.30 = (f32[2,24,3072]{2,1,0:T(8,128)}, f32[2,24,3072]{2,1,0:T(8,128)}, u32[]{:S(2)}, u32[]{:S(2)}) collective-permute-start(f32[2,24,3072]{2,1,0:T(8,128)} %get-tuple-element.137.refs_4_), channel_id=1, source_target_pairs={{0,1},{1,0},{2,3},{3,2},{4,5},{5,4},{6,7},{7,6},{8,9},{9,8},{10,11... | collective-permute-start | bytes 1769480 | tf_op jit(solution)/shard_map/ppermute | solution.py:361
  194.0 1.0 copy-start.6
  194.0 1.3 copy-start.7
  195.3 5.6 %copy-start.20 = (f32[4,1,768]{2,1,0:T(1,128)S(1)}, f32[4,1,768]{2,1,0:T(1,128)}, u32[]{:S(2)}) copy-start(f32[4,1,768]{2,1,0:T(1,128)} %get-tuple-element.142) | copy-start | bytes 36868
  195.3 5.6 %copy-start.18 = (f32[8,768]{1,0:T(8,128)S(1)}, f32[8,768]{1,0:T(8,128)}, u32[]{:S(2)}) copy-start(f32[8,768]{1,0:T(8,128)} %get-tuple-element.128.refs_3_) | copy-start | bytes 73732
  195.3 5.6 %copy-start.19 = (f32[8,768]{1,0:T(8,128)S(1)}, f32[8,768]{1,0:T(8,128)}, u32[]{:S(2)}) copy-start(f32[8,768]{1,0:T(8,128)} %get-tuple-element.140) | copy-start | bytes 73732
  198.8 22.4 %collective-permute-start.27 = (f32[2,2,24,1280]{3,2,1,0:T(8,128)}, f32[2,2,24,1280]{3,2,1,0:T(8,128)S(1)}, u32[]{:S(2)}, u32[]{:S(2)}) collective-permute-start(f32[2,2,24,1280]{3,2,1,0:T(8,128)} %get-tuple-element.147.refs_3_), channel_id=1, source_target_pairs={{0,1},{1,0},{2,3},{3,2},{4,5},{5,4},{6,7},{7,6},{8,9},{9,8},{10,11... | collective-permute-start | bytes 1474568 | tf_op jit(solution)/shard_map/ppermute | solution.py:361
  199.2 22.0 %collective-permute-start.28 = (f32[2,2,24,1280]{3,2,1,0:T(8,128)}, f32[2,2,24,1280]{3,2,1,0:T(8,128)S(1)}, u32[]{:S(2)}, u32[]{:S(2)}) collective-permute-start(f32[2,2,24,1280]{3,2,1,0:T(8,128)} %get-tuple-element.149.refs_5_), channel_id=1, source_target_pairs={{0,8},{2,10},{4,12},{6,14},{8,0},{10,2},{12,4},{14,6},{16,24},{18,... | collective-permute-start | bytes 1474568 | tf_op jit(solution)/shard_map/ppermute | solution.py:361
  202.7 10.5 %collective-permute-start.18 = (f32[68,768]{1,0:T(8,128)S(1)}, f32[68,768]{1,0:T(8,128)S(1)}, u32[]{:S(2)}, u32[]{:S(2)}) collective-permute-start(f32[68,768]{1,0:T(8,128)S(1)} %concatenate.3), channel_id=1, source_target_pairs={{0,16},{2,18},{4,20},{6,22},{8,24},{10,26},{12,28},{14,30},{16,0},... | collective-permute-start | bytes 626696 | tf_op jit(solution)/shard_map/ppermute | solution.py:361
  205.4 15.8 %collective-permute-start.29 = (f32[2,2,24,512]{3,2,1,0:T(8,128)}, f32[2,2,24,512]{3,2,1,0:T(8,128)S(1)}, u32[]{:S(2)}, u32[]{:S(2)}) collective-permute-start(f32[2,2,24,512]{3,2,1,0:T(8,128)} %get-tuple-element.151.refs_7_), channel_id=1, source_target_pairs={{0,4},{2,6},{4,0},{6,2},{8,12},{10,14},{12,8},{14,10},{16,20},{18,... | collective-permute-start | bytes 589832 | tf_op jit(solution)/shard_map/ppermute | solution.py:361
  213.3 13.2 %collective-permute-start.19 = (f32[68,768]{1,0:T(8,128)S(1)}, f32[68,768]{1,0:T(8,128)S(1)}, u32[]{:S(2)}, u32[]{:S(2)}) collective-permute-start(f32[68,768]{1,0:T(8,128)S(1)} %add.58), channel_id=1, source_target_pairs={{0,8},{2,10},{4,12},{6,14},{8,0},{10,2},{12,4},{14,6},{16,24},{18,... | collective-permute-start | bytes 626696 | tf_op jit(solution)/shard_map/ppermute | solution.py:361
  221.2 0.7 copy-start.16
  221.2 0.8 copy-start.8
  221.2 1.0 copy-start.9
  222.2 8.0 %copy-start.10 = (f32[96,768]{1,0:T(8,128)S(1)}, f32[96,768]{1,0:T(8,128)}, u32[]{:S(2)}) copy-start(f32[96,768]{1,0:T(8,128)} %get-tuple-element.144.refs_7_) | copy-start | bytes 884740
  224.9 8.6 %collective-permute-start.31 = (f32[2,24,1280]{2,1,0:T(8,128)}, f32[2,24,1280]{2,1,0:T(8,128)S(1)}, u32[]{:S(2)}, u32[]{:S(2)}) collective-permute-start(f32[2,24,1280]{2,1,0:T(8,128)} %get-tuple-element.155), channel_id=1, source_target_pairs={{0,8},{2,10},{4,12},{6,14},{8,0},{10,2},{12,4},{14,6},{16,24},{18,... | collective-permute-start | bytes 737288 | tf_op jit(solution)/shard_map/ppermute | solution.py:361
  225.0 28.2 %copy-start.1 = (f32[96,768]{1,0:T(8,128)S(1)}, f32[96,768]{1,0:T(8,128)}, u32[]{:S(2)}) copy-start(f32[96,768]{1,0:T(8,128)} %get-tuple-element.145.refs_8_) | copy-start | bytes 884740
  225.0 8.5 %collective-permute-start.32 = (f32[2,24,1280]{2,1,0:T(8,128)}, f32[2,24,1280]{2,1,0:T(8,128)S(1)}, u32[]{:S(2)}, u32[]{:S(2)}) collective-permute-start(f32[2,24,1280]{2,1,0:T(8,128)} %get-tuple-element.157), channel_id=1, source_target_pairs={{0,4},{2,6},{4,0},{6,2},{8,12},{10,14},{12,8},{14,10},{16,20},{18,... | collective-permute-start | bytes 737288 | tf_op jit(solution)/shard_map/ppermute | solution.py:361
  226.6 12.4 %collective-permute-start.20 = (f32[68,768]{1,0:T(8,128)S(1)}, f32[68,768]{1,0:T(8,128)S(1)}, u32[]{:S(2)}, u32[]{:S(2)}) collective-permute-start(f32[68,768]{1,0:T(8,128)S(1)} %add.59), channel_id=1, source_target_pairs={{0,4},{2,6},{4,0},{6,2},{8,12},{10,14},{12,8},{14,10},{16,20},{18,... | collective-permute-start | bytes 626696 | tf_op jit(solution)/shard_map/ppermute | solution.py:361
  228.1 4.9 %collective-permute-start.33 = (f32[2,24,512]{2,1,0:T(8,128)}, f32[2,24,512]{2,1,0:T(8,128)S(1)}, u32[]{:S(2)}, u32[]{:S(2)}) collective-permute-start(f32[2,24,512]{2,1,0:T(8,128)} %get-tuple-element.159), channel_id=1, source_target_pairs={{0,1},{1,0},{2,3},{3,2},{4,5},{5,4},{6,7},{7,6},{8,9},{9,8},{10,11... | collective-permute-start | bytes 294920 | tf_op jit(solution)/shard_map/ppermute | solution.py:361
  230.2 23.0 %collective-permute-start.38 = (f32[96,768]{1,0:T(8,128)S(1)}, f32[96,768]{1,0:T(8,128)S(1)}, u32[]{:S(2)}, u32[]{:S(2)}) collective-permute-start(f32[96,768]{1,0:T(8,128)S(1)} %copy-done.10), channel_id=1, source_target_pairs={{0,16},{2,18},{4,20},{6,22},{8,24},{10,26},{12,28},{14,30},{16,0},... | collective-permute-start | bytes 884744 | tf_op jit(solution)/shard_map/ppermute | solution.py:361
  233.0 0.6 copy-start.17
  233.0 25.9 %collective-permute-start.36 = (f32[24,3072]{1,0:T(8,128)}, f32[24,3072]{1,0:T(8,128)S(1)}, u32[]{:S(2)}, u32[]{:S(2)}) collective-permute-start(f32[24,3072]{1,0:T(8,128)} %get-tuple-element.152.refs_7_), channel_id=1, source_target_pairs={{0,16},{2,18},{4,20},{6,22},{8,24},{10,26},{12,28},{14,30},{16,0},... | collective-permute-start | bytes 884744 | tf_op jit(solution)/shard_map/ppermute | solution.py:361
  233.5 0.7 copy-start.14
  233.5 0.8 copy-start.15
  234.3 24.6 %copy-start.2 = (f32[24,3072]{1,0:T(8,128)S(1)}, f32[24,3072]{1,0:T(8,128)}, u32[]{:S(2)}) copy-start(f32[24,3072]{1,0:T(8,128)} %get-tuple-element.153.refs_8_) | copy-start | bytes 884740
  236.5 25.5 %copy-start.11 = (f32[24,3072]{1,0:T(8,128)S(1)}, f32[24,3072]{1,0:T(8,128)}, u32[]{:S(2)}) copy-start(f32[24,3072]{1,0:T(8,128)} %get-tuple-element.160) | copy-start | bytes 884740
  236.5 25.5 %collective-permute-start.34 = (f32[24,3072]{1,0:T(8,128)}, f32[24,3072]{1,0:T(8,128)S(1)}, u32[]{:S(2)}, u32[]{:S(2)}) collective-permute-start(f32[24,3072]{1,0:T(8,128)} %get-tuple-element.161), channel_id=1, source_target_pairs={{0,16},{2,18},{4,20},{6,22},{8,24},{10,26},{12,28},{14,30},{16,0},... | collective-permute-start | bytes 884744 | tf_op jit(solution)/shard_map/ppermute | solution.py:361
  239.0 1.5 collective-permute-start.21
  240.6 22.1 %collective-permute-start.22 = (f32[68,768]{1,0:T(8,128)S(1)}, f32[68,768]{1,0:T(8,128)S(1)}, u32[]{:S(2)}, u32[]{:S(2)}) collective-permute-start(f32[68,768]{1,0:T(8,128)S(1)} %add.61), channel_id=1, source_target_pairs={{0,1},{1,0},{2,3},{3,2},{4,5},{5,4},{6,7},{7,6},{8,9},{9,8},{10,11... | collective-permute-start | bytes 626696 | tf_op jit(solution)/shard_map/ppermute | solution.py:361
  253.2 11.4 %copy-start.4 = (f32[96,768]{1,0:T(8,128)}, f32[96,768]{1,0:T(8,128)S(1)}, u32[]{:S(2)}) copy-start(f32[96,768]{1,0:T(8,128)S(1)} %add.65.refs_1_) | copy-start | bytes 884740
  253.3 11.4 %collective-permute-start.39 = (f32[96,768]{1,0:T(8,128)S(1)}, f32[96,768]{1,0:T(8,128)S(1)}, u32[]{:S(2)}, u32[]{:S(2)}) collective-permute-start(f32[96,768]{1,0:T(8,128)S(1)} %add.65.refs_1_), channel_id=1, source_target_pairs={{0,1},{1,0},{2,3},{3,2},{4,5},{5,4},{6,7},{7,6},{8,9},{9,8},{10,11... | collective-permute-start | bytes 884744 | tf_op jit(solution)/shard_map/ppermute | solution.py:361
  258.9 8.6 %copy-start.5 = (f32[24,3072]{1,0:T(8,128)}, f32[24,3072]{1,0:T(8,128)S(1)}, u32[]{:S(2)}) copy-start(f32[24,3072]{1,0:T(8,128)S(1)} %add.64.refs_1_) | copy-start | bytes 884740
  258.9 8.6 %collective-permute-start.37 = (f32[24,3072]{1,0:T(8,128)S(1)}, f32[24,3072]{1,0:T(8,128)}, u32[]{:S(2)}, u32[]{:S(2)}) collective-permute-start(f32[24,3072]{1,0:T(8,128)S(1)} %add.64.refs_1_), channel_id=1, source_target_pairs={{0,1},{1,0},{2,3},{3,2},{4,5},{5,4},{6,7},{7,6},{8,9},{9,8},{10,11... | collective-permute-start | bytes 884744 | tf_op jit(solution)/shard_map/ppermute | solution.py:361
  262.1 7.3 %copy-start.3 = (f32[24,3072]{1,0:T(8,128)}, f32[24,3072]{1,0:T(8,128)S(1)}, u32[]{:S(2)}) copy-start(f32[24,3072]{1,0:T(8,128)S(1)} %add.63.refs_1_) | copy-start | bytes 884740
  262.1 8.5 %collective-permute-start.35 = (f32[24,3072]{1,0:T(8,128)S(1)}, f32[24,3072]{1,0:T(8,128)S(1)}, u32[]{:S(2)}, u32[]{:S(2)}) collective-permute-start(f32[24,3072]{1,0:T(8,128)S(1)} %add.63.refs_1_), channel_id=1, source_target_pairs={{0,1},{1,0},{2,3},{3,2},{4,5},{5,4},{6,7},{7,6},{8,9},{9,8},{10,11... | collective-permute-start | bytes 884744 | tf_op jit(solution)/shard_map/ppermute | solution.py:361
  264.6 0.7 copy-start.13
  270.6 0.7 copy-start.12

commit v3 on v2

--- a/solution.py
+++ b/solution.py
@@ -6,10 +6,20 @@
 from jax.sharding import PartitionSpec as P
 
 HEADS = 12
-FORWARD_GROUP, BACK_GROUP = 2, 4
-LAST_SHARES = (1280, 1280, 512)
-NB = 100
-VMEM_BYTES = 62 * 1024 * 1024
+FORWARD_GROUP, BACK_GROUP = 2, 2
+LEADS_AT = 16
+SMALL_COLUMNS = 256
+LAST_SHARES = (1024, 1024, 1024)
+SEQUENCE = (
+    "DO", "M", "UO", "A0", "D2", "A1", "U2", "D3", "QO", "U3", "NB", "D4", "BO", "U4", "Q2",
+    "DA", "Q3", "DP", "UA", "Q4", "SX", "SZ", "QA", "UP", "SO", "QP",
+)
+PLAIN = ("M", "A0", "A1", "NB", "BO")
+SMALL_NAMES = ("gain1", "bias1", "query", "value", "out", "gain2", "bias2", "down", "up", "table")
+OUTPUTS = ("block_out", "grad_patches", "gain1", "bias1", "table", "sum_qkv", "query", "value")
+OUTPUTS += ("sum_out", "out", "gain2", "bias2", "sum_up", "up", "sum_down", "down")
+COSTS = {"D3": 100, "DO": 30, "A1": 2}
+VMEM_BYTES = 63 * 1024 * 1024
 
 
 norm_epsilon = 1e-05
@@ -167,9 +177,10 @@
             grad = (cotangent[window].astype(jnp.float32) * weight).astype(jnp.bfloat16)
             grad_down[window * rows : (window + 1) * rows, :] = grad
 
+    bias = bias_up[pl.ds(pl.multiple_of(step * width, 128), width)]
     for window in range(windows):
         at = slice(window * rows, (window + 1) * rows)
-        pre = dot_nn(normed2[at, :], w_up[...]) + bias_up[pl.ds(step, 1), :]
+        pre = dot_nn(normed2[at, :], w_up[...]) + bias.reshape(1, -1)
         out, steep = gelu_pair(pre)
         out = out.astype(jnp.bfloat16)
         activated[at, :] = out
@@ -238,6 +249,44 @@
     delta[0] = dot_nt(head_rows[...], high) + dot_nt(head_rows[...], low)
 
 
+def attend_back_heads(first, lengths, refs, log_total, delta, out, columns):
+    queries, keys, values, grad_attended = refs
+    rows, width = queries.shape
+    row = lax.broadcasted_iota(jnp.int32, (rows, 1), 0)
+    blocked = jnp.where(row < lengths[pl.program_id(0)], 0.0, masked_score)
+    span = BACK_GROUP * 64
+    place = lax.broadcasted_iota(jnp.int32, (rows, span), 1) // 64
+
+    def start(at):
+        query = each_alone(queries[:, at : at + span], place)
+        grad_group = each_alone(grad_attended[:, at : at + span], place)
+        scores = dot_nt(keys[:, at : at + span], query) + blocked
+        return query, grad_group, scores, dot_nt(values[:, at : at + span], grad_group)
+
+    ahead = start(0)
+    for at in range(0, width, span):
+        query, grad_group, scores, grad_probs = ahead
+        if at + span < width:
+            ahead = start(at + span)
+        heads = range(first + at // 64, first + at // 64 + BACK_GROUP)
+        totals = jnp.concatenate([log_total[0, h : h + 1, :] for h in heads], axis=1)
+        shift = jnp.concatenate([delta[0, h : h + 1, :] for h in heads], axis=1)
+        probs = jnp.exp(scores - totals)
+        grad_scores = (probs * (grad_probs - shift)).astype(jnp.bfloat16)
+        grad_query = own_columns(dot_tn(grad_scores, keys[:, at : at + span]), place) * 0.125
+        grad_key = dot_nn(grad_scores, query)
+        grad_value = dot_nn(probs.astype(jnp.bfloat16), grad_group)
+        for index, grad in enumerate((grad_query, grad_key, grad_value)):
+            to = columns[index] + at
+            out[:, to : to + span] = grad.astype(jnp.bfloat16)
+
+
+def attend_back_first_kernel(lengths, queries, keys, values, grad_attended, log_total, delta, out):
+    half = queries.shape[1]
+    refs = (queries, keys, values, grad_attended)
+    attend_back_heads(0, lengths, refs, log_total, delta, out, (0, half, 2 * half))
+
+
 def attend_back_kernel(
     lengths,
     here,
@@ -250,6 +299,7 @@
     delta,
     attended,
     branch,
+    first,
     grad_projected,
     sums,
     keep,
@@ -257,35 +307,20 @@
     grad_w,
 ):
     window = pl.program_id(0)
-    rows, width = queries.shape
+    half = queries.shape[1]
+    width = 2 * half
 
     @pl.when(window == 0)
     def _():
         grad_w[...] = jnp.zeros_like(grad_w)
         sums[...] = jnp.zeros_like(sums)
 
-    row = lax.broadcasted_iota(jnp.int32, (rows, 1), 0)
-    blocked = jnp.where(row < lengths[window], 0.0, masked_score)
-    span = BACK_GROUP * 64
-    place = lax.broadcasted_iota(jnp.int32, (rows, span), 1) // 64
-    for at in range(0, width, span):
-        query = each_alone(queries[:, at : at + span], place)
-        key = keys[:, at : at + span]
-        value = values[:, at : at + span]
-        grad_group = each_alone(grad_attended[:, at : at + span], place)
-        heads = range(at // 64, at // 64 + BACK_GROUP)
-        totals = jnp.concatenate([log_total[0, h : h + 1, :] for h in heads], axis=1)
-        shift = jnp.concatenate([delta[0, h : h + 1, :] for h in heads], axis=1)
-        scores = dot_nt(key, query) + blocked
-        probs = jnp.exp(scores - totals)
-        grad_probs = dot_nt(value, grad_group)
-        grad_scores = (probs * (grad_probs - shift)).astype(jnp.bfloat16)
-        grad_query = own_columns(dot_tn(grad_scores, key), place) * 0.125
-        grad_key = dot_nn(grad_scores, query)
-        grad_value = dot_nn(probs.astype(jnp.bfloat16), grad_group)
-        for index, grad in enumerate((grad_query, grad_key, grad_value)):
-            to = index * width + at
-            grad_projected[:, to : to + span] = grad.astype(jnp.bfloat16)
+    refs = (queries, keys, values, grad_attended)
+    columns = (half, width + half, 2 * width + half)
+    attend_back_heads(HEADS // 2, lengths, refs, log_total, delta, grad_projected, columns)
+    for third in range(3):
+        part = first[:, third * half : (third + 1) * half]
+        grad_projected[:, third * width : third * width + half] = part
     grad_w[:, : 3 * width] += dot_tn(normed[...], grad_projected[...])
     grad_w[:, 3 * width :] += dot_tn(attended[...], branch[...])
     sums[0:1, :] += column_sum(grad_projected[:, :width].astype(jnp.float32))
@@ -297,23 +332,44 @@
 
 
 def norm_back_kernel(
-    leads, patches, grad_residual, grad_projected, w_qkv, gain, grad_patches, sums, grad_leads
+    leads,
+    patches,
+    grad_residual,
+    grad_projected,
+    w_qkv,
+    gain,
+    middle_sums,
+    bias_sums,
+    bias_rows,
+    grad_patches,
+    small,
 ):
     window = pl.program_id(0)
 
+    def put(row, value, add=False):
+        for piece in range(value.shape[1] // SMALL_COLUMNS):
+            at = pl.ds(row * (value.shape[1] // SMALL_COLUMNS) + piece, 1)
+            part = value[:, piece * SMALL_COLUMNS : (piece + 1) * SMALL_COLUMNS]
+            small[at, :] = small[at, :] + part if add else part
+
     @pl.when(window == 0)
     def _():
-        sums[...] = jnp.zeros_like(sums)
-        grad_leads[...] = jnp.zeros_like(grad_leads)
+        small[...] = jnp.zeros_like(small)
+        for row in range(4):
+            put(row, middle_sums[row : row + 1, :])
+        for row in range(2):
+            put(4 + row, bias_sums[row : row + 1, :])
+        for row in range(bias_rows.shape[0]):
+            put(8 + row, bias_rows[row])
 
     grad_norm = dot_nt(grad_projected[...], w_qkv[...])
     unit, inverse = normalise(patches[0].astype(jnp.float32))
     back = normalise_back(grad_norm * line(gain), unit, inverse)
     grad_patches[0] = (grad_residual[...] + back).astype(jnp.bfloat16)
     total = column_sum(grad_norm)
-    sums[0:1, :] += column_sum(grad_norm * unit)
-    sums[1:2, :] += total
-    grad_leads[pl.ds(leads[window], 1), :] += total
+    put(6, column_sum(grad_norm * unit), add=True)
+    put(7, total, add=True)
+    put(LEADS_AT + leads[window], total, add=True)
 
 
 def block_out_kernel(activated, w_down, bias_down, residual, block_out):
@@ -325,8 +381,8 @@
 LINKS = (("dp", 3), ("dp", 2), ("dp", 1), ("outer", 0))
 
 
-def split_kernel(pairs, parts, axes, merge, gridded, bits, *refs):
-    outs = refs[2 * len(pairs) :]
+def split_kernel(pairs, parts, axes, merge, gridded, riders, bits, *refs):
+    outs = refs[2 * len(pairs) + (riders == "join") :]
     start = 0
     for index, (pieces, axis) in enumerate(zip(parts, axes)):
         send, keep = outs[:2] if merge else outs[2 * index : 2 * index + 2]
@@ -346,14 +402,59 @@
                 to = (Ellipsis, slice(start, start + width))
                 out[(0,) + to if gridded else to] = value
             start += width
-
-
-def place_kernel(moves, bits, own, other, *outs):
+    if riders == "join":
+        rider = refs[2 * len(pairs)]
+        rows, wide = outs[0].shape[0], rider.shape[1]
+        for out in outs[:2]:
+            for side in range(2):
+                to = slice(start + side * wide, start + (side + 1) * wide)
+                out[:, to] = rider[side * rows : (side + 1) * rows, :]
+
+
+def add_kernel(held, come, out):
+    out[...] = held[...] + come[...]
+
+
+SMALL_ROWS = (6, 7, 4, 5, 2, 0, 1, 3)
+
+
+def small_out_kernel(held, come, *outs):
+    total = held[...] + come[...]
+    columns = total.shape[1]
+    vectors, bias_up, table = outs[:8], outs[8], outs[9]
+    pieces = table.shape[1] // columns
+
+    def copy(row, out, start):
+        for piece in range(pieces):
+            value = total[row * pieces + piece : row * pieces + piece + 1, :]
+            out[pl.ds(start + piece * columns, columns)] = value.reshape(columns)
+
+    for row, out in zip(SMALL_ROWS, vectors):
+        copy(row, out, 0)
+    for row in range(bias_up.shape[0] // table.shape[1]):
+        copy(8 + row, bias_up, row * table.shape[1])
+    for row in range(table.shape[0]):
+        for piece in range(pieces):
+            at = (LEADS_AT + row) * pieces + piece
+            table[row : row + 1, piece * columns : (piece + 1) * columns] = total[at : at + 1, :]
+
+
+def place_kernel(moves, rider, bits, own, other, *outs):
     rows = own.shape[0]
     mine = bits[Y]
     for out, to, start, width in moves:
         for value, side in ((own, mine), (other, 1 - mine)):
             outs[out][pl.ds(side * rows, rows), to : to + width] = value[:, start : start + width]
+    if rider is not None:
+        wide = outs[-1].shape[1]
+        for side in range(2):
+            at = slice(rider + side * wide, rider + (side + 1) * wide)
+            outs[-1][side * rows : (side + 1) * rows, :] = own[:, at] + other[:, at]
+
+
+DOWN_ORDERS, DOWN_SHARES = [(X, Y, Z0, Z1), (Y, X, Z0, Z1)], (384, 384)
+UP_ORDERS, UP_SHARES = [(Z0, X, Y, Z1), (X, Z0, Y, Z1)], (1920, 1152)
+LAST_ORDERS = [(X, Y, Z0, Z1), (Y, Z0, X, Z1), (Z0, X, Y, Z1)]
 
 
 def swap(values, axis, bit):
@@ -367,12 +468,6 @@
 
 def dp_bits():
     return lax.axis_size("dp").bit_length() - 1
-
-
-def sum_small(values):
-    for bit in reversed(range(dp_bits())):
-        values = values + swap(values, "dp", bit)
-    return values + swap(values, "outer", 0)
 
 
 def exchange(values, dp_mask, outer_mask):
@@ -462,7 +557,7 @@
     f32, bf16 = jnp.float32, jnp.bfloat16
     parts = lax.axis_size("dp")
     share = width // parts
-    fast = parts == 16 and share % 16 == 0
+    fast = parts == 16 and share % 16 == 0 and slots == 4
 
     smem = pl.BlockSpec(memory_space=pltpu.SMEM)
     params = pltpu.CompilerParams(vmem_limit_bytes=VMEM_BYTES)
@@ -473,7 +568,9 @@
     def by_window(columns, at=0):
         return pl.BlockSpec((rows, columns), lambda i: (i, at))
 
-    def call(kernel, grid, inputs, outs, scratch=(), after=(), carry=(), micros=0):
+    current = [""]
+
+    def call(kernel, grid, inputs, outs, scratch=(), after=(), carry=()):
         count, extra, carried = len(inputs), len(after) + len(carry), len(carry)
         made = count + extra + len(outs)
 
@@ -494,7 +591,7 @@
             scratch_shapes=scratch,
             compiler_params=params,
             cost_estimate=pl.CostEstimate(
-                flops=int(micros * 1.15e9), bytes_accessed=0, transcendentals=0
+                flops=int(COSTS.get(current[0], 0) * 1.15e9), bytes_accessed=0, transcendentals=0
             ),
         )(*[value for _, value in inputs], *after, *carry)
 
@@ -585,7 +682,7 @@
             (whole(*cotangent.shape), cotangent),
             (whole(total, width), normed2),
             (up_spec, w_up),
-            flat(bias_up.reshape(steps, width)),
+            flat(bias_up),
         ],
         [
             (by_lanes, (total, hidden), bf16),
@@ -620,33 +717,40 @@
     def core_swap(send):
         return swap(send, "dp", 0) if fast else send
 
-    def split_round(pairs, dims, parts, axes, after=(), carry=()):
+    def split_round(pairs, dims, parts, axes, done, rider=None):
+        riders = "join" if rider is not None else None
         merge = len(set(axes)) == 1 and len({tuple(dims[p[0][0]]) for p in parts}) == 1
-        gridded = all(d[0] == Z1 and len(d) > 1 for d in dims) and Z1 not in axes
+        gridded = all(d[0] == Z1 and len(d) > 1 for d in dims) and Z1 not in axes and not riders
         rows_here = pairs[0][0].shape[-2]
         blocks = 2 if gridded and rows_here % 48 == 0 else 1
         widths = [sum(width for _, _, width in part) for part in parts]
         left = [[d for d in dims[part[0][0]] if d != axis] for part, axis in zip(parts, axes)]
         if merge:
             widths, left = [sum(widths)], left[:1]
+            if riders == "join":
+                widths = [widths[0] + 2 * rider.shape[-1]]
         shapes = [(2,) * len(d) + (rows_here, width) for d, width in zip(left, widths)]
 
         def spec(shape):
             if not gridded:
                 return whole(*shape)
             block = (1,) + shape[1:-2] + (rows_here // blocks, shape[-1])
-            return pl.BlockSpec(block, lambda i, j: (i,) + (0,) * (len(shape) - 3) + (j, 0))
-
-        values = call(
-            lambda *refs: split_kernel(dims, parts, axes, merge, gridded, *refs),
-            (2, blocks) if gridded else (),
-            [(smem, bits)] + [(spec(v.shape), v) for pair in pairs for v in pair],
-            [(spec(shape), shape, f32) for shape in shapes for _ in range(2)],
-            after=after,
-            carry=carry,
-        )
-        states = [(values[2 * i], values[2 * i + 1]) for i in range(len(shapes))]
-        return states, left, values[2 * len(shapes) :]
+            middle = (0,) * (len(shape) - 3)
+            return pl.BlockSpec(block, lambda i: (i // blocks, *middle, i % blocks, 0))
+
+        inputs = [(smem, bits)] + [(spec(v.shape), v) for pair in pairs for v in pair]
+        if riders == "join":
+            inputs.append((spec(rider.shape), rider))
+        outs = [(spec(shape), shape, f32) for shape in shapes for _ in range(2)]
+
+        def kernel(*refs):
+            split_kernel(dims, parts, axes, merge, gridded, riders, *refs)
+
+        def finish(values):
+            done([(values[2 * i], values[2 * i + 1]) for i in range(len(shapes))], left)
+            return list(values)
+
+        return kernel, (2 * blocks,) if gridded else (), inputs, outs, [], finish
 
     class Chunk:
         def __init__(self, sources, orders, shares):
@@ -658,16 +762,16 @@
                     pieces.append((i, start, width))
                     start += width
 
-        def open(self, after=()):
+        def open(self):
             shaped = lambda v: v.reshape((2, 2, 2, 2, -1, v.shape[-1]))
             pairs = [(shaped(keep), shaped(come)) for keep, come in self.sources]
             axes = [order[0] for order in self.orders]
             dims = [[Z1, Z0, X, Y]] * len(pairs)
-            self.put(split_round(pairs, dims, self.columns, axes, after), axes)
-
-        def put(self, result, axes):
-            self.states, self.dims, self.carried = result
-            self.axes = axes[: len(self.states)]
+            return split_round(pairs, dims, self.columns, axes, self.put)
+
+        def put(self, states, dims):
+            self.states, self.dims = states, dims
+            self.axes = [order[self.step_count] for order in self.orders][: len(states)]
             self.step_count += 1
 
         def pairs(self):
@@ -676,15 +780,25 @@
                 for (send, keep), axis in zip(self.states, self.axes)
             ]
 
-        def step(self, after=(), carry=()):
+        def step(self, rider=None):
             pairs = self.pairs()
             axes = [order[self.step_count] for order in self.orders][: len(pairs)]
             parts = [[(i, 0, keep.shape[-1])] for i, (keep, _) in enumerate(pairs)]
-            self.put(split_round(pairs, self.dims, parts, axes, after, carry), axes)
-
-        def finish(self, outputs):
+            return split_round(pairs, self.dims, parts, axes, self.put, rider)
+
+        def add(self):
             ((keep, come),) = self.pairs()
-            own = keep + come
+            spec = whole(*keep.shape)
+
+            def finish(values):
+                (self.own,) = values
+                return values
+
+            inputs = [(spec, keep), (spec, come)]
+            return add_kernel, (), inputs, [(spec, keep.shape, f32)], [], finish
+
+        def place(self, outputs, finish, rider=False):
+            own = self.own
             other = swap(own, *LINKS[Y])
             moves, start = [], 0
             for pieces in self.columns:
@@ -695,167 +809,221 @@
                             moves.append((out, begin - low, start + begin - first, end - begin))
                     start += wide
             shapes = [(2 * own.shape[0], size) for _, _, size in outputs]
-            return call(
-                lambda *refs: place_kernel(moves, *refs),
-                (),
-                [(smem, bits), (whole(*own.shape), own), (whole(*other.shape), other)],
-                [(whole(*shape), shape, f32) for shape in shapes],
-            )
-
-        def tokens(self):
-            return [value for state in self.states for value in state]
+            if rider:
+                shapes.append((2 * own.shape[0], (own.shape[1] - start) // 2))
+
+            def kernel(*refs):
+                place_kernel(moves, start if rider else None, *refs)
+
+            inputs = [(smem, bits), (whole(*own.shape), own), (whole(*other.shape), other)]
+            outs = [(whole(*shape), shape, f32) for shape in shapes]
+            return kernel, (), inputs, outs, [], finish
 
     come_down = core_swap(send_down)
     come_up = core_swap(send_up)
-    two_orders = [(X, Y, Z0, Z1), (Y, X, Z0, Z1)]
-    orders = [(X, Y, Z0, Z1), (Y, Z0, X, Z1), (Z0, X, Y, Z1)]
-    tokens = []
-    if fast:
-        down = Chunk([(keep_down, come_down)], two_orders, [(width // 2,) * 2])
-        down.open([grad_normed2])
-        tokens = down.tokens()
     head_rows = (
         jnp.arange(16, dtype=jnp.int32)[:, None]
         == jnp.arange(width, dtype=jnp.int32)[None, :] // (width // HEADS)
     ).astype(bf16)
-    grad_residual, grad_attended, delta, sums, branch_low = call(
-        middle_back_kernel,
-        (slots,),
-        [
-            (smem, lengths),
-            (smem, scales),
-            (smem, here),
-            (by_slot, cotangent),
-            (by_window(width), residual),
-            (by_window(width), grad_normed2),
-            (by_window(width), attended),
-            (whole(*w_out.shape), w_out),
-            flat(norm2_gain),
-            (whole(*head_rows.shape), head_rows),
-        ],
-        [
-            (by_window(width), (total, width), f32),
-            (by_window(width), (total, width), bf16),
-            (by_head, (slots, 16, rows), f32),
-            (whole(8, width), (8, width), f32),
-            (by_window(width), (total, width), bf16),
-        ],
-        after=tokens,
-    )
-    tokens = []
-    if fast:
-        up = Chunk(
-            [(keep_up, come_up)], [(Z0, X, Y, Z1), (X, Z0, Y, Z1)], [(hidden // 2,) * 2]
+    made = {}
+
+    def keep_results(*names):
+        def finish(values):
+            made.update(zip(names, values))
+            return list(values[:1])
+
+        return finish
+
+    def middle():
+        return (
+            middle_back_kernel,
+            (slots,),
+            [
+                (smem, lengths),
+                (smem, scales),
+                (smem, here),
+                (by_slot, cotangent),
+                (by_window(width), residual),
+                (by_window(width), grad_normed2),
+                (by_window(width), attended),
+                (whole(*w_out.shape), w_out),
+                flat(norm2_gain),
+                (whole(*head_rows.shape), head_rows),
+            ],
+            [
+                (by_window(width), (total, width), f32),
+                (by_window(width), (total, width), bf16),
+                (by_head, (slots, 16, rows), f32),
+                (whole(8, width), (8, width), f32),
+                (by_window(width), (total, width), bf16),
+            ],
+            [],
+            keep_results("grad_residual", "grad_attended", "delta", "sums", "branch"),
         )
-        up.open([grad_residual])
-        tokens = up.tokens()
-
-    grad_projected, bias_sums, keep_qkvo, send_qkvo = call(
-        attend_back_kernel,
-        (slots,),
-        [
-            (smem, lengths),
-            (smem, here),
-            (by_window(width, 0), qkv),
-            (by_window(width, 1), qkv),
-            (by_window(width, 2), qkv),
-            (by_window(width), grad_attended),
-            (by_window(width), normed),
-            (by_head, log_total),
-            (by_head, delta),
-            (by_window(width), attended),
-            (by_window(width), branch_low),
-        ],
-        [
-            (by_window(3 * width), (total, 3 * width), bf16),
-            (whole(8, width), (8, width), f32),
-        ]
-        + halves(parts // 2, 4 * width),
-        [pltpu.VMEM((width, 4 * width), f32)],
-        after=tokens,
-    )
-    come_qkvo = core_swap(send_qkvo)
-    tokens = []
-    if fast:
-        down.step([grad_projected])
-        up.step(down.tokens())
-        tokens = up.tokens()
-    grad_patches, late_sums, grad_leads = call(
-        norm_back_kernel,
-        (slots,),
-        [
-            (smem, leads),
-            (by_slot, patches),
-            (by_window(width), grad_residual),
-            (by_window(3 * width), grad_projected),
-            (whole(*w_qkv.shape), w_qkv),
-            flat(norm1_gain),
-        ],
-        [
-            (by_slot, patches.shape, bf16),
-            (whole(8, width), (8, width), f32),
-            (whole(lead_count, width), (lead_count, width), f32),
-        ],
-        after=tokens,
-        micros=NB,
-    )
-    tokens = []
-    if fast:
-        last = Chunk([(keep_qkvo, come_qkvo)], orders, [LAST_SHARES])
-        last.open([late_sums])
-        down.step(last.tokens())
-        up.step(down.tokens())
-        tokens = up.tokens()
-
-    (block_out,) = call(
-        block_out_kernel,
-        (slots,),
-        [
-            (by_window(hidden), activated),
-            (whole(*w_down.shape), w_down),
-            flat(bias_down),
-            (by_window(width), residual),
-        ],
-        [(by_slot, patches.shape, bf16)],
-        after=tokens,
-    )
-
-    bias_rows = grad_bias_up[:, 0]
-    small = sum_small(jnp.concatenate([sums, bias_sums, late_sums, bias_rows, grad_leads], axis=0))
-    up_rows = bias_rows.shape[0]
-
-    if fast:
-        down.step([block_out])
-        last.step(down.tokens())
-        up.step(last.tokens())
-        (sum_down,) = down.finish([(0, 0, width)])
-        last.step(up.tokens())
-        last.step()
-        (sum_up,) = up.finish([(0, 0, hidden)])
-        sum_qkv, sum_out = last.finish([(0, 0, 3 * width), (0, 3 * width, width)])
-    else:
-        sum_down = scatter_sum(keep_down)
-        sum_up = scatter_sum(keep_up)
-        joined = scatter_sum(keep_qkvo)
-        sum_qkv, sum_out = joined[:, : 3 * width], joined[:, 3 * width :]
-    return (
-        block_out,
-        grad_patches,
-        small[16],
-        small[17],
-        small[24 + up_rows :],
-        sum_qkv,
-        small[8],
-        small[9],
-        sum_out,
-        small[2],
-        small[0],
-        small[1],
-        sum_up,
-        small[24 : 24 + up_rows].reshape(-1),
-        sum_down,
-        small[3],
-    )
+
+    half = width // 2
+
+    def attention_first():
+        return (
+            attend_back_first_kernel,
+            (slots,),
+            [
+                (smem, lengths),
+                (by_window(half, 0), qkv),
+                (by_window(half, 2), qkv),
+                (by_window(half, 4), qkv),
+                (by_window(half, 0), made["grad_attended"]),
+                (by_head, log_total),
+                (by_head, made["delta"]),
+            ],
+            [(by_window(3 * half), (total, 3 * half), bf16)],
+            [],
+            keep_results("projected_first"),
+        )
+
+    def attention():
+        return (
+            attend_back_kernel,
+            (slots,),
+            [
+                (smem, lengths),
+                (smem, here),
+                (by_window(half, 1), qkv),
+                (by_window(half, 3), qkv),
+                (by_window(half, 5), qkv),
+                (by_window(half, 1), made["grad_attended"]),
+                (by_window(width), normed),
+                (by_head, log_total),
+                (by_head, made["delta"]),
+                (by_window(width), attended),
+                (by_window(width), made["branch"]),
+                (by_window(3 * half), made["projected_first"]),
+            ],
+            [
+                (by_window(3 * width), (total, 3 * width), bf16),
+                (whole(8, width), (8, width), f32),
+            ]
+            + halves(parts // 2, 4 * width),
+            [pltpu.VMEM((width, 4 * width), f32)],
+            keep_results("grad_projected", "bias_sums", "keep_last", "send_last"),
+        )
+
+    def first_norm():
+        small_rows = 64 * width // SMALL_COLUMNS
+        return (
+            norm_back_kernel,
+            (slots,),
+            [
+                (smem, leads),
+                (by_slot, patches),
+                (by_window(width), made["grad_residual"]),
+                (by_window(3 * width), made["grad_projected"]),
+                (whole(*w_qkv.shape), w_qkv),
+                flat(norm1_gain),
+                (whole(*made["sums"].shape), made["sums"]),
+                (whole(*made["bias_sums"].shape), made["bias_sums"]),
+                (whole(*grad_bias_up.shape), grad_bias_up),
+            ],
+            [
+                (by_slot, patches.shape, bf16),
+                (whole(small_rows, SMALL_COLUMNS), (small_rows, SMALL_COLUMNS), f32),
+            ],
+            [],
+            keep_results("grad_patches", "small"),
+        )
+
+    def output():
+        return (
+            block_out_kernel,
+            (slots,),
+            [
+                (by_window(hidden), activated),
+                (whole(*w_down.shape), w_down),
+                flat(bias_down),
+                (by_window(width), residual),
+            ],
+            [(by_slot, patches.shape, bf16)],
+            [],
+            keep_results("block_out"),
+        )
+
+    def add_small(bit):
+        small = made["small"]
+        spec = whole(*small.shape)
+        inputs = [(spec, small), (spec, swap(small, "dp", bit))]
+        return add_kernel, (), inputs, [(spec, small.shape, f32)], [], keep_results("small")
+
+    def small_outs():
+        small = made["small"]
+        spec = whole(*small.shape)
+        shapes = [(width,)] * 8 + [bias_up.shape, lead_table.shape]
+        outs = [(whole(*shape), shape, f32) for shape in shapes]
+        inputs = [(spec, small), (spec, swap(small, "dp", 0))]
+        return small_out_kernel, (), inputs, outs, [], keep_results(*SMALL_NAMES)
+
+    def run(works, after):
+        counts = [[len(work[part]) for work in works] for part in (2, 3, 4)]
+
+        def kernel(*refs):
+            at = 0
+            groups = [[] for _ in works]
+            for part in counts:
+                for group, count in zip(groups, part):
+                    group.extend(refs[at : at + count])
+                    at += count
+            for work, group in zip(works, groups):
+                work[0](*group)
+
+        joined = [[item for work in works for item in work[part]] for part in (2, 3, 4)]
+        values = call(kernel, works[0][1], *joined, after=after)
+        tokens, at = [], 0
+        for work, count in zip(works, counts[1]):
+            tokens += work[5](values[at : at + count])
+            at += count
+        return tokens
+
+    def build(event):
+        name, step = event[0], event[1:]
+        if event in PLAIN:
+            works = (middle, attention_first, attention, first_norm, output)
+            return works[PLAIN.index(event)]()
+        if name == "S":
+            return small_outs() if step == "O" else add_small({"X": 1, "Z": 2}[step])
+        if step == "O":
+            keep, send, orders, shares = {
+                "D": (keep_down, send_down, DOWN_ORDERS, DOWN_SHARES),
+                "U": (keep_up, send_up, UP_ORDERS, UP_SHARES),
+                "Q": (made.get("keep_last"), made.get("send_last"), LAST_ORDERS, LAST_SHARES),
+            }[name]
+            chunks[name] = Chunk([(keep, core_swap(send))], orders, [shares])
+            return chunks[name].open()
+        chunk = chunks[name]
+        if step == "A":
+            return chunk.add()
+        if event == "DP":
+            return chunk.place([(0, 0, width)], keep_results("sum_down", "small"), rider=True)
+        if event == "UP":
+            return chunk.place([(0, 0, hidden)], keep_results("sum_up"))
+        if event == "QP":
+            outputs = [(0, 0, 3 * width), (0, 3 * width, width)]
+            return chunk.place(outputs, keep_results("sum_qkv", "sum_out"))
+        return chunk.step(made["small"] if event == "D4" else None)
+
+    chunks = {}
+    tokens = [grad_normed2]
+    for group in SEQUENCE if fast else PLAIN:
+        current[0] = group
+        tokens = run([build(event) for event in group.split("+")], tokens)
+    if not fast:
+        for bit in range(1, dp_bits()):
+            made["small"] = made["small"] + swap(made["small"], "dp", bit)
+        made["small"] = made["small"] + swap(made["small"], "outer", 0)
+        run([small_outs()], ())
+        made["sum_down"] = scatter_sum(keep_down)
+        made["sum_up"] = scatter_sum(keep_up)
+        joined = scatter_sum(made["keep_last"])
+        made["sum_qkv"], made["sum_out"] = joined[:, : 3 * width], joined[:, 3 * width :]
+    return tuple(made[name] for name in OUTPUTS)
 
 
 def solution(mesh):

time: 274 us -> 256 us (0.934)
  waiting for transfers between devices: 44.1 us -> 26.5 us
  Pallas kernels: 163 us -> 176 us
  starting transfers between devices: 50 us -> 42.3 us
  local copies, waits for them, and re-layouts: 10.5 us -> 4.79 us
    ppermute x33 -> x31, waiting for transfers between devices: 44.1 us -> 25.7 us  [swap(): return lax.ppermute(values, axis, [(i, i ^ 1 << bit) for i in range(size)])]
    pallas_call x23 -> x30, Pallas kernels: 163 us -> 176 us  [call(): pl.pallas_call(body, grid=grid, in_specs=[spec for spec, _ in inputs] + [...]
    ppermute x33 -> x31, starting transfers between devices: 40.8 us -> 32.8 us  [swap(): return lax.ppermute(values, axis, [(i, i ^ 1 << bit) for i in range(size)])]
    unnamed x49 -> x26, local copies, waits for them, and re-layouts: 5.52 us -> 4.79 us
  transfers between devices with their start and end apart: 40 -> 38, of which waited for: 12 -> 12; matrix products, arithmetic and copies ran while one was open for 2% -> 0% of each run, Pallas kernels for 52% -> 61%
where the time goes in v3:
time: 256 us; the launch traced here: 255 us
  Pallas kernels  176 us (69%)
  starting transfers between devices  42.3 us (17%)
  waiting for transfers between devices  26.5 us (10%)
  local copies, waits for them, and re-layouts  4.79 us (2%)
  other arithmetic  4.01 us (2%)
    pallas_call x30, Pallas kernels, call(): pl.pallas_call(body, grid=grid, in_specs=[spec for spec, _ in inputs] + [...  176 us
    ppermute x31, starting transfers between devices, swap(): return lax.ppermute(values, axis, [(i, i ^ 1 << bit) for i in range(size)])  32.8 us
    ppermute x31, waiting for transfers between devices, swap(): return lax.ppermute(values, axis, [(i, i ^ 1 << bit) for i in range(size)])  25.7 us
    ppermute x7, starting transfers between devices, exchange(): lax.ppermute(values, ('dp', 'outer'), [(i, i ^ flip) for i in range(size)])  9.45 us
  transfers between devices with their start and end apart: 38, of which 12 were waited for; matrix products, arithmetic and copies ran while one was open for 0% of the time, Pallas kernels for 61%

profile of v3, /device:TPU:0, one launch (start us, length us, event | category | flops | bytes accessed | tf_op | source)
XLA Modules:
  0.0 254.8 jit_solution(13950278388825608163)
XLA Ops:
  1.3 0.7 select_reduce_fusion.1
  2.5 0.8 collective-permute-done
  3.4 3.8 %collective-permute-start.3 = (f32[40]{0:T(128)S(1)}, f32[40]{0:T(128)S(1)}, u32[]{:S(2)}, u32[]{:S(2)}) collective-permute-start(f32[40]{0:T(128)S(1)} %add.27.refs_8_), channel_id=1, source_target_pairs={{0,12},{1,13},{2,14},{3,15},{4,8},{5,9},{6,10},{7,11},{8,4},{9,5},... | collective-permute-start | bytes 488 | tf_op jit(solution)/shard_map/ppermute | solution.py:477
  7.8 8.7 %shard_map.306 = (bf16[1024,768]{1,0:T(8,128)(2,1)}, bf16[1024,2304]{1,0:T(8,128)(2,1)}) custom-call(s32[4]{0:T(128)} %refs_0_.13, bf16[4,256,768]{2,1,0:T(8,128)(2,1)} %refs_1_.6, f32[768]{0:T(1024)} %refs_5_.9, f32[768]{0:T(1024)} %refs_3_.4, f32[768]{0:T(1024)} %refs_4_.4, f32[768]{0:T(1024)} %refs_5_.5, f32[40,768]{1,0:T(8,128)} %refs_6_.3, ...), custom_call_target="tpu_custom_call" | custom-call | tf_op jit(solution)/shard_map/pallas_call | solution.py:581
  17.2 3.9 %collective-permute-start.6 = (f32[40]{0:T(128)S(1)}, f32[40]{0:T(128)S(1)}, u32[]{:S(2)}, u32[]{:S(2)}) collective-permute-start(f32[40]{0:T(128)S(1)} %add_add_fusion.1.refs_7_), channel_id=1, source_target_pairs={{0,17},{1,16},{2,19},{3,18},{4,21},{5,20},{6,23},{7,22},{8,25},{9,... | collective-permute-start | bytes 488 | tf_op jit(solution)/shard_map/ppermute | solution.py:477
  21.7 11.7 %shard_map.307 = (bf16[1024,768]{1,0:T(8,128)(2,1)}, f32[1024,768]{1,0:T(8,128)}, bf16[1024,768]{1,0:T(8,128)(2,1)}, bf16[768,1024]{1,0:T(8,128)(2,1)}, f32[4,16,256]{2,1,0:T(8,128)}) custom-call(s32[4]{0:T(128)} %refs_0_.12, bf16[4,256,768]{2,1,0:T(8,128)(2,1)} %refs_1_.6, bf16[1024,2304]{1,0:T(8,128)(2,1)} %get-tuple-element.101.refs_2_.refs_1_.refs_3_.refs_4_, ...), custom_call_target="tpu_custom_call" | custom-call | tf_op jit(solution)/shard_map/pallas_call | solution.py:581
  34.9 18.4 %shard_map.308 = (bf16[1024,3072]{1,0:T(8,128)(2,1)}, bf16[1024,3072]{1,0:T(8,128)(2,1)}, bf16[1024,768]{1,0:T(8,128)(2,1)}, f32[8,192,768]{2,1,0:T(8,128)}, f32[8,192,768]{2,1,0:T(8,128)}) custom-call(s32[4]{0:T(128)} %refs_0_.12, f32[4]{0:T(128)} %compare_select_fusion.refs_1_, s32[1]{0:T(128)} %bitcast.1.refs_2_.refs_0_.refs_1_, ...), custom_call_target="tpu_custom_call" | custom-call | tf_op jit(solution)/shard_map/pallas_call | solution.py:581
  53.3 21.1 %shard_map.309 = (f32[4,1,768]{2,1,0:T(1,128)}, f32[1024,768]{1,0:T(8,128)}, f32[8,48,3072]{2,1,0:T(8,128)}, f32[8,48,3072]{2,1,0:T(8,128)}) custom-call(s32[1]{0:T(128)} %bitcast.1.refs_2_.refs_0_.refs_1_, bf16[1024,768]{1,0:T(8,128)(2,1)} %get-tuple-element.107.refs_1_, bf16[1024,3072]{1,0:T(8,128)(2,1)} %get-tuple-element.108.refs_2_, ...), custom_call_target="tpu_custom_call" | custom-call | tf_op jit(solution)/shard_map/pallas_call | solution.py:581
  75.5 6.3 %shard_map.310 = (f32[2,2,2,96,384]{4,3,2,1,0:T(8,128)}, f32[2,2,2,96,384]{4,3,2,1,0:T(8,128)}, f32[2,2,2,96,384]{4,3,2,1,0:T(8,128)}, f32[2,2,2,96,384]{4,3,2,1,0:T(8,128)}) custom-call(s32[4]{0:T(128)} %pad_add_fusion.refs_0_, f32[2,2,2,2,96,768]{5,4,3,2,1,0:T(8,128)} %bitcast.16, f32[2,2,2,2,96,768]{5,4,3,2,1,0:T(8,128)} %bitcast.7.refs_2_, ...), custom_call_target="tpu_custom_call" | custom-call | flops 34500001792 | tf_op jit(solution)/shard_map/pallas_call | solution.py:581
  81.8 1.7 collective-permute-start.8
  83.5 1.5 collective-permute-start.9
  85.6 9.7 %shard_map.311 = (f32[1024,768]{1,0:T(8,128)}, bf16[1024,768]{1,0:T(8,128)(2,1)}, f32[4,16,256]{2,1,0:T(8,128)}, f32[8,768]{1,0:T(8,128)}, bf16[1024,768]{1,0:T(8,128)(2,1)}) custom-call(s32[4]{0:T(128)} %refs_0_.12, f32[4]{0:T(128)} %compare_select_fusion.refs_1_, s32[1]{0:T(128)} %bitcast.1.refs_2_.refs_0_.refs_1_, bf16[4,256,768]{2,1,0:T(8,128)(2,1)} %refs_3_.7, ...), custom_call_target="tpu_custom_call" | custom-call | tf_op jit(solution)/shard_map/pallas_call | solution.py:581
  95.3 6.0 %shard_map.312 = (f32[2,2,2,24,1920]{4,3,2,1,0:T(8,128)}, f32[2,2,2,24,1920]{4,3,2,1,0:T(8,128)}, f32[2,2,2,24,1152]{4,3,2,1,0:T(8,128)}, f32[2,2,2,24,1152]{4,3,2,1,0:T(8,128)}) custom-call(s32[4]{0:T(128)} %pad_add_fusion.refs_0_, f32[2,2,2,2,24,3072]{5,4,3,2,1,0:T(8,128)} %bitcast.14, f32[2,2,2,2,24,3072]{5,4,3,2,1,0:T(8,128)} %bitcast.9.refs_2_, ...), custom_call_target="tpu_custom_call" | custom-call | tf_op jit(solution)/shard_map/pallas_call | solution.py:581
  101.3 1.6 collective-permute-start.13
  103.4 7.3 %shard_map.313.refs_5_.refs_11_ = bf16[1024,1152]{1,0:T(8,128)(2,1)} custom-call(s32[4]{0:T(128)} %refs_0_.12, bf16[1024,2304]{1,0:T(8,128)(2,1)} %get-tuple-element.101.refs_2_.refs_1_.refs_3_.refs_4_, bf16[1024,2304]{1,0:T(8,128)(2,1)} %get-tuple-element.101.refs_2_.refs_1_.refs_3_.refs_4_, ...), custom_call_target="tpu_custom_call" | custom-call | tf_op jit(solution)/shard_map/pallas_call | solution.py:581
  111.4 4.3 %shard_map.314 = (f32[2,2,96,384]{3,2,1,0:T(8,128)}, f32[2,2,96,384]{3,2,1,0:T(8,128)}, f32[2,2,96,384]{3,2,1,0:T(8,128)}, f32[2,2,96,384]{3,2,1,0:T(8,128)}) custom-call(s32[4]{0:T(128)} %pad_add_fusion.refs_0_, f32[2,2,2,96,384]{4,3,2,1,0:T(8,128)} %get-tuple-element.111.refs_11_.refs_1_, f32[2,2,2,96,384]{4,3,2,1,0:T(8,128)} %collective-permute-done.8.refs_2_, ...), custom_call_target="tpu_custom_call" | custom-call | tf_op jit(solution)/shard_map/pallas_call | solution.py:581
  115.8 1.5 collective-permute-start.11
  117.3 1.2 collective-permute-start.12
  118.5 17.6 %shard_map.315 = (bf16[1024,2304]{1,0:T(8,128)(2,1)}, f32[8,768]{1,0:T(8,128)}, f32[8,48,3072]{2,1,0:T(8,128)}, f32[8,48,3072]{2,1,0:T(8,128)}) custom-call(s32[4]{0:T(128)} %refs_0_.12, s32[1]{0:T(128)} %bitcast.1.refs_2_.refs_0_.refs_1_, bf16[1024,2304]{1,0:T(8,128)(2,1)} %get-tuple-element.101.refs_2_.refs_1_.refs_3_.refs_4_, ...), custom_call_target="tpu_custom_call" | custom-call | flops 2300000000 | tf_op jit(solution)/shard_map/pallas_call | solution.py:581
  136.2 0.9 copy-done.1
  137.1 3.5 %shard_map.316 = (f32[2,2,24,1920]{3,2,1,0:T(8,128)}, f32[2,2,24,1920]{3,2,1,0:T(8,128)}, f32[2,2,24,1152]{3,2,1,0:T(8,128)}, f32[2,2,24,1152]{3,2,1,0:T(8,128)}) custom-call(s32[4]{0:T(128)} %pad_add_fusion.refs_0_, f32[2,2,2,24,1920]{4,3,2,1,0:T(8,128)} %get-tuple-element.123.refs_8_.refs_1_, f32[2,2,2,24,1920]{4,3,2,1,0:T(8,128)} %collective-permute-done.13.refs_2_, ...), custom_call_target="tpu_custom_call" | custom-call | tf_op jit(solution)/shard_map/pallas_call | solution.py:581
  140.5 0.8 collective-permute-start.16
  141.4 1.6 collective-permute-start.17
  142.9 3.8 %shard_map.317 = (f32[2,96,768]{2,1,0:T(8,128)}, f32[2,96,768]{2,1,0:T(8,128)}) custom-call(s32[4]{0:T(128)} %pad_add_fusion.refs_0_, f32[2,2,96,384]{3,2,1,0:T(8,128)} %get-tuple-element.126.refs_13_.refs_1_, f32[2,2,96,384]{3,2,1,0:T(8,128)} %collective-permute-done.11.refs_2_, f32[2,2,96,384]{3,2,1,0:T(8,128)} %get-tuple-element.128.refs_15_.refs_3_, ...), custom_call_target="tpu_custom_call" | custom-call | flops 115000000512 | tf_op jit(solution)/shard_map/pallas_call | solution.py:581
  147.1 5.8 %shard_map.318 = (f32[2,2,2,24,1024]{4,3,2,1,0:T(8,128)}, f32[2,2,2,24,1024]{4,3,2,1,0:T(8,128)}, f32[2,2,2,24,1024]{4,3,2,1,0:T(8,128)}, f32[2,2,2,24,1024]{4,3...) custom-call(s32[4]{0:T(128)} %pad_add_fusion.refs_0_, ...), custom_call_target="tpu_custom_call" | custom-call | tf_op jit(solution)/shard_map/pallas_call | solution.py:581
  152.9 1.5 collective-permute-start.20
  154.4 1.5 collective-permute-start.21
  156.3 3.8 %collective-permute-done.16.refs_2_ = f32[2,2,24,1920]{3,2,1,0:T(8,128)} collective-permute-done((f32[2,2,24,1920]{3,2,1,0:T(8,128)}, f32[2,2,24,1920]{3,2,1,0:T(8,128)}, u32[]{:S(2)}, u32[]{:S(2)}) %collective-permute-start.16) | collective-permute-done | bytes 737312 | tf_op jit(solution)/shard_map/ppermute | solution.py:462
  160.1 2.5 shard_map.319
  163.1 9.8 %shard_map.320 = (bf16[4,256,768]{2,1,0:T(8,128)(2,1)}, f32[192,256]{1,0:T(8,128)}) custom-call(s32[4]{0:T(128)} %refs_0_.13, bf16[4,256,768]{2,1,0:T(8,128)(2,1)} %refs_1_.6, f32[1024,768]{1,0:T(8,128)} %get-tuple-element.121.refs_3_.refs_2_, bf16[1024,2304]{1,0:T(8,128)(2,1)} %get-tuple-element.132.refs_5_.refs_3_, bf16[768,2304]{1,0:T(8,128)(2,1)} %refs_4_.7, ...), custom_call_target="tpu_custom_call" | custom-call | tf_op jit(solution)/shard_map/pallas_call | solution.py:581
  173.0 2.3 shard_map.321
  175.3 2.6 %collective-permute-start.19 = (f32[96,1280]{1,0:T(8,128)}, f32[96,1280]{1,0:T(8,128)}, u32[]{:S(2)}, u32[]{:S(2)}) collective-permute-start(f32[96,1280]{1,0:T(8,128)} %get-tuple-element.154.refs_4_), channel_id=1, source_target_pairs={{0,16},{2,18},{4,20},{6,22},{8,24},{10,26},{12,28},{14,30},{16,0},... | collective-permute-start | bytes 1474568 | tf_op jit(solution)/shard_map/ppermute | solution.py:462
  177.9 9.9 %shard_map.322.refs_3_ = bf16[4,256,768]{2,1,0:T(8,128)(2,1)} custom-call(bf16[1024,3072]{1,0:T(8,128)(2,1)} %get-tuple-element.103.refs_0_, bf16[3072,768]{1,0:T(8,128)(2,1)} %refs_1_.7, f32[768]{0:T(1024)} %refs_2_.3, f32[1024,768]{1,0:T(8,128)} %get-tuple-element.104.refs_4_.refs_3_, f32[96,1280]{1,0:T(8,128)} %get-tuple-element.154.refs_4_, ...), custom_call_target="tpu_custom_call" | custom-call | tf_op jit(solution)/shard_map/pallas_call | solution.py:581
  187.8 2.1 shard_map.323
  190.0 0.9 collective-permute-done.22.refs_6_
  190.8 3.5 %shard_map.324 = (f32[2,2,24,1024]{3,2,1,0:T(8,128)}, f32[2,2,24,1024]{3,2,1,0:T(8,128)}, f32[2,2,24,1024]{3,2,1,0:T(8,128)}, f32[2,2,24,1024]{3,2,1,0:T(8,128)}...) custom-call(s32[4]{0:T(128)} %pad_add_fusion.refs_0_, ...), custom_call_target="tpu_custom_call" | custom-call | tf_op jit(solution)/shard_map/pallas_call | solution.py:581
  194.3 1.6 collective-permute-start.25
  195.9 1.6 collective-permute-start.26
  197.5 1.9 collective-permute-done.19.refs_1_
  199.4 2.0 shard_map.325.refs_7_.refs_1_
  201.4 1.5 collective-permute-start.24
  202.9 0.8 collective-permute-start.27
  203.7 3.0 %collective-permute-done.25.refs_2_ = f32[2,2,24,1024]{3,2,1,0:T(8,128)S(1)} collective-permute-done((f32[2,2,24,1024]{3,2,1,0:T(8,128)}, f32[2,2,24,1024]{3,2,1,0:T(8,128)S(1)}, u32[]{:S(2)}, u32[]{:S(2)}) %collective-permute-start.25) | collective-permute-done | bytes 393248 | tf_op jit(solution)/shard_map/ppermute | solution.py:462
  206.6 2.1 collective-permute-done.26.refs_4_
  208.7 3.2 %collective-permute-done.27.refs_6_ = f32[2,2,24,1024]{3,2,1,0:T(8,128)} collective-permute-done((f32[2,2,24,1024]{3,2,1,0:T(8,128)}, f32[2,2,24,1024]{3,2,1,0:T(8,128)}, u32[]{:S(2)}, u32[]{:S(2)}) %collective-permute-start.27) | collective-permute-done | bytes 393248 | tf_op jit(solution)/shard_map/ppermute | solution.py:462
  212.0 2.6 %shard_map.326 = (f32[2,24,1024]{2,1,0:T(8,128)}, f32[2,24,1024]{2,1,0:T(8,128)}, f32[2,24,1024]{2,1,0:T(8,128)}, f32[2,24,1024]{2,1,0:T(8,128)}, f32[2,24,1024]{2,1,0:T(8,128)}, /*index=5*/f32[2,24,1024]{2,1,0:T(8,128)}) custom-call(s32[4]{0:T(128)} %pad_add_fusion.refs_0_, f32[2,2,24,1024]{3,2,1,0:T(8,128)} %get-tuple-element.159.refs_3_.refs_1_, ...), custom_call_target="tpu_custom_call" | custom-call | tf_op jit(solution)/shard_map/pallas_call | solution.py:581
  214.6 0.9 collective-permute-start.29
  215.5 0.8 collective-permute-start.30
  216.8 0.8 copy-done.3
  217.6 2.1 shard_map.327
  219.7 1.2 collective-permute-start.28
  220.9 1.8 shard_map.328.refs_7_.refs_1_
  223.4 2.2 shard_map.329
  225.6 3.4 %collective-permute-start.36 = (f32[24,3072]{1,0:T(8,128)}, f32[24,3072]{1,0:T(8,128)S(1)}, u32[]{:S(2)}, u32[]{:S(2)}) collective-permute-start(f32[24,3072]{1,0:T(8,128)} %get-tuple-element.172.refs_2_), channel_id=1, source_target_pairs={{0,16},{2,18},{4,20},{6,22},{8,24},{10,26},{12,28},{14,30},{16,0},... | collective-permute-start | bytes 884744 | tf_op jit(solution)/shard_map/ppermute | solution.py:462
  229.7 1.7 shard_map.330.refs_0_.refs_2_
  231.5 1.5 collective-permute-start.35
  233.0 8.0 %collective-permute-done.33.refs_1_ = f32[192,256]{1,0:T(8,128)} collective-permute-done((f32[192,256]{1,0:T(8,128)}, f32[192,256]{1,0:T(8,128)}, u32[]{:S(2)}, u32[]{:S(2)}) %collective-permute-start.33) | collective-permute-done | bytes 196640 | tf_op jit(solution)/shard_map/ppermute | solution.py:462
  241.0 1.7 shard_map.331.refs_2_.refs_0_
  243.4 1.8 shard_map.332.refs_3_.refs_1_
  245.2 0.9 collective-permute-start.37
  246.8 1.9 shard_map.333.refs_2_
  248.7 1.7 shard_map.334
  250.5 1.7 collective-permute-done.37.refs_2_
  252.9 1.9 shard_map.335
  (78 shorter events, 12.5 us)
Async XLA Ops:
  2.0 1.3 collective-permute-start
  3.4 4.4 %copy-start.12 = (f32[40]{0:T(128)}, f32[40]{0:T(128)S(1)}, u32[]{:S(2)}) copy-start(f32[40]{0:T(128)S(1)} %add.27.refs_8_) | copy-start | bytes 484
  3.4 13.1 %collective-permute-start.3 = (f32[40]{0:T(128)S(1)}, f32[40]{0:T(128)S(1)}, u32[]{:S(2)}, u32[]{:S(2)}) collective-permute-start(f32[40]{0:T(128)S(1)} %add.27.refs_8_), channel_id=1, source_target_pairs={{0,12},{1,13},{2,14},{3,15},{4,8},{5,9},{6,10},{7,11},{8,4},{9,5},... | collective-permute-start | bytes 488 | tf_op jit(solution)/shard_map/ppermute | solution.py:477
  7.2 9.3 %collective-permute-start.1 = (f32[40]{0:T(128)S(1)}, f32[40]{0:T(128)S(1)}, u32[]{:S(2)}, u32[]{:S(2)}) collective-permute-start(f32[40]{0:T(128)S(1)} %add.27.refs_8_), channel_id=1, source_target_pairs={{0,4},{1,5},{2,6},{3,7},{4,0},{5,1},{6,2},{7,3},{8,12},{9,13},{10,... | collective-permute-start | bytes 488 | tf_op jit(solution)/shard_map/ppermute | solution.py:477
  7.7 8.8 %collective-permute-start.2 = (f32[40]{0:T(128)S(1)}, f32[40]{0:T(128)S(1)}, u32[]{:S(2)}, u32[]{:S(2)}) collective-permute-start(f32[40]{0:T(128)S(1)} %add.27.refs_8_), channel_id=1, source_target_pairs={{0,8},{1,9},{2,10},{3,11},{4,12},{5,13},{6,14},{7,15},{8,0},{9,1},... | collective-permute-start | bytes 488 | tf_op jit(solution)/shard_map/ppermute | solution.py:477
  17.2 4.5 %copy-start.10 = (f32[40]{0:T(128)}, f32[40]{0:T(128)S(1)}, u32[]{:S(2)}) copy-start(f32[40]{0:T(128)S(1)} %add_add_fusion.1.refs_7_) | copy-start | bytes 484
  17.2 16.3 %collective-permute-start.6 = (f32[40]{0:T(128)S(1)}, f32[40]{0:T(128)S(1)}, u32[]{:S(2)}, u32[]{:S(2)}) collective-permute-start(f32[40]{0:T(128)S(1)} %add_add_fusion.1.refs_7_), channel_id=1, source_target_pairs={{0,17},{1,16},{2,19},{3,18},{4,21},{5,20},{6,23},{7,22},{8,25},{9,... | collective-permute-start | bytes 488 | tf_op jit(solution)/shard_map/ppermute | solution.py:477
  21.1 12.4 %collective-permute-start.4 = (f32[40]{0:T(128)S(1)}, f32[40]{0:T(128)S(1)}, u32[]{:S(2)}, u32[]{:S(2)}) collective-permute-start(f32[40]{0:T(128)S(1)} %add_add_fusion.1.refs_7_), channel_id=1, source_target_pairs={{0,16},{1,17},{2,18},{3,19},{4,20},{5,21},{6,22},{7,23},{8,24},{9,... | collective-permute-start | bytes 488 | tf_op jit(solution)/shard_map/ppermute | solution.py:477
  21.4 12.1 %collective-permute-start.5 = (f32[40]{0:T(128)S(1)}, f32[40]{0:T(128)S(1)}, u32[]{:S(2)}, u32[]{:S(2)}) collective-permute-start(f32[40]{0:T(128)S(1)} %add_add_fusion.1.refs_7_), channel_id=1, source_target_pairs={{0,1},{1,0},{2,3},{3,2},{4,5},{5,4},{6,7},{7,6},{8,9},{9,8},{10,11... | collective-permute-start | bytes 488 | tf_op jit(solution)/shard_map/ppermute | solution.py:477
  21.7 12.4 %copy-start.11 = (s32[4]{0:T(128)S(1)}, s32[4]{0:T(128)}, u32[]{:S(2)}) copy-start(s32[4]{0:T(128)} %refs_0_.13) | copy-start | bytes 52
  53.3 22.2 %collective-permute-start.7 = (f32[8,192,768]{2,1,0:T(8,128)}, f32[8,192,768]{2,1,0:T(8,128)}, u32[]{:S(2)}, u32[]{:S(2)}) collective-permute-start(f32[8,192,768]{2,1,0:T(8,128)} %get-tuple-element.106), channel_id=1, source_target_pairs={{0,2},{2,0},{4,6},{6,4},{8,10},{10,8},{12,14},{14,12},{16,18},{18,... | collective-permute-start | bytes 14155784 | tf_op jit(solution)/shard_map/ppermute | solution.py:462
  74.3 20.9 %collective-permute-start.10 = (f32[8,48,3072]{2,1,0:T(8,128)}, f32[8,48,3072]{2,1,0:T(8,128)}, u32[]{:S(2)}, u32[]{:S(2)}) collective-permute-start(f32[8,48,3072]{2,1,0:T(8,128)} %get-tuple-element.120), channel_id=1, source_target_pairs={{0,2},{2,0},{4,6},{6,4},{8,10},{10,8},{12,14},{14,12},{16,18},{18,... | collective-permute-start | bytes 14155784 | tf_op jit(solution)/shard_map/ppermute | solution.py:462
  81.8 29.1 %collective-permute-start.8 = (f32[2,2,2,96,384]{4,3,2,1,0:T(8,128)}, f32[2,2,2,96,384]{4,3,2,1,0:T(8,128)}, u32[]{:S(2)}, u32[]{:S(2)}) collective-permute-start(f32[2,2,2,96,384]{4,3,2,1,0:T(8,128)} %get-tuple-element.112.refs_10_), channel_id=1, source_target_pairs={{0,4},{2,6},{4,0},{6,2},{8,12},{10,14},{12,8},{14,10},{16,20},{18,... | collective-permute-start | bytes 3538952 | tf_op jit(solution)/shard_map/ppermute | solution.py:462
  83.5 28.0 %collective-permute-start.9 = (f32[2,2,2,96,384]{4,3,2,1,0:T(8,128)}, f32[2,2,2,96,384]{4,3,2,1,0:T(8,128)}, u32[]{:S(2)}, u32[]{:S(2)}) collective-permute-start(f32[2,2,2,96,384]{4,3,2,1,0:T(8,128)} %get-tuple-element.114.refs_12_), channel_id=1, source_target_pairs={{0,1},{1,0},{2,3},{3,2},{4,5},{5,4},{6,7},{7,6},{8,9},{9,8},{10,11... | collective-permute-start | bytes 3538952 | tf_op jit(solution)/shard_map/ppermute | solution.py:462
  101.3 34.9 %collective-permute-start.13 = (f32[2,2,2,24,1920]{4,3,2,1,0:T(8,128)}, f32[2,2,2,24,1920]{4,3,2,1,0:T(8,128)}, u32[]{:S(2)}, u32[]{:S(2)}) collective-permute-start(f32[2,2,2,24,1920]{4,3,2,1,0:T(8,128)} %get-tuple-element.122.refs_7_), channel_id=1, source_target_pairs={{0,8},{2,10},{4,12},{6,14},{8,0},{10,2},{12,4},{14,6},{16,24},{18,... | collective-permute-start | bytes 4423688 | tf_op jit(solution)/shard_map/ppermute | solution.py:462
  102.9 33.3 %collective-permute-start.14 = (f32[2,2,2,24,1152]{4,3,2,1,0:T(8,128)}, f32[2,2,2,24,1152]{4,3,2,1,0:T(8,128)S(1)}, u32[]{:S(2)}, u32[]{:S(2)}) collective-permute-start(f32[2,2,2,24,1152]{4,3,2,1,0:T(8,128)} %get-tuple-element.124.refs_9_), channel_id=1, source_target_pairs={{0,4},{2,6},{4,0},{6,2},{8,12},{10,14},{12,8},{14,10},{16,20},{18,... | collective-permute-start | bytes 2654216 | tf_op jit(solution)/shard_map/ppermute | solution.py:462
  115.8 27.2 %collective-permute-start.11 = (f32[2,2,96,384]{3,2,1,0:T(8,128)}, f32[2,2,96,384]{3,2,1,0:T(8,128)}, u32[]{:S(2)}, u32[]{:S(2)}) collective-permute-start(f32[2,2,96,384]{3,2,1,0:T(8,128)} %get-tuple-element.127.refs_12_), channel_id=1, source_target_pairs={{0,1},{1,0},{2,3},{3,2},{4,5},{5,4},{6,7},{7,6},{8,9},{9,8},{10,11... | collective-permute-start | bytes 1769480 | tf_op jit(solution)/shard_map/ppermute | solution.py:462
  117.3 25.6 %collective-permute-start.12 = (f32[2,2,96,384]{3,2,1,0:T(8,128)}, f32[2,2,96,384]{3,2,1,0:T(8,128)}, u32[]{:S(2)}, u32[]{:S(2)}) collective-permute-start(f32[2,2,96,384]{3,2,1,0:T(8,128)} %get-tuple-element.129.refs_14_), channel_id=1, source_target_pairs={{0,4},{2,6},{4,0},{6,2},{8,12},{10,14},{12,8},{14,10},{16,20},{18,... | collective-permute-start | bytes 1769480 | tf_op jit(solution)/shard_map/ppermute | solution.py:462
  136.1 11.1 %collective-permute-start.18 = (f32[8,48,3072]{2,1,0:T(8,128)}, f32[8,48,3072]{2,1,0:T(8,128)}, u32[]{:S(2)}, u32[]{:S(2)}) collective-permute-start(f32[8,48,3072]{2,1,0:T(8,128)} %get-tuple-element.143), channel_id=1, source_target_pairs={{0,2},{2,0},{4,6},{6,4},{8,10},{10,8},{12,14},{14,12},{16,18},{18,... | collective-permute-start | bytes 14155784 | tf_op jit(solution)/shard_map/ppermute | solution.py:462
  136.2 0.9 copy-start.1
  140.5 19.6 %collective-permute-start.16 = (f32[2,2,24,1920]{3,2,1,0:T(8,128)}, f32[2,2,24,1920]{3,2,1,0:T(8,128)}, u32[]{:S(2)}, u32[]{:S(2)}) collective-permute-start(f32[2,2,24,1920]{3,2,1,0:T(8,128)} %get-tuple-element.133.refs_5_), channel_id=1, source_target_pairs={{0,4},{2,6},{4,0},{6,2},{8,12},{10,14},{12,8},{14,10},{16,20},{18,... | collective-permute-start | bytes 2211848 | tf_op jit(solution)/shard_map/ppermute | solution.py:462
  141.4 14.5 %collective-permute-start.17 = (f32[2,2,24,1152]{3,2,1,0:T(8,128)}, f32[2,2,24,1152]{3,2,1,0:T(8,128)}, u32[]{:S(2)}, u32[]{:S(2)}) collective-permute-start(f32[2,2,24,1152]{3,2,1,0:T(8,128)} %get-tuple-element.135.refs_7_), channel_id=1, source_target_pairs={{0,8},{2,10},{4,12},{6,14},{8,0},{10,2},{12,4},{14,6},{16,24},{18,... | collective-permute-start | bytes 1327112 | tf_op jit(solution)/shard_map/ppermute | solution.py:462
  146.7 26.3 %collective-permute-start.15 = (f32[2,96,768]{2,1,0:T(8,128)}, f32[2,96,768]{2,1,0:T(8,128)}, u32[]{:S(2)}, u32[]{:S(2)}) collective-permute-start(f32[2,96,768]{2,1,0:T(8,128)} %get-tuple-element.138.refs_3_), channel_id=1, source_target_pairs={{0,8},{2,10},{4,12},{6,14},{8,0},{10,2},{12,4},{14,6},{16,24},{18,... | collective-permute-start | bytes 1769480 | tf_op jit(solution)/shard_map/ppermute | solution.py:462
  152.9 37.0 %collective-permute-start.20 = (f32[2,2,2,24,1024]{4,3,2,1,0:T(8,128)}, f32[2,2,2,24,1024]{4,3,2,1,0:T(8,128)S(1)}, u32[]{:S(2)}, u32[]{:S(2)}) collective-permute-start(f32[2,2,2,24,1024]{4,3,2,1,0:T(8,128)} %get-tuple-element.144.refs_5_), channel_id=1, source_target_pairs={{0,4},{2,6},{4,0},{6,2},{8,12},{10,14},{12,8},{14,10},{16,20},{18,... | collective-permute-start | bytes 2359304 | tf_op jit(solution)/shard_map/ppermute | solution.py:462
  154.4 35.6 %collective-permute-start.21 = (f32[2,2,2,24,1024]{4,3,2,1,0:T(8,128)}, f32[2,2,2,24,1024]{4,3,2,1,0:T(8,128)}, u32[]{:S(2)}, u32[]{:S(2)}) collective-permute-start(f32[2,2,2,24,1024]{4,3,2,1,0:T(8,128)} %get-tuple-element.146.refs_7_), channel_id=1, source_target_pairs={{0,1},{1,0},{2,3},{3,2},{4,5},{5,4},{6,7},{7,6},{8,9},{9,8},{10,11... | collective-permute-start | bytes 2359304 | tf_op jit(solution)/shard_map/ppermute | solution.py:462
  155.9 34.9 %collective-permute-start.22 = (f32[2,2,2,24,1024]{4,3,2,1,0:T(8,128)}, f32[2,2,2,24,1024]{4,3,2,1,0:T(8,128)}, u32[]{:S(2)}, u32[]{:S(2)}) collective-permute-start(f32[2,2,2,24,1024]{4,3,2,1,0:T(8,128)} %get-tuple-element.148.refs_9_), channel_id=1, source_target_pairs={{0,8},{2,10},{4,12},{6,14},{8,0},{10,2},{12,4},{14,6},{16,24},{18,... | collective-permute-start | bytes 2359304 | tf_op jit(solution)/shard_map/ppermute | solution.py:462
  162.6 25.2 %collective-permute-start.23 = (f32[2,24,3072]{2,1,0:T(8,128)}, f32[2,24,3072]{2,1,0:T(8,128)}, u32[]{:S(2)}, u32[]{:S(2)}) collective-permute-start(f32[2,24,3072]{2,1,0:T(8,128)} %get-tuple-element.150.refs_9_), channel_id=1, source_target_pairs={{0,1},{1,0},{2,3},{3,2},{4,5},{5,4},{6,7},{7,6},{8,9},{9,8},{10,11... | collective-permute-start | bytes 1769480 | tf_op jit(solution)/shard_map/ppermute | solution.py:462
  175.3 24.1 %collective-permute-start.19 = (f32[96,1280]{1,0:T(8,128)}, f32[96,1280]{1,0:T(8,128)}, u32[]{:S(2)}, u32[]{:S(2)}) collective-permute-start(f32[96,1280]{1,0:T(8,128)} %get-tuple-element.154.refs_4_), channel_id=1, source_target_pairs={{0,16},{2,18},{4,20},{6,22},{8,24},{10,26},{12,28},{14,30},{16,0},... | collective-permute-start | bytes 1474568 | tf_op jit(solution)/shard_map/ppermute | solution.py:462
  189.9 0.9 copy-start.2
  194.3 12.3 %collective-permute-start.25 = (f32[2,2,24,1024]{3,2,1,0:T(8,128)}, f32[2,2,24,1024]{3,2,1,0:T(8,128)S(1)}, u32[]{:S(2)}, u32[]{:S(2)}) collective-permute-start(f32[2,2,24,1024]{3,2,1,0:T(8,128)} %get-tuple-element.158.refs_2_), channel_id=1, source_target_pairs={{0,1},{1,0},{2,3},{3,2},{4,5},{5,4},{6,7},{7,6},{8,9},{9,8},{10,11... | collective-permute-start | bytes 1179656 | tf_op jit(solution)/shard_map/ppermute | solution.py:462
  195.9 12.9 %collective-permute-start.26 = (f32[2,2,24,1024]{3,2,1,0:T(8,128)}, f32[2,2,24,1024]{3,2,1,0:T(8,128)}, u32[]{:S(2)}, u32[]{:S(2)}) collective-permute-start(f32[2,2,24,1024]{3,2,1,0:T(8,128)} %get-tuple-element.160.refs_4_), channel_id=1, source_target_pairs={{0,8},{2,10},{4,12},{6,14},{8,0},{10,2},{12,4},{14,6},{16,24},{18,... | collective-permute-start | bytes 1179656 | tf_op jit(solution)/shard_map/ppermute | solution.py:462
  201.4 15.4 %collective-permute-start.24 = (f32[96,1280]{1,0:T(8,128)}, f32[96,1280]{1,0:T(8,128)S(1)}, u32[]{:S(2)}, u32[]{:S(2)}) collective-permute-start(f32[96,1280]{1,0:T(8,128)} %shard_map.325.refs_7_.refs_1_), channel_id=1, source_target_pairs={{0,1},{1,0},{2,3},{3,2},{4,5},{5,4},{6,7},{7,6},{8,9},{9,8},{10,11... | collective-permute-start | bytes 1474568 | tf_op jit(solution)/shard_map/ppermute | solution.py:462
  202.9 9.1 %collective-permute-start.27 = (f32[2,2,24,1024]{3,2,1,0:T(8,128)}, f32[2,2,24,1024]{3,2,1,0:T(8,128)}, u32[]{:S(2)}, u32[]{:S(2)}) collective-permute-start(f32[2,2,24,1024]{3,2,1,0:T(8,128)} %get-tuple-element.162.refs_6_), channel_id=1, source_target_pairs={{0,4},{2,6},{4,0},{6,2},{8,12},{10,14},{12,8},{14,10},{16,20},{18,... | collective-permute-start | bytes 1179656 | tf_op jit(solution)/shard_map/ppermute | solution.py:462
  203.7 17.3 %collective-permute-start.32 = (f32[24,3072]{1,0:T(8,128)}, f32[24,3072]{1,0:T(8,128)}, u32[]{:S(2)}, u32[]{:S(2)}) collective-permute-start(f32[24,3072]{1,0:T(8,128)} %get-tuple-element.156.refs_7_), channel_id=1, source_target_pairs={{0,16},{2,18},{4,20},{6,22},{8,24},{10,26},{12,28},{14,30},{16,0},... | collective-permute-start | bytes 884744 | tf_op jit(solution)/shard_map/ppermute | solution.py:462
  206.6 5.3 %copy-start.4 = (f32[2,2,24,1024]{3,2,1,0:T(8,128)}, f32[2,2,24,1024]{3,2,1,0:T(8,128)S(1)}, u32[]{:S(2)}) copy-start(f32[2,2,24,1024]{3,2,1,0:T(8,128)S(1)} %collective-permute-done.25.refs_2_) | copy-start | bytes 1179652
  214.6 8.2 %collective-permute-start.29 = (f32[2,24,1024]{2,1,0:T(8,128)}, f32[2,24,1024]{2,1,0:T(8,128)S(1)}, u32[]{:S(2)}, u32[]{:S(2)}) collective-permute-start(f32[2,24,1024]{2,1,0:T(8,128)} %get-tuple-element.164.refs_3_), channel_id=1, source_target_pairs={{0,8},{2,10},{4,12},{6,14},{8,0},{10,2},{12,4},{14,6},{16,24},{18,... | collective-permute-start | bytes 589832 | tf_op jit(solution)/shard_map/ppermute | solution.py:462
  215.5 7.6 %collective-permute-start.30 = (f32[2,24,1024]{2,1,0:T(8,128)}, f32[2,24,1024]{2,1,0:T(8,128)}, u32[]{:S(2)}, u32[]{:S(2)}) collective-permute-start(f32[2,24,1024]{2,1,0:T(8,128)} %get-tuple-element.166.refs_5_), channel_id=1, source_target_pairs={{0,4},{2,6},{4,0},{6,2},{8,12},{10,14},{12,8},{14,10},{16,20},{18,... | collective-permute-start | bytes 589832 | tf_op jit(solution)/shard_map/ppermute | solution.py:462
  216.3 6.9 %collective-permute-start.31 = (f32[2,24,1024]{2,1,0:T(8,128)}, f32[2,24,1024]{2,1,0:T(8,128)}, u32[]{:S(2)}, u32[]{:S(2)}) collective-permute-start(f32[2,24,1024]{2,1,0:T(8,128)} %get-tuple-element.168.refs_7_), channel_id=1, source_target_pairs={{0,1},{1,0},{2,3},{3,2},{4,5},{5,4},{6,7},{7,6},{8,9},{9,8},{10,11... | collective-permute-start | bytes 589832 | tf_op jit(solution)/shard_map/ppermute | solution.py:462
  216.8 0.8 copy-start.3
  219.7 9.3 %collective-permute-start.28 = (f32[192,256]{1,0:T(8,128)}, f32[192,256]{1,0:T(8,128)S(1)}, u32[]{:S(2)}, u32[]{:S(2)}) collective-permute-start(f32[192,256]{1,0:T(8,128)} %get-tuple-element.170.refs_0_), channel_id=1, source_target_pairs={{0,4},{2,6},{4,0},{6,2},{8,12},{10,14},{12,8},{14,10},{16,20},{18,... | collective-permute-start | bytes 589832 | tf_op jit(solution)/shard_map/ppermute | solution.py:462
  222.7 8.8 %copy-start = (f32[24,3072]{1,0:T(8,128)S(1)}, f32[24,3072]{1,0:T(8,128)}, u32[]{:S(2)}) copy-start(f32[24,3072]{1,0:T(8,128)} %shard_map.328.refs_7_.refs_1_) | copy-start | bytes 884740
  222.7 0.7 copy-start.9
  225.6 17.1 %collective-permute-start.36 = (f32[24,3072]{1,0:T(8,128)}, f32[24,3072]{1,0:T(8,128)S(1)}, u32[]{:S(2)}, u32[]{:S(2)}) collective-permute-start(f32[24,3072]{1,0:T(8,128)} %get-tuple-element.172.refs_2_), channel_id=1, source_target_pairs={{0,16},{2,18},{4,20},{6,22},{8,24},{10,26},{12,28},{14,30},{16,0},... | collective-permute-start | bytes 884744 | tf_op jit(solution)/shard_map/ppermute | solution.py:462
  229.0 0.7 copy-start.8
  231.4 9.6 %collective-permute-start.33 = (f32[192,256]{1,0:T(8,128)}, f32[192,256]{1,0:T(8,128)}, u32[]{:S(2)}, u32[]{:S(2)}) collective-permute-start(f32[192,256]{1,0:T(8,128)} %shard_map.330.refs_0_.refs_2_), channel_id=1, source_target_pairs={{0,8},{2,10},{4,12},{6,14},{8,0},{10,2},{12,4},{14,6},{16,24},{18,... | collective-permute-start | bytes 589832 | tf_op jit(solution)/shard_map/ppermute | solution.py:462
  231.5 14.6 %collective-permute-start.35 = (f32[24,3072]{1,0:T(8,128)S(1)}, f32[24,3072]{1,0:T(8,128)S(1)}, u32[]{:S(2)}, u32[]{:S(2)}) collective-permute-start(f32[24,3072]{1,0:T(8,128)S(1)} %copy-done), channel_id=1, source_target_pairs={{0,1},{1,0},{2,3},{3,2},{4,5},{5,4},{6,7},{7,6},{8,9},{9,8},{10,11... | collective-permute-start | bytes 884744 | tf_op jit(solution)/shard_map/ppermute | solution.py:462
  242.7 0.7 copy-start.6
  245.2 6.9 %collective-permute-start.37 = (f32[24,3072]{1,0:T(8,128)}, f32[24,3072]{1,0:T(8,128)S(1)}, u32[]{:S(2)}, u32[]{:S(2)}) collective-permute-start(f32[24,3072]{1,0:T(8,128)} %shard_map.332.refs_3_.refs_1_), channel_id=1, source_target_pairs={{0,1},{1,0},{2,3},{3,2},{4,5},{5,4},{6,7},{7,6},{8,9},{9,8},{10,11... | collective-permute-start | bytes 884744 | tf_op jit(solution)/shard_map/ppermute | solution.py:462
  246.1 2.6 %collective-permute-start.34 = (f32[192,256]{1,0:T(8,128)}, f32[192,256]{1,0:T(8,128)}, u32[]{:S(2)}, u32[]{:S(2)}) collective-permute-start(f32[192,256]{1,0:T(8,128)} %shard_map.331.refs_2_.refs_0_), channel_id=1, source_target_pairs={{0,2},{2,0},{4,6},{6,4},{8,10},{10,8},{12,14},{14,12},{16,18},{18,... | collective-permute-start | bytes 589832 | tf_op jit(solution)/shard_map/ppermute | solution.py:462
  246.1 0.7 copy-start.7
  252.2 0.7 copy-start.5

commit v4 on v3

--- a/solution.py
+++ b/solution.py
@@ -214,7 +214,6 @@
     attended,
     w_out,
     gain,
-    head_rows,
     grad_residual,
     grad_attended,
     delta,
@@ -246,7 +245,10 @@
     product = grad_att.astype(jnp.float32) * attended[...].astype(jnp.float32)
     high = product.astype(jnp.bfloat16)
     low = (product - high.astype(jnp.float32)).astype(jnp.bfloat16)
-    delta[0] = dot_nt(head_rows[...], high) + dot_nt(head_rows[...], low)
+    head = lax.broadcasted_iota(jnp.int32, (delta.shape[1], width), 0)
+    column = lax.broadcasted_iota(jnp.int32, (delta.shape[1], width), 1)
+    head_rows = (column // (width // HEADS) == head).astype(jnp.bfloat16)
+    delta[0] = dot_nt(head_rows, high) + dot_nt(head_rows, low)
 
 
 def attend_back_heads(first, lengths, refs, log_total, delta, out, columns):
@@ -722,7 +724,6 @@
         merge = len(set(axes)) == 1 and len({tuple(dims[p[0][0]]) for p in parts}) == 1
         gridded = all(d[0] == Z1 and len(d) > 1 for d in dims) and Z1 not in axes and not riders
         rows_here = pairs[0][0].shape[-2]
-        blocks = 2 if gridded and rows_here % 48 == 0 else 1
         widths = [sum(width for _, _, width in part) for part in parts]
         left = [[d for d in dims[part[0][0]] if d != axis] for part, axis in zip(parts, axes)]
         if merge:
@@ -734,9 +735,7 @@
         def spec(shape):
             if not gridded:
                 return whole(*shape)
-            block = (1,) + shape[1:-2] + (rows_here // blocks, shape[-1])
-            middle = (0,) * (len(shape) - 3)
-            return pl.BlockSpec(block, lambda i: (i // blocks, *middle, i % blocks, 0))
+            return pl.BlockSpec((1,) + shape[1:], lambda i: (i,) + (0,) * (len(shape) - 1))
 
         inputs = [(smem, bits)] + [(spec(v.shape), v) for pair in pairs for v in pair]
         if riders == "join":
@@ -750,7 +749,7 @@
             done([(values[2 * i], values[2 * i + 1]) for i in range(len(shapes))], left)
             return list(values)
 
-        return kernel, (2 * blocks,) if gridded else (), inputs, outs, [], finish
+        return kernel, (2,) if gridded else (), inputs, outs, [], finish
 
     class Chunk:
         def __init__(self, sources, orders, shares):
@@ -821,10 +820,6 @@
 
     come_down = core_swap(send_down)
     come_up = core_swap(send_up)
-    head_rows = (
-        jnp.arange(16, dtype=jnp.int32)[:, None]
-        == jnp.arange(width, dtype=jnp.int32)[None, :] // (width // HEADS)
-    ).astype(bf16)
     made = {}
 
     def keep_results(*names):
@@ -848,7 +843,6 @@
                 (by_window(width), attended),
                 (whole(*w_out.shape), w_out),
                 flat(norm2_gain),
-                (whole(*head_rows.shape), head_rows),
             ],
             [
                 (by_window(width), (total, width), f32),

time: 256 us -> 254 us (level)
  Pallas kernels: 176 us -> 173 us
    pallas_call x30, Pallas kernels: 176 us -> 173 us  [call(): pl.pallas_call(body, grid=grid, in_specs=[spec for spec, _ in inputs] + [...]
  transfers between devices with their start and end apart: 38 -> 38, of which waited for: 12 -> 10; matrix products, arithmetic and copies ran while one was open for 0% -> 0% of each run, Pallas kernels for 61% -> 60%
where the time goes in v4:
time: 254 us; the launch traced here: 253 us
  Pallas kernels  173 us (68%)
  starting transfers between devices  40.7 us (16%)
  waiting for transfers between devices  28.8 us (11%)
  local copies, waits for them, and re-layouts  6.03 us (2%)
  other arithmetic  3.38 us (1%)
    pallas_call x30, Pallas kernels, call(): pl.pallas_call(body, grid=grid, in_specs=[spec for spec, _ in inputs] + [...  173 us
    ppermute x31, starting transfers between devices, swap(): return lax.ppermute(values, axis, [(i, i ^ 1 << bit) for i in range(size)])  31.3 us
    ppermute x31, waiting for transfers between devices, swap(): return lax.ppermute(values, axis, [(i, i ^ 1 << bit) for i in range(size)])  28 us
    ppermute x7, starting transfers between devices, exchange(): lax.ppermute(values, ('dp', 'outer'), [(i, i ^ flip) for i in range(size)])  9.45 us
    unnamed x26, local copies, waits for them, and re-layouts  6.03 us
  transfers between devices with their start and end apart: 38, of which 10 were waited for; matrix products, arithmetic and copies ran while one was open for 0% of the time, Pallas kernels for 60%

profile of v4, /device:TPU:0, one launch (start us, length us, event | category | flops | bytes accessed | tf_op | source)
XLA Modules:
  0.0 253.5 jit_solution(2646351975814983178)
XLA Ops:
  1.3 0.7 select_reduce_fusion.1
  2.5 0.8 collective-permute-done
  3.4 3.8 %collective-permute-start.3 = (f32[40]{0:T(128)S(1)}, f32[40]{0:T(128)S(1)}, u32[]{:S(2)}, u32[]{:S(2)}) collective-permute-start(f32[40]{0:T(128)S(1)} %add.21.refs_8_), channel_id=1, source_target_pairs={{0,12},{1,13},{2,14},{3,15},{4,8},{5,9},{6,10},{7,11},{8,4},{9,5},... | collective-permute-start | bytes 488 | tf_op jit(solution)/shard_map/ppermute | solution.py:479
  7.8 8.7 %shard_map.306 = (bf16[1024,768]{1,0:T(8,128)(2,1)}, bf16[1024,2304]{1,0:T(8,128)(2,1)}) custom-call(s32[4]{0:T(128)} %refs_0_.13, bf16[4,256,768]{2,1,0:T(8,128)(2,1)} %refs_1_.6, f32[768]{0:T(1024)} %refs_5_.9, f32[768]{0:T(1024)} %refs_3_.4, f32[768]{0:T(1024)} %refs_4_.4, f32[768]{0:T(1024)} %refs_5_.5, f32[40,768]{1,0:T(8,128)} %refs_6_.3, ...), custom_call_target="tpu_custom_call" | custom-call | tf_op jit(solution)/shard_map/pallas_call | solution.py:583
  17.2 3.9 %collective-permute-start.6 = (f32[40]{0:T(128)S(1)}, f32[40]{0:T(128)S(1)}, u32[]{:S(2)}, u32[]{:S(2)}) collective-permute-start(f32[40]{0:T(128)S(1)} %add_add_fusion.1.refs_7_), channel_id=1, source_target_pairs={{0,17},{1,16},{2,19},{3,18},{4,21},{5,20},{6,23},{7,22},{8,25},{9,... | collective-permute-start | bytes 488 | tf_op jit(solution)/shard_map/ppermute | solution.py:479
  21.7 11.7 %shard_map.307 = (bf16[1024,768]{1,0:T(8,128)(2,1)}, f32[1024,768]{1,0:T(8,128)}, bf16[1024,768]{1,0:T(8,128)(2,1)}, bf16[768,1024]{1,0:T(8,128)(2,1)}, f32[4,16,256]{2,1,0:T(8,128)}) custom-call(s32[4]{0:T(128)} %refs_0_.12, bf16[4,256,768]{2,1,0:T(8,128)(2,1)} %refs_1_.6, bf16[1024,2304]{1,0:T(8,128)(2,1)} %get-tuple-element.101.refs_2_.refs_1_.refs_3_.refs_4_, ...), custom_call_target="tpu_custom_call" | custom-call | tf_op jit(solution)/shard_map/pallas_call | solution.py:583
  34.9 18.4 %shard_map.308 = (bf16[1024,3072]{1,0:T(8,128)(2,1)}, bf16[1024,3072]{1,0:T(8,128)(2,1)}, bf16[1024,768]{1,0:T(8,128)(2,1)}, f32[8,192,768]{2,1,0:T(8,128)}, f32[8,192,768]{2,1,0:T(8,128)}) custom-call(s32[4]{0:T(128)} %refs_0_.12, f32[4]{0:T(128)} %compare_select_fusion.refs_1_, s32[1]{0:T(128)} %bitcast.1.refs_2_.refs_0_.refs_1_, ...), custom_call_target="tpu_custom_call" | custom-call | tf_op jit(solution)/shard_map/pallas_call | solution.py:583
  53.3 21.1 %shard_map.309 = (f32[4,1,768]{2,1,0:T(1,128)}, f32[1024,768]{1,0:T(8,128)}, f32[8,48,3072]{2,1,0:T(8,128)}, f32[8,48,3072]{2,1,0:T(8,128)}) custom-call(s32[1]{0:T(128)} %bitcast.1.refs_2_.refs_0_.refs_1_, bf16[1024,768]{1,0:T(8,128)(2,1)} %get-tuple-element.107.refs_1_, bf16[1024,3072]{1,0:T(8,128)(2,1)} %get-tuple-element.108.refs_2_, ...), custom_call_target="tpu_custom_call" | custom-call | tf_op jit(solution)/shard_map/pallas_call | solution.py:583
  75.5 5.8 %shard_map.310 = (f32[2,2,2,96,384]{4,3,2,1,0:T(8,128)}, f32[2,2,2,96,384]{4,3,2,1,0:T(8,128)}, f32[2,2,2,96,384]{4,3,2,1,0:T(8,128)}, f32[2,2,2,96,384]{4,3,2,1,0:T(8,128)}) custom-call(s32[4]{0:T(128)} %pad_add_fusion.refs_0_, f32[2,2,2,2,96,768]{5,4,3,2,1,0:T(8,128)} %bitcast.16, f32[2,2,2,2,96,768]{5,4,3,2,1,0:T(8,128)} %bitcast.7.refs_2_, ...), custom_call_target="tpu_custom_call" | custom-call | flops 34500001792 | tf_op jit(solution)/shard_map/pallas_call | solution.py:583
  81.2 1.7 collective-permute-start.8
  82.9 1.5 collective-permute-start.9
  84.5 9.7 %shard_map.311 = (f32[1024,768]{1,0:T(8,128)}, bf16[1024,768]{1,0:T(8,128)(2,1)}, f32[4,16,256]{2,1,0:T(8,128)}, f32[8,768]{1,0:T(8,128)}, bf16[1024,768]{1,0:T(8,128)(2,1)}) custom-call(s32[4]{0:T(128)} %refs_0_.12, f32[4]{0:T(128)} %compare_select_fusion.refs_1_, s32[1]{0:T(128)} %bitcast.1.refs_2_.refs_0_.refs_1_, bf16[4,256,768]{2,1,0:T(8,128)(2,1)} %refs_3_.7, ...), custom_call_target="tpu_custom_call" | custom-call | tf_op jit(solution)/shard_map/pallas_call | solution.py:583
  94.2 6.0 %shard_map.312 = (f32[2,2,2,24,1920]{4,3,2,1,0:T(8,128)}, f32[2,2,2,24,1920]{4,3,2,1,0:T(8,128)}, f32[2,2,2,24,1152]{4,3,2,1,0:T(8,128)}, f32[2,2,2,24,1152]{4,3,2,1,0:T(8,128)}) custom-call(s32[4]{0:T(128)} %pad_add_fusion.refs_0_, f32[2,2,2,2,24,3072]{5,4,3,2,1,0:T(8,128)} %bitcast.14, f32[2,2,2,2,24,3072]{5,4,3,2,1,0:T(8,128)} %bitcast.9.refs_2_, ...), custom_call_target="tpu_custom_call" | custom-call | tf_op jit(solution)/shard_map/pallas_call | solution.py:583
  100.2 1.6 collective-permute-start.13
  102.3 7.3 %shard_map.313.refs_5_.refs_11_ = bf16[1024,1152]{1,0:T(8,128)(2,1)} custom-call(s32[4]{0:T(128)} %refs_0_.12, bf16[1024,2304]{1,0:T(8,128)(2,1)} %get-tuple-element.101.refs_2_.refs_1_.refs_3_.refs_4_, bf16[1024,2304]{1,0:T(8,128)(2,1)} %get-tuple-element.101.refs_2_.refs_1_.refs_3_.refs_4_, ...), custom_call_target="tpu_custom_call" | custom-call | tf_op jit(solution)/shard_map/pallas_call | solution.py:583
  109.6 0.8 collective-permute-done.8.refs_2_
  110.9 3.5 %shard_map.314 = (f32[2,2,96,384]{3,2,1,0:T(8,128)}, f32[2,2,96,384]{3,2,1,0:T(8,128)}, f32[2,2,96,384]{3,2,1,0:T(8,128)}, f32[2,2,96,384]{3,2,1,0:T(8,128)}) custom-call(s32[4]{0:T(128)} %pad_add_fusion.refs_0_, f32[2,2,2,96,384]{4,3,2,1,0:T(8,128)} %get-tuple-element.111.refs_10_.refs_1_, f32[2,2,2,96,384]{4,3,2,1,0:T(8,128)} %collective-permute-done.8.refs_2_, ...), custom_call_target="tpu_custom_call" | custom-call | tf_op jit(solution)/shard_map/pallas_call | solution.py:583
  114.4 1.5 collective-permute-start.11
  115.9 1.2 collective-permute-start.12
  117.1 17.6 %shard_map.315 = (bf16[1024,2304]{1,0:T(8,128)(2,1)}, f32[8,768]{1,0:T(8,128)}, f32[8,48,3072]{2,1,0:T(8,128)}, f32[8,48,3072]{2,1,0:T(8,128)}) custom-call(s32[4]{0:T(128)} %refs_0_.12, s32[1]{0:T(128)} %bitcast.1.refs_2_.refs_0_.refs_1_, bf16[1024,2304]{1,0:T(8,128)(2,1)} %get-tuple-element.101.refs_2_.refs_1_.refs_3_.refs_4_, ...), custom_call_target="tpu_custom_call" | custom-call | flops 2300000000 | tf_op jit(solution)/shard_map/pallas_call | solution.py:583
  134.8 0.9 copy-done.1
  135.7 3.5 %shard_map.316 = (f32[2,2,24,1920]{3,2,1,0:T(8,128)}, f32[2,2,24,1920]{3,2,1,0:T(8,128)}, f32[2,2,24,1152]{3,2,1,0:T(8,128)}, f32[2,2,24,1152]{3,2,1,0:T(8,128)}) custom-call(s32[4]{0:T(128)} %pad_add_fusion.refs_0_, f32[2,2,2,24,1920]{4,3,2,1,0:T(8,128)} %get-tuple-element.123.refs_8_.refs_1_, f32[2,2,2,24,1920]{4,3,2,1,0:T(8,128)} %collective-permute-done.13.refs_2_, ...), custom_call_target="tpu_custom_call" | custom-call | tf_op jit(solution)/shard_map/pallas_call | solution.py:583
  139.1 1.6 collective-permute-start.17
  140.7 0.8 collective-permute-start.16
  141.5 2.5 shard_map.317
  144.0 1.3 collective-permute-start.15
  145.4 5.8 %shard_map.318 = (f32[2,2,2,24,1024]{4,3,2,1,0:T(8,128)}, f32[2,2,2,24,1024]{4,3,2,1,0:T(8,128)}, f32[2,2,2,24,1024]{4,3,2,1,0:T(8,128)}, f32[2,2,2,24,1024]{4,3...) custom-call(s32[4]{0:T(128)} %pad_add_fusion.refs_0_, ...), custom_call_target="tpu_custom_call" | custom-call | tf_op jit(solution)/shard_map/pallas_call | solution.py:583
  151.1 1.5 collective-permute-start.20
  152.6 1.7 collective-permute-start.21
  154.6 5.8 %collective-permute-done.16.refs_2_ = f32[2,2,24,1920]{3,2,1,0:T(8,128)} collective-permute-done((f32[2,2,24,1920]{3,2,1,0:T(8,128)}, f32[2,2,24,1920]{3,2,1,0:T(8,128)}, u32[]{:S(2)}, u32[]{:S(2)}) %collective-permute-start.16) | collective-permute-done | bytes 737312 | tf_op jit(solution)/shard_map/ppermute | solution.py:464
  160.3 2.5 shard_map.319
  163.3 9.8 %shard_map.320 = (bf16[4,256,768]{2,1,0:T(8,128)(2,1)}, f32[192,256]{1,0:T(8,128)}) custom-call(s32[4]{0:T(128)} %refs_0_.13, bf16[4,256,768]{2,1,0:T(8,128)(2,1)} %refs_1_.6, f32[1024,768]{1,0:T(8,128)} %get-tuple-element.121.refs_3_.refs_2_, bf16[1024,2304]{1,0:T(8,128)(2,1)} %get-tuple-element.132.refs_5_.refs_3_, bf16[768,2304]{1,0:T(8,128)(2,1)} %refs_4_.7, ...), custom_call_target="tpu_custom_call" | custom-call | tf_op jit(solution)/shard_map/pallas_call | solution.py:583
  173.2 2.3 shard_map.321
  175.5 2.6 %collective-permute-start.19 = (f32[96,1280]{1,0:T(8,128)}, f32[96,1280]{1,0:T(8,128)}, u32[]{:S(2)}, u32[]{:S(2)}) collective-permute-start(f32[96,1280]{1,0:T(8,128)} %get-tuple-element.154.refs_4_), channel_id=1, source_target_pairs={{0,16},{2,18},{4,20},{6,22},{8,24},{10,26},{12,28},{14,30},{16,0},... | collective-permute-start | bytes 1474568 | tf_op jit(solution)/shard_map/ppermute | solution.py:464
  178.1 9.9 %shard_map.322.refs_3_ = bf16[4,256,768]{2,1,0:T(8,128)(2,1)} custom-call(bf16[1024,3072]{1,0:T(8,128)(2,1)} %get-tuple-element.103.refs_0_, bf16[3072,768]{1,0:T(8,128)(2,1)} %refs_1_.7, f32[768]{0:T(1024)} %refs_2_.3, f32[1024,768]{1,0:T(8,128)} %get-tuple-element.104.refs_4_.refs_3_, f32[96,1280]{1,0:T(8,128)} %get-tuple-element.154.refs_4_, ...), custom_call_target="tpu_custom_call" | custom-call | tf_op jit(solution)/shard_map/pallas_call | solution.py:583
  188.0 2.1 shard_map.323
  190.2 0.9 copy-done.2
  191.0 3.5 %shard_map.324 = (f32[2,2,24,1024]{3,2,1,0:T(8,128)}, f32[2,2,24,1024]{3,2,1,0:T(8,128)}, f32[2,2,24,1024]{3,2,1,0:T(8,128)}, f32[2,2,24,1024]{3,2,1,0:T(8,128)}...) custom-call(s32[4]{0:T(128)} %pad_add_fusion.refs_0_, ...), custom_call_target="tpu_custom_call" | custom-call | tf_op jit(solution)/shard_map/pallas_call | solution.py:583
  194.5 1.6 collective-permute-start.25
  196.5 2.4 collective-permute-done.19.refs_1_
  198.9 2.0 shard_map.325.refs_7_.refs_1_
  200.9 1.5 collective-permute-start.24
  202.4 0.8 collective-permute-start.27
  203.3 3.3 %collective-permute-done.25.refs_2_ = f32[2,2,24,1024]{3,2,1,0:T(8,128)S(1)} collective-permute-done((f32[2,2,24,1024]{3,2,1,0:T(8,128)}, f32[2,2,24,1024]{3,2,1,0:T(8,128)S(1)}, u32[]{:S(2)}, u32[]{:S(2)}) %collective-permute-start.25) | collective-permute-done | bytes 393248 | tf_op jit(solution)/shard_map/ppermute | solution.py:464
  206.6 1.8 collective-permute-done.26.refs_4_
  208.4 2.4 collective-permute-done.27.refs_6_
  210.9 2.6 %shard_map.326 = (f32[2,24,1024]{2,1,0:T(8,128)}, f32[2,24,1024]{2,1,0:T(8,128)}, f32[2,24,1024]{2,1,0:T(8,128)}, f32[2,24,1024]{2,1,0:T(8,128)}, f32[2,24,1024]{2,1,0:T(8,128)}, /*index=5*/f32[2,24,1024]{2,1,0:T(8,128)}) custom-call(s32[4]{0:T(128)} %pad_add_fusion.refs_0_, f32[2,2,24,1024]{3,2,1,0:T(8,128)} %get-tuple-element.159.refs_3_.refs_1_, ...), custom_call_target="tpu_custom_call" | custom-call | tf_op jit(solution)/shard_map/pallas_call | solution.py:583
  213.6 0.9 collective-permute-start.30
  214.5 1.2 collective-permute-start.31
  215.7 0.8 copy-done.3
  216.5 2.1 shard_map.327
  219.1 1.8 shard_map.328.refs_7_.refs_1_
  221.5 2.2 shard_map.329
  223.7 3.2 %collective-permute-start.36 = (f32[24,3072]{1,0:T(8,128)}, f32[24,3072]{1,0:T(8,128)S(1)}, u32[]{:S(2)}, u32[]{:S(2)}) collective-permute-start(f32[24,3072]{1,0:T(8,128)} %get-tuple-element.172.refs_2_), channel_id=1, source_target_pairs={{0,16},{2,18},{4,20},{6,22},{8,24},{10,26},{12,28},{14,30},{16,0},... | collective-permute-start | bytes 884744 | tf_op jit(solution)/shard_map/ppermute | solution.py:464
  227.6 1.7 shard_map.330.refs_0_.refs_2_
  229.4 1.4 collective-permute-start.35
  230.8 8.9 %collective-permute-done.33.refs_1_ = f32[192,256]{1,0:T(8,128)} collective-permute-done((f32[192,256]{1,0:T(8,128)}, f32[192,256]{1,0:T(8,128)}, u32[]{:S(2)}, u32[]{:S(2)}) %collective-permute-start.33) | collective-permute-done | bytes 196640 | tf_op jit(solution)/shard_map/ppermute | solution.py:464
  239.7 1.7 shard_map.331.refs_2_.refs_0_
  241.4 0.7 copy-done.6
  242.2 1.8 shard_map.332.refs_3_.refs_1_
  245.3 1.9 shard_map.333.refs_2_
  247.2 1.7 shard_map.334
  248.9 2.0 collective-permute-done.37.refs_2_
  251.6 1.9 shard_map.335
  (76 shorter events, 11.3 us)
Async XLA Ops:
  2.0 1.3 collective-permute-start
  3.4 4.4 %copy-start.12 = (f32[40]{0:T(128)}, f32[40]{0:T(128)S(1)}, u32[]{:S(2)}) copy-start(f32[40]{0:T(128)S(1)} %add.21.refs_8_) | copy-start | bytes 484
  3.4 13.1 %collective-permute-start.3 = (f32[40]{0:T(128)S(1)}, f32[40]{0:T(128)S(1)}, u32[]{:S(2)}, u32[]{:S(2)}) collective-permute-start(f32[40]{0:T(128)S(1)} %add.21.refs_8_), channel_id=1, source_target_pairs={{0,12},{1,13},{2,14},{3,15},{4,8},{5,9},{6,10},{7,11},{8,4},{9,5},... | collective-permute-start | bytes 488 | tf_op jit(solution)/shard_map/ppermute | solution.py:479
  7.2 9.3 %collective-permute-start.2 = (f32[40]{0:T(128)S(1)}, f32[40]{0:T(128)S(1)}, u32[]{:S(2)}, u32[]{:S(2)}) collective-permute-start(f32[40]{0:T(128)S(1)} %add.21.refs_8_), channel_id=1, source_target_pairs={{0,8},{1,9},{2,10},{3,11},{4,12},{5,13},{6,14},{7,15},{8,0},{9,1},... | collective-permute-start | bytes 488 | tf_op jit(solution)/shard_map/ppermute | solution.py:479
  7.6 8.9 %collective-permute-start.1 = (f32[40]{0:T(128)S(1)}, f32[40]{0:T(128)S(1)}, u32[]{:S(2)}, u32[]{:S(2)}) collective-permute-start(f32[40]{0:T(128)S(1)} %add.21.refs_8_), channel_id=1, source_target_pairs={{0,4},{1,5},{2,6},{3,7},{4,0},{5,1},{6,2},{7,3},{8,12},{9,13},{10,... | collective-permute-start | bytes 488 | tf_op jit(solution)/shard_map/ppermute | solution.py:479
  17.2 4.5 %copy-start.10 = (f32[40]{0:T(128)}, f32[40]{0:T(128)S(1)}, u32[]{:S(2)}) copy-start(f32[40]{0:T(128)S(1)} %add_add_fusion.1.refs_7_) | copy-start | bytes 484
  17.2 16.3 %collective-permute-start.6 = (f32[40]{0:T(128)S(1)}, f32[40]{0:T(128)S(1)}, u32[]{:S(2)}, u32[]{:S(2)}) collective-permute-start(f32[40]{0:T(128)S(1)} %add_add_fusion.1.refs_7_), channel_id=1, source_target_pairs={{0,17},{1,16},{2,19},{3,18},{4,21},{5,20},{6,23},{7,22},{8,25},{9,... | collective-permute-start | bytes 488 | tf_op jit(solution)/shard_map/ppermute | solution.py:479
  21.1 12.4 %collective-permute-start.5 = (f32[40]{0:T(128)S(1)}, f32[40]{0:T(128)S(1)}, u32[]{:S(2)}, u32[]{:S(2)}) collective-permute-start(f32[40]{0:T(128)S(1)} %add_add_fusion.1.refs_7_), channel_id=1, source_target_pairs={{0,1},{1,0},{2,3},{3,2},{4,5},{5,4},{6,7},{7,6},{8,9},{9,8},{10,11... | collective-permute-start | bytes 488 | tf_op jit(solution)/shard_map/ppermute | solution.py:479
  21.6 11.9 %collective-permute-start.4 = (f32[40]{0:T(128)S(1)}, f32[40]{0:T(128)S(1)}, u32[]{:S(2)}, u32[]{:S(2)}) collective-permute-start(f32[40]{0:T(128)S(1)} %add_add_fusion.1.refs_7_), channel_id=1, source_target_pairs={{0,16},{1,17},{2,18},{3,19},{4,20},{5,21},{6,22},{7,23},{8,24},{9,... | collective-permute-start | bytes 488 | tf_op jit(solution)/shard_map/ppermute | solution.py:479
  21.7 12.4 %copy-start.11 = (s32[4]{0:T(128)S(1)}, s32[4]{0:T(128)}, u32[]{:S(2)}) copy-start(s32[4]{0:T(128)} %refs_0_.13) | copy-start | bytes 52
  53.3 22.2 %collective-permute-start.7 = (f32[8,192,768]{2,1,0:T(8,128)}, f32[8,192,768]{2,1,0:T(8,128)}, u32[]{:S(2)}, u32[]{:S(2)}) collective-permute-start(f32[8,192,768]{2,1,0:T(8,128)} %get-tuple-element.106), channel_id=1, source_target_pairs={{0,2},{2,0},{4,6},{6,4},{8,10},{10,8},{12,14},{14,12},{16,18},{18,... | collective-permute-start | bytes 14155784 | tf_op jit(solution)/shard_map/ppermute | solution.py:464
  74.3 19.8 %collective-permute-start.10 = (f32[8,48,3072]{2,1,0:T(8,128)}, f32[8,48,3072]{2,1,0:T(8,128)}, u32[]{:S(2)}, u32[]{:S(2)}) collective-permute-start(f32[8,48,3072]{2,1,0:T(8,128)} %get-tuple-element.120), channel_id=1, source_target_pairs={{0,2},{2,0},{4,6},{6,4},{8,10},{10,8},{12,14},{14,12},{16,18},{18,... | collective-permute-start | bytes 14155784 | tf_op jit(solution)/shard_map/ppermute | solution.py:464
  81.2 29.1 %collective-permute-start.8 = (f32[2,2,2,96,384]{4,3,2,1,0:T(8,128)}, f32[2,2,2,96,384]{4,3,2,1,0:T(8,128)}, u32[]{:S(2)}, u32[]{:S(2)}) collective-permute-start(f32[2,2,2,96,384]{4,3,2,1,0:T(8,128)} %get-tuple-element.112.refs_9_), channel_id=1, source_target_pairs={{0,4},{2,6},{4,0},{6,2},{8,12},{10,14},{12,8},{14,10},{16,20},{18,... | collective-permute-start | bytes 3538952 | tf_op jit(solution)/shard_map/ppermute | solution.py:464
  82.9 28.0 %collective-permute-start.9 = (f32[2,2,2,96,384]{4,3,2,1,0:T(8,128)}, f32[2,2,2,96,384]{4,3,2,1,0:T(8,128)}, u32[]{:S(2)}, u32[]{:S(2)}) collective-permute-start(f32[2,2,2,96,384]{4,3,2,1,0:T(8,128)} %get-tuple-element.114.refs_11_), channel_id=1, source_target_pairs={{0,1},{1,0},{2,3},{3,2},{4,5},{5,4},{6,7},{7,6},{8,9},{9,8},{10,11... | collective-permute-start | bytes 3538952 | tf_op jit(solution)/shard_map/ppermute | solution.py:464
  100.2 34.6 %collective-permute-start.13 = (f32[2,2,2,24,1920]{4,3,2,1,0:T(8,128)}, f32[2,2,2,24,1920]{4,3,2,1,0:T(8,128)}, u32[]{:S(2)}, u32[]{:S(2)}) collective-permute-start(f32[2,2,2,24,1920]{4,3,2,1,0:T(8,128)} %get-tuple-element.122.refs_7_), channel_id=1, source_target_pairs={{0,8},{2,10},{4,12},{6,14},{8,0},{10,2},{12,4},{14,6},{16,24},{18,... | collective-permute-start | bytes 4423688 | tf_op jit(solution)/shard_map/ppermute | solution.py:464
  101.8 33.0 %collective-permute-start.14 = (f32[2,2,2,24,1152]{4,3,2,1,0:T(8,128)}, f32[2,2,2,24,1152]{4,3,2,1,0:T(8,128)S(1)}, u32[]{:S(2)}, u32[]{:S(2)}) collective-permute-start(f32[2,2,2,24,1152]{4,3,2,1,0:T(8,128)} %get-tuple-element.124.refs_9_), channel_id=1, source_target_pairs={{0,4},{2,6},{4,0},{6,2},{8,12},{10,14},{12,8},{14,10},{16,20},{18,... | collective-permute-start | bytes 2654216 | tf_op jit(solution)/shard_map/ppermute | solution.py:464
  114.4 27.2 %collective-permute-start.11 = (f32[2,2,96,384]{3,2,1,0:T(8,128)}, f32[2,2,96,384]{3,2,1,0:T(8,128)}, u32[]{:S(2)}, u32[]{:S(2)}) collective-permute-start(f32[2,2,96,384]{3,2,1,0:T(8,128)} %get-tuple-element.127.refs_12_), channel_id=1, source_target_pairs={{0,1},{1,0},{2,3},{3,2},{4,5},{5,4},{6,7},{7,6},{8,9},{9,8},{10,11... | collective-permute-start | bytes 1769480 | tf_op jit(solution)/shard_map/ppermute | solution.py:464
  115.9 25.7 %collective-permute-start.12 = (f32[2,2,96,384]{3,2,1,0:T(8,128)}, f32[2,2,96,384]{3,2,1,0:T(8,128)}, u32[]{:S(2)}, u32[]{:S(2)}) collective-permute-start(f32[2,2,96,384]{3,2,1,0:T(8,128)} %get-tuple-element.129.refs_14_), channel_id=1, source_target_pairs={{0,4},{2,6},{4,0},{6,2},{8,12},{10,14},{12,8},{14,10},{16,20},{18,... | collective-permute-start | bytes 1769480 | tf_op jit(solution)/shard_map/ppermute | solution.py:464
  134.7 10.7 %collective-permute-start.18 = (f32[8,48,3072]{2,1,0:T(8,128)}, f32[8,48,3072]{2,1,0:T(8,128)}, u32[]{:S(2)}, u32[]{:S(2)}) collective-permute-start(f32[8,48,3072]{2,1,0:T(8,128)} %get-tuple-element.143), channel_id=1, source_target_pairs={{0,2},{2,0},{4,6},{6,4},{8,10},{10,8},{12,14},{14,12},{16,18},{18,... | collective-permute-start | bytes 14155784 | tf_op jit(solution)/shard_map/ppermute | solution.py:464
  134.8 0.9 copy-start.1
  139.1 15.2 %collective-permute-start.17 = (f32[2,2,24,1152]{3,2,1,0:T(8,128)}, f32[2,2,24,1152]{3,2,1,0:T(8,128)}, u32[]{:S(2)}, u32[]{:S(2)}) collective-permute-start(f32[2,2,24,1152]{3,2,1,0:T(8,128)} %get-tuple-element.135.refs_7_), channel_id=1, source_target_pairs={{0,8},{2,10},{4,12},{6,14},{8,0},{10,2},{12,4},{14,6},{16,24},{18,... | collective-permute-start | bytes 1327112 | tf_op jit(solution)/shard_map/ppermute | solution.py:464
  140.7 19.6 %collective-permute-start.16 = (f32[2,2,24,1920]{3,2,1,0:T(8,128)}, f32[2,2,24,1920]{3,2,1,0:T(8,128)}, u32[]{:S(2)}, u32[]{:S(2)}) collective-permute-start(f32[2,2,24,1920]{3,2,1,0:T(8,128)} %get-tuple-element.133.refs_5_), channel_id=1, source_target_pairs={{0,4},{2,6},{4,0},{6,2},{8,12},{10,14},{12,8},{14,10},{16,20},{18,... | collective-permute-start | bytes 2211848 | tf_op jit(solution)/shard_map/ppermute | solution.py:464
  144.0 29.2 %collective-permute-start.15 = (f32[2,96,768]{2,1,0:T(8,128)}, f32[2,96,768]{2,1,0:T(8,128)}, u32[]{:S(2)}, u32[]{:S(2)}) collective-permute-start(f32[2,96,768]{2,1,0:T(8,128)} %get-tuple-element.138.refs_3_), channel_id=1, source_target_pairs={{0,8},{2,10},{4,12},{6,14},{8,0},{10,2},{12,4},{14,6},{16,24},{18,... | collective-permute-start | bytes 1769480 | tf_op jit(solution)/shard_map/ppermute | solution.py:464
  151.1 39.0 %collective-permute-start.20 = (f32[2,2,2,24,1024]{4,3,2,1,0:T(8,128)}, f32[2,2,2,24,1024]{4,3,2,1,0:T(8,128)S(1)}, u32[]{:S(2)}, u32[]{:S(2)}) collective-permute-start(f32[2,2,2,24,1024]{4,3,2,1,0:T(8,128)} %get-tuple-element.144.refs_5_), channel_id=1, source_target_pairs={{0,4},{2,6},{4,0},{6,2},{8,12},{10,14},{12,8},{14,10},{16,20},{18,... | collective-permute-start | bytes 2359304 | tf_op jit(solution)/shard_map/ppermute | solution.py:464
  152.6 37.5 %collective-permute-start.21 = (f32[2,2,2,24,1024]{4,3,2,1,0:T(8,128)}, f32[2,2,2,24,1024]{4,3,2,1,0:T(8,128)}, u32[]{:S(2)}, u32[]{:S(2)}) collective-permute-start(f32[2,2,2,24,1024]{4,3,2,1,0:T(8,128)} %get-tuple-element.146.refs_7_), channel_id=1, source_target_pairs={{0,1},{1,0},{2,3},{3,2},{4,5},{5,4},{6,7},{7,6},{8,9},{9,8},{10,11... | collective-permute-start | bytes 2359304 | tf_op jit(solution)/shard_map/ppermute | solution.py:464
  154.3 35.8 %collective-permute-start.22 = (f32[2,2,2,24,1024]{4,3,2,1,0:T(8,128)}, f32[2,2,2,24,1024]{4,3,2,1,0:T(8,128)}, u32[]{:S(2)}, u32[]{:S(2)}) collective-permute-start(f32[2,2,2,24,1024]{4,3,2,1,0:T(8,128)} %get-tuple-element.148.refs_9_), channel_id=1, source_target_pairs={{0,8},{2,10},{4,12},{6,14},{8,0},{10,2},{12,4},{14,6},{16,24},{18,... | collective-permute-start | bytes 2359304 | tf_op jit(solution)/shard_map/ppermute | solution.py:464
  162.8 25.2 %collective-permute-start.23 = (f32[2,24,3072]{2,1,0:T(8,128)}, f32[2,24,3072]{2,1,0:T(8,128)}, u32[]{:S(2)}, u32[]{:S(2)}) collective-permute-start(f32[2,24,3072]{2,1,0:T(8,128)} %get-tuple-element.150.refs_9_), channel_id=1, source_target_pairs={{0,1},{1,0},{2,3},{3,2},{4,5},{5,4},{6,7},{7,6},{8,9},{9,8},{10,11... | collective-permute-start | bytes 1769480 | tf_op jit(solution)/shard_map/ppermute | solution.py:464
  175.5 23.4 %collective-permute-start.19 = (f32[96,1280]{1,0:T(8,128)}, f32[96,1280]{1,0:T(8,128)}, u32[]{:S(2)}, u32[]{:S(2)}) collective-permute-start(f32[96,1280]{1,0:T(8,128)} %get-tuple-element.154.refs_4_), channel_id=1, source_target_pairs={{0,16},{2,18},{4,20},{6,22},{8,24},{10,26},{12,28},{14,30},{16,0},... | collective-permute-start | bytes 1474568 | tf_op jit(solution)/shard_map/ppermute | solution.py:464
  190.1 0.9 copy-start.2
  194.5 12.1 %collective-permute-start.25 = (f32[2,2,24,1024]{3,2,1,0:T(8,128)}, f32[2,2,24,1024]{3,2,1,0:T(8,128)S(1)}, u32[]{:S(2)}, u32[]{:S(2)}) collective-permute-start(f32[2,2,24,1024]{3,2,1,0:T(8,128)} %get-tuple-element.158.refs_2_), channel_id=1, source_target_pairs={{0,1},{1,0},{2,3},{3,2},{4,5},{5,4},{6,7},{7,6},{8,9},{9,8},{10,11... | collective-permute-start | bytes 1179656 | tf_op jit(solution)/shard_map/ppermute | solution.py:464
  196.1 12.4 %collective-permute-start.26 = (f32[2,2,24,1024]{3,2,1,0:T(8,128)}, f32[2,2,24,1024]{3,2,1,0:T(8,128)}, u32[]{:S(2)}, u32[]{:S(2)}) collective-permute-start(f32[2,2,24,1024]{3,2,1,0:T(8,128)} %get-tuple-element.160.refs_4_), channel_id=1, source_target_pairs={{0,8},{2,10},{4,12},{6,14},{8,0},{10,2},{12,4},{14,6},{16,24},{18,... | collective-permute-start | bytes 1179656 | tf_op jit(solution)/shard_map/ppermute | solution.py:464
  200.9 14.8 %collective-permute-start.24 = (f32[96,1280]{1,0:T(8,128)}, f32[96,1280]{1,0:T(8,128)S(1)}, u32[]{:S(2)}, u32[]{:S(2)}) collective-permute-start(f32[96,1280]{1,0:T(8,128)} %shard_map.325.refs_7_.refs_1_), channel_id=1, source_target_pairs={{0,1},{1,0},{2,3},{3,2},{4,5},{5,4},{6,7},{7,6},{8,9},{9,8},{10,11... | collective-permute-start | bytes 1474568 | tf_op jit(solution)/shard_map/ppermute | solution.py:464
  202.4 8.4 %collective-permute-start.27 = (f32[2,2,24,1024]{3,2,1,0:T(8,128)}, f32[2,2,24,1024]{3,2,1,0:T(8,128)}, u32[]{:S(2)}, u32[]{:S(2)}) collective-permute-start(f32[2,2,24,1024]{3,2,1,0:T(8,128)} %get-tuple-element.162.refs_6_), channel_id=1, source_target_pairs={{0,4},{2,6},{4,0},{6,2},{8,12},{10,14},{12,8},{14,10},{16,20},{18,... | collective-permute-start | bytes 1179656 | tf_op jit(solution)/shard_map/ppermute | solution.py:464
  203.3 15.8 %collective-permute-start.32 = (f32[24,3072]{1,0:T(8,128)}, f32[24,3072]{1,0:T(8,128)}, u32[]{:S(2)}, u32[]{:S(2)}) collective-permute-start(f32[24,3072]{1,0:T(8,128)} %get-tuple-element.156.refs_7_), channel_id=1, source_target_pairs={{0,16},{2,18},{4,20},{6,22},{8,24},{10,26},{12,28},{14,30},{16,0},... | collective-permute-start | bytes 884744 | tf_op jit(solution)/shard_map/ppermute | solution.py:464
  206.6 4.3 %copy-start.4 = (f32[2,2,24,1024]{3,2,1,0:T(8,128)}, f32[2,2,24,1024]{3,2,1,0:T(8,128)S(1)}, u32[]{:S(2)}) copy-start(f32[2,2,24,1024]{3,2,1,0:T(8,128)S(1)} %collective-permute-done.25.refs_2_) | copy-start | bytes 1179652
  213.5 7.4 %collective-permute-start.29 = (f32[2,24,1024]{2,1,0:T(8,128)}, f32[2,24,1024]{2,1,0:T(8,128)S(1)}, u32[]{:S(2)}, u32[]{:S(2)}) collective-permute-start(f32[2,24,1024]{2,1,0:T(8,128)} %get-tuple-element.164.refs_3_), channel_id=1, source_target_pairs={{0,8},{2,10},{4,12},{6,14},{8,0},{10,2},{12,4},{14,6},{16,24},{18,... | collective-permute-start | bytes 589832 | tf_op jit(solution)/shard_map/ppermute | solution.py:464
  213.6 7.3 %collective-permute-start.30 = (f32[2,24,1024]{2,1,0:T(8,128)}, f32[2,24,1024]{2,1,0:T(8,128)}, u32[]{:S(2)}, u32[]{:S(2)}) collective-permute-start(f32[2,24,1024]{2,1,0:T(8,128)} %get-tuple-element.166.refs_5_), channel_id=1, source_target_pairs={{0,4},{2,6},{4,0},{6,2},{8,12},{10,14},{12,8},{14,10},{16,20},{18,... | collective-permute-start | bytes 589832 | tf_op jit(solution)/shard_map/ppermute | solution.py:464
  214.5 6.4 %collective-permute-start.31 = (f32[2,24,1024]{2,1,0:T(8,128)}, f32[2,24,1024]{2,1,0:T(8,128)}, u32[]{:S(2)}, u32[]{:S(2)}) collective-permute-start(f32[2,24,1024]{2,1,0:T(8,128)} %get-tuple-element.168.refs_7_), channel_id=1, source_target_pairs={{0,1},{1,0},{2,3},{3,2},{4,5},{5,4},{6,7},{7,6},{8,9},{9,8},{10,11... | collective-permute-start | bytes 589832 | tf_op jit(solution)/shard_map/ppermute | solution.py:464
  215.7 0.8 copy-start.3
  218.6 8.4 %collective-permute-start.28 = (f32[192,256]{1,0:T(8,128)}, f32[192,256]{1,0:T(8,128)S(1)}, u32[]{:S(2)}, u32[]{:S(2)}) collective-permute-start(f32[192,256]{1,0:T(8,128)} %get-tuple-element.170.refs_0_), channel_id=1, source_target_pairs={{0,4},{2,6},{4,0},{6,2},{8,12},{10,14},{12,8},{14,10},{16,20},{18,... | collective-permute-start | bytes 589832 | tf_op jit(solution)/shard_map/ppermute | solution.py:464
  220.8 8.6 %copy-start = (f32[24,3072]{1,0:T(8,128)S(1)}, f32[24,3072]{1,0:T(8,128)}, u32[]{:S(2)}) copy-start(f32[24,3072]{1,0:T(8,128)} %shard_map.328.refs_7_.refs_1_) | copy-start | bytes 884740
  220.9 0.7 copy-start.9
  223.7 17.7 %collective-permute-start.36 = (f32[24,3072]{1,0:T(8,128)}, f32[24,3072]{1,0:T(8,128)S(1)}, u32[]{:S(2)}, u32[]{:S(2)}) collective-permute-start(f32[24,3072]{1,0:T(8,128)} %get-tuple-element.172.refs_2_), channel_id=1, source_target_pairs={{0,16},{2,18},{4,20},{6,22},{8,24},{10,26},{12,28},{14,30},{16,0},... | collective-permute-start | bytes 884744 | tf_op jit(solution)/shard_map/ppermute | solution.py:464
  226.9 0.7 copy-start.8
  229.3 10.4 %collective-permute-start.33 = (f32[192,256]{1,0:T(8,128)}, f32[192,256]{1,0:T(8,128)}, u32[]{:S(2)}, u32[]{:S(2)}) collective-permute-start(f32[192,256]{1,0:T(8,128)} %shard_map.330.refs_0_.refs_2_), channel_id=1, source_target_pairs={{0,8},{2,10},{4,12},{6,14},{8,0},{10,2},{12,4},{14,6},{16,24},{18,... | collective-permute-start | bytes 589832 | tf_op jit(solution)/shard_map/ppermute | solution.py:464
  229.4 15.1 %collective-permute-start.35 = (f32[24,3072]{1,0:T(8,128)S(1)}, f32[24,3072]{1,0:T(8,128)S(1)}, u32[]{:S(2)}, u32[]{:S(2)}) collective-permute-start(f32[24,3072]{1,0:T(8,128)S(1)} %copy-done), channel_id=1, source_target_pairs={{0,1},{1,0},{2,3},{3,2},{4,5},{5,4},{6,7},{7,6},{8,9},{9,8},{10,11... | collective-permute-start | bytes 884744 | tf_op jit(solution)/shard_map/ppermute | solution.py:464
  241.4 0.7 copy-start.6
  243.9 6.9 %collective-permute-start.37 = (f32[24,3072]{1,0:T(8,128)}, f32[24,3072]{1,0:T(8,128)S(1)}, u32[]{:S(2)}, u32[]{:S(2)}) collective-permute-start(f32[24,3072]{1,0:T(8,128)} %shard_map.332.refs_3_.refs_1_), channel_id=1, source_target_pairs={{0,1},{1,0},{2,3},{3,2},{4,5},{5,4},{6,7},{7,6},{8,9},{9,8},{10,11... | collective-permute-start | bytes 884744 | tf_op jit(solution)/shard_map/ppermute | solution.py:464
  244.6 2.6 %collective-permute-start.34 = (f32[192,256]{1,0:T(8,128)}, f32[192,256]{1,0:T(8,128)}, u32[]{:S(2)}, u32[]{:S(2)}) collective-permute-start(f32[192,256]{1,0:T(8,128)} %shard_map.331.refs_2_.refs_0_), channel_id=1, source_target_pairs={{0,2},{2,0},{4,6},{6,4},{8,10},{10,8},{12,14},{14,12},{16,18},{18,... | collective-permute-start | bytes 589832 | tf_op jit(solution)/shard_map/ppermute | solution.py:464
  244.6 0.7 copy-start.7
  250.9 0.7 copy-start.5

commit v5 on v4

--- a/solution.py
+++ b/solution.py
@@ -19,7 +19,7 @@
 OUTPUTS = ("block_out", "grad_patches", "gain1", "bias1", "table", "sum_qkv", "query", "value")
 OUTPUTS += ("sum_out", "out", "gain2", "bias2", "sum_up", "up", "sum_down", "down")
 COSTS = {"D3": 100, "DO": 30, "A1": 2}
-VMEM_BYTES = 63 * 1024 * 1024
+VMEM_BYTES = 255 * 256 * 1024
 
 
 norm_epsilon = 1e-05
@@ -185,7 +185,7 @@
         out = out.astype(jnp.bfloat16)
         activated[at, :] = out
         slope[at, :] = steep.astype(jnp.bfloat16)
-    store_halves(dot_tn(activated[...], grad_down[...]), here[0], keep, send)
+    store_halves(dot_tn(activated[...], grad_down[...]), here[CORE], keep, send)
 
 
 def mlp_back_kernel(
@@ -200,7 +200,7 @@
     grad_act = dot_nt(grad_down[...], w_down[...])
     grad_up = (grad_act * slope[...].astype(jnp.float32)).astype(jnp.bfloat16)
     grad_bias_up[0] = column_sum(grad_up.astype(jnp.float32))
-    store_halves(dot_nn(turned[...], grad_up), here[0], keep, send)
+    store_halves(dot_nn(turned[...], grad_up), here[CORE], keep, send)
     grad_normed2[...] += dot_nt(grad_up, w_up[...])
 
 
@@ -330,7 +330,7 @@
 
     @pl.when(window == pl.num_programs(0) - 1)
     def _():
-        store_halves(grad_w[...], here[0], keep, send)
+        store_halves(grad_w[...], here[CORE], keep, send)
 
 
 def norm_back_kernel(
@@ -379,7 +379,7 @@
     block_out[0] = final.astype(jnp.bfloat16)
 
 
-Z1, Z0, X, Y = range(4)
+Z1, Z0, X, Y, CORE = range(5)
 LINKS = (("dp", 3), ("dp", 2), ("dp", 1), ("outer", 0))
 
 
@@ -602,9 +602,9 @@
     rounds = count_rounds(jnp.sum(onehot * live[:, None].astype(f32), axis=0))
     counted = next(rounds)
 
-    dp_at, outer_at = lax.axis_index("dp"), lax.axis_index("outer")
-    here = lax.rem(dp_at, 2).reshape(1)
-    bits = jnp.stack([bit_of("dp", 3), bit_of("dp", 2), bit_of("dp", 1), outer_at])
+    outer_at = lax.axis_index("outer")
+    bits = jnp.stack([bit_of("dp", b) for b in (3, 2, 1)] + [outer_at, bit_of("dp", 0)])
+    here = bits
     def flat(vector):
         return whole(*vector.shape), vector
 

time: 254 us -> 251 us (0.988)
  local copies, waits for them, and re-layouts: 6.03 us -> 2.7 us
  starting transfers between devices: 40.7 us -> 43.4 us
    unnamed x26 -> x12, local copies, waits for them, and re-layouts: 6.03 us -> 2.04 us
    ppermute x31, starting transfers between devices: 31.3 us -> 33.9 us  [swap(): return lax.ppermute(values, axis, [(i, i ^ 1 << bit) for i in range(size)])]
  transfers between devices with their start and end apart: 38 -> 38, of which waited for: 10 -> 11; matrix products, arithmetic and copies ran while one was open for 0% -> 0% of each run, Pallas kernels for 60% -> 61%
where the time goes in v5:
time: 251 us; the launch traced here: 250 us
  Pallas kernels  173 us (69%)
  starting transfers between devices  43.4 us (17%)
  waiting for transfers between devices  26.9 us (11%)
  other arithmetic  2.78 us (1%)
  local copies, waits for them, and re-layouts  2.7 us (1%)
    pallas_call x30, Pallas kernels, call(): pl.pallas_call(body, grid=grid, in_specs=[spec for spec, _ in inputs] + [...  173 us
    ppermute x31, starting transfers between devices, swap(): return lax.ppermute(values, axis, [(i, i ^ 1 << bit) for i in range(size)])  33.9 us
    ppermute x31, waiting for transfers between devices, swap(): return lax.ppermute(values, axis, [(i, i ^ 1 << bit) for i in range(size)])  26.8 us
    ppermute x7, starting transfers between devices, exchange(): lax.ppermute(values, ('dp', 'outer'), [(i, i ^ flip) for i in range(size)])  9.45 us
  transfers between devices with their start and end apart: 38, of which 11 were waited for; matrix products, arithmetic and copies ran while one was open for 0% of the time, Pallas kernels for 61%

profile of v5, /device:TPU:0, one launch (start us, length us, event | category | flops | bytes accessed | tf_op | source)
XLA Modules:
  0.0 250.3 jit_solution(9973148226291321543)
XLA Ops:
  1.3 0.7 select_reduce_fusion.1
  2.5 0.7 stack.23.refs_2_.refs_0_.refs_1_
  3.4 3.8 %collective-permute-start.3 = (f32[40]{0:T(128)S(1)}, f32[40]{0:T(128)S(1)}, u32[]{:S(2)}, u32[]{:S(2)}) collective-permute-start(f32[40]{0:T(128)S(1)} %add.21.refs_8_), channel_id=1, source_target_pairs={{0,12},{1,13},{2,14},{3,15},{4,8},{5,9},{6,10},{7,11},{8,4},{9,5},... | collective-permute-start | bytes 488 | tf_op jit(solution)/shard_map/ppermute | solution.py:479
  7.8 8.7 %shard_map.306 = (bf16[1024,768]{1,0:T(8,128)(2,1)}, bf16[1024,2304]{1,0:T(8,128)(2,1)}) custom-call(s32[4]{0:T(128)} %refs_0_.13, bf16[4,256,768]{2,1,0:T(8,128)(2,1)} %refs_1_.6, f32[768]{0:T(1024)} %refs_5_.9, f32[768]{0:T(1024)} %refs_3_.4, f32[768]{0:T(1024)} %refs_4_.4, f32[768]{0:T(1024)} %refs_5_.5, f32[40,768]{1,0:T(8,128)} %refs_6_.3, ...), custom_call_target="tpu_custom_call" | custom-call | tf_op jit(solution)/shard_map/pallas_call | solution.py:583
  17.2 3.9 %collective-permute-start.6 = (f32[40]{0:T(128)S(1)}, f32[40]{0:T(128)S(1)}, u32[]{:S(2)}, u32[]{:S(2)}) collective-permute-start(f32[40]{0:T(128)S(1)} %add_add_fusion.1.refs_7_), channel_id=1, source_target_pairs={{0,17},{1,16},{2,19},{3,18},{4,21},{5,20},{6,23},{7,22},{8,25},{9,... | collective-permute-start | bytes 488 | tf_op jit(solution)/shard_map/ppermute | solution.py:479
  21.7 11.8 %shard_map.307 = (bf16[1024,768]{1,0:T(8,128)(2,1)}, f32[1024,768]{1,0:T(8,128)}, bf16[1024,768]{1,0:T(8,128)(2,1)}, bf16[768,1024]{1,0:T(8,128)(2,1)}, f32[4,16,256]{2,1,0:T(8,128)}) custom-call(s32[4]{0:T(128)} %refs_0_.12, bf16[4,256,768]{2,1,0:T(8,128)(2,1)} %refs_1_.6, bf16[1024,2304]{1,0:T(8,128)(2,1)} %get-tuple-element.101.refs_2_.refs_1_.refs_3_.refs_4_, ...), custom_call_target="tpu_custom_call" | custom-call | tf_op jit(solution)/shard_map/pallas_call | solution.py:583
  34.9 18.1 %shard_map.308 = (bf16[1024,3072]{1,0:T(8,128)(2,1)}, bf16[1024,3072]{1,0:T(8,128)(2,1)}, bf16[1024,768]{1,0:T(8,128)(2,1)}, f32[8,192,768]{2,1,0:T(8,128)}, f32[8,192,768]{2,1,0:T(8,128)}) custom-call(s32[4]{0:T(128)} %refs_0_.12, f32[4]{0:T(128)} %compare_select_fusion.refs_1_, s32[5]{0:T(128)} %stack.23.refs_2_.refs_0_.refs_1_, ...), custom_call_target="tpu_custom_call" | custom-call | tf_op jit(solution)/shard_map/pallas_call | solution.py:583
  52.9 21.2 %shard_map.309 = (f32[4,1,768]{2,1,0:T(1,128)}, f32[1024,768]{1,0:T(8,128)}, f32[8,48,3072]{2,1,0:T(8,128)}, f32[8,48,3072]{2,1,0:T(8,128)}) custom-call(s32[5]{0:T(128)} %stack.23.refs_2_.refs_0_.refs_1_, bf16[1024,768]{1,0:T(8,128)(2,1)} %get-tuple-element.107.refs_1_, bf16[1024,3072]{1,0:T(8,128)(2,1)} %get-tuple-element.108.refs_2_, ...), custom_call_target="tpu_custom_call" | custom-call | tf_op jit(solution)/shard_map/pallas_call | solution.py:583
  74.7 5.8 %shard_map.310 = (f32[2,2,2,96,384]{4,3,2,1,0:T(8,128)}, f32[2,2,2,96,384]{4,3,2,1,0:T(8,128)}, f32[2,2,2,96,384]{4,3,2,1,0:T(8,128)}, f32[2,2,2,96,384]{4,3,2,1,0:T(8,128)}) custom-call(s32[5]{0:T(128)} %stack.23.refs_2_.refs_0_.refs_1_, f32[2,2,2,2,96,768]{5,4,3,2,1,0:T(8,128)} %bitcast.16, f32[2,2,2,2,96,768]{5,4,3,2,1,0:T(8,128)} %bitcast.7.refs_2_, ...), custom_call_target="tpu_custom_call" | custom-call | flops 34500001792 | tf_op jit(solution)/shard_map/pallas_call | solution.py:583
  80.4 1.7 collective-permute-start.8
  82.1 1.5 collective-permute-start.9
  83.7 9.7 %shard_map.311 = (f32[1024,768]{1,0:T(8,128)}, bf16[1024,768]{1,0:T(8,128)(2,1)}, f32[4,16,256]{2,1,0:T(8,128)}, f32[8,768]{1,0:T(8,128)}, bf16[1024,768]{1,0:T(8,128)(2,1)}) custom-call(s32[4]{0:T(128)} %refs_0_.12, f32[4]{0:T(128)} %compare_select_fusion.refs_1_, s32[5]{0:T(128)} %stack.23.refs_2_.refs_0_.refs_1_, bf16[4,256,768]{2,1,0:T(8,128)(2,1)} %refs_3_.7, ...), custom_call_target="tpu_custom_call" | custom-call | tf_op jit(solution)/shard_map/pallas_call | solution.py:583
  93.4 6.0 %shard_map.312 = (f32[2,2,2,24,1920]{4,3,2,1,0:T(8,128)}, f32[2,2,2,24,1920]{4,3,2,1,0:T(8,128)}, f32[2,2,2,24,1152]{4,3,2,1,0:T(8,128)}, f32[2,2,2,24,1152]{4,3,2,1,0:T(8,128)}) custom-call(s32[5]{0:T(128)} %stack.23.refs_2_.refs_0_.refs_1_, f32[2,2,2,2,24,3072]{5,4,3,2,1,0:T(8,128)} %bitcast.15, f32[2,2,2,2,24,3072]{5,4,3,2,1,0:T(8,128)} %bitcast.9.refs_2_, ...), custom_call_target="tpu_custom_call" | custom-call | tf_op jit(solution)/shard_map/pallas_call | solution.py:583
  99.4 1.6 collective-permute-start.13
  101.5 7.3 %shard_map.313.refs_5_.refs_11_ = bf16[1024,1152]{1,0:T(8,128)(2,1)} custom-call(s32[4]{0:T(128)} %refs_0_.12, bf16[1024,2304]{1,0:T(8,128)(2,1)} %get-tuple-element.101.refs_2_.refs_1_.refs_3_.refs_4_, bf16[1024,2304]{1,0:T(8,128)(2,1)} %get-tuple-element.101.refs_2_.refs_1_.refs_3_.refs_4_, ...), custom_call_target="tpu_custom_call" | custom-call | tf_op jit(solution)/shard_map/pallas_call | solution.py:583
  108.8 0.8 collective-permute-done.8.refs_2_
  110.1 3.5 %shard_map.314 = (f32[2,2,96,384]{3,2,1,0:T(8,128)}, f32[2,2,96,384]{3,2,1,0:T(8,128)}, f32[2,2,96,384]{3,2,1,0:T(8,128)}, f32[2,2,96,384]{3,2,1,0:T(8,128)}) custom-call(s32[5]{0:T(128)} %stack.23.refs_2_.refs_0_.refs_1_, f32[2,2,2,96,384]{4,3,2,1,0:T(8,128)} %get-tuple-element.111.refs_10_.refs_1_, f32[2,2,2,96,384]{4,3,2,1,0:T(8,128)} %collective-permute-done.8.refs_2_, ...), custom_call_target="tpu_custom_call" | custom-call | tf_op jit(solution)/shard_map/pallas_call | solution.py:583
  113.5 1.5 collective-permute-start.11
  115.1 1.2 collective-permute-start.12
  116.3 17.6 %shard_map.315 = (bf16[1024,2304]{1,0:T(8,128)(2,1)}, f32[8,768]{1,0:T(8,128)}, f32[8,48,3072]{2,1,0:T(8,128)}, f32[8,48,3072]{2,1,0:T(8,128)}) custom-call(s32[4]{0:T(128)} %refs_0_.12, s32[5]{0:T(128)} %stack.23.refs_2_.refs_0_.refs_1_, bf16[1024,2304]{1,0:T(8,128)(2,1)} %get-tuple-element.101.refs_2_.refs_1_.refs_3_.refs_4_, ...), custom_call_target="tpu_custom_call" | custom-call | flops 2300000000 | tf_op jit(solution)/shard_map/pallas_call | solution.py:583
  134.0 3.4 %shard_map.316 = (f32[2,2,24,1920]{3,2,1,0:T(8,128)}, f32[2,2,24,1920]{3,2,1,0:T(8,128)}, f32[2,2,24,1152]{3,2,1,0:T(8,128)}, f32[2,2,24,1152]{3,2,1,0:T(8,128)}) custom-call(s32[5]{0:T(128)} %stack.23.refs_2_.refs_0_.refs_1_, f32[2,2,2,24,1920]{4,3,2,1,0:T(8,128)} %get-tuple-element.123.refs_8_.refs_1_, ...), custom_call_target="tpu_custom_call" | custom-call | tf_op jit(solution)/shard_map/pallas_call | solution.py:583
  137.5 1.6 collective-permute-start.17
  139.0 0.8 collective-permute-start.16
  140.3 2.5 shard_map.317
  142.7 1.8 collective-permute-start.15
  144.6 5.8 %shard_map.318 = (f32[2,2,2,24,1024]{4,3,2,1,0:T(8,128)}, f32[2,2,2,24,1024]{4,3,2,1,0:T(8,128)}, f32[2,2,2,24,1024]{4,3,2,1,0:T(8,128)}, f32[2,2,2,24,1024]{4,3...) custom-call(s32[5]{0:T(128)} %stack.23.refs_2_.refs_0_.refs_1_, ...), custom_call_target="tpu_custom_call" | custom-call | tf_op jit(solution)/shard_map/pallas_call | solution.py:583
  150.3 1.5 collective-permute-start.20
  151.8 2.4 collective-permute-start.21
  154.2 4.4 %collective-permute-done.16.refs_2_ = f32[2,2,24,1920]{3,2,1,0:T(8,128)} collective-permute-done((f32[2,2,24,1920]{3,2,1,0:T(8,128)}, f32[2,2,24,1920]{3,2,1,0:T(8,128)}, u32[]{:S(2)}, u32[]{:S(2)}) %collective-permute-start.16) | collective-permute-done | bytes 737312 | tf_op jit(solution)/shard_map/ppermute | solution.py:464
  158.7 2.5 shard_map.319
  161.7 9.8 %shard_map.320 = (bf16[4,256,768]{2,1,0:T(8,128)(2,1)}, f32[192,256]{1,0:T(8,128)}) custom-call(s32[4]{0:T(128)} %refs_0_.13, bf16[4,256,768]{2,1,0:T(8,128)(2,1)} %refs_1_.6, f32[1024,768]{1,0:T(8,128)} %get-tuple-element.121.refs_3_.refs_2_, bf16[1024,2304]{1,0:T(8,128)(2,1)} %get-tuple-element.132.refs_5_.refs_3_, bf16[768,2304]{1,0:T(8,128)(2,1)} %refs_4_.7, ...), custom_call_target="tpu_custom_call" | custom-call | tf_op jit(solution)/shard_map/pallas_call | solution.py:583
  171.5 2.3 shard_map.321
  173.9 2.6 %collective-permute-start.19 = (f32[96,1280]{1,0:T(8,128)}, f32[96,1280]{1,0:T(8,128)}, u32[]{:S(2)}, u32[]{:S(2)}) collective-permute-start(f32[96,1280]{1,0:T(8,128)} %get-tuple-element.154.refs_4_), channel_id=1, source_target_pairs={{0,16},{2,18},{4,20},{6,22},{8,24},{10,26},{12,28},{14,30},{16,0},... | collective-permute-start | bytes 1474568 | tf_op jit(solution)/shard_map/ppermute | solution.py:464
  176.5 9.9 %shard_map.322.refs_3_ = bf16[4,256,768]{2,1,0:T(8,128)(2,1)} custom-call(bf16[1024,3072]{1,0:T(8,128)(2,1)} %get-tuple-element.103.refs_0_, bf16[3072,768]{1,0:T(8,128)(2,1)} %refs_1_.7, f32[768]{0:T(1024)} %refs_2_.3, f32[1024,768]{1,0:T(8,128)} %get-tuple-element.104.refs_4_.refs_3_, f32[96,1280]{1,0:T(8,128)} %get-tuple-element.154.refs_4_, ...), custom_call_target="tpu_custom_call" | custom-call | tf_op jit(solution)/shard_map/pallas_call | solution.py:583
  186.4 2.1 shard_map.323
  188.5 3.5 %shard_map.324 = (f32[2,2,24,1024]{3,2,1,0:T(8,128)}, f32[2,2,24,1024]{3,2,1,0:T(8,128)}, f32[2,2,24,1024]{3,2,1,0:T(8,128)}, f32[2,2,24,1024]{3,2,1,0:T(8,128)}...) custom-call(s32[5]{0:T(128)} %stack.23.refs_2_.refs_0_.refs_1_, ...), custom_call_target="tpu_custom_call" | custom-call | tf_op jit(solution)/shard_map/pallas_call | solution.py:583
  192.0 1.6 collective-permute-start.25
  194.0 3.2 %collective-permute-done.19.refs_1_ = f32[96,1280]{1,0:T(8,128)} collective-permute-done((f32[96,1280]{1,0:T(8,128)}, f32[96,1280]{1,0:T(8,128)}, u32[]{:S(2)}, u32[]{:S(2)}) %collective-permute-start.19) | collective-permute-done | bytes 491552 | tf_op jit(solution)/shard_map/ppermute | solution.py:464
  197.2 2.0 shard_map.325.refs_7_.refs_1_
  199.3 1.5 collective-permute-start.24
  200.8 0.8 collective-permute-start.27
  201.6 1.8 collective-permute-done.25.refs_2_
  203.4 3.1 %collective-permute-done.26.refs_4_ = f32[2,2,24,1024]{3,2,1,0:T(8,128)} collective-permute-done((f32[2,2,24,1024]{3,2,1,0:T(8,128)}, f32[2,2,24,1024]{3,2,1,0:T(8,128)}, u32[]{:S(2)}, u32[]{:S(2)}) %collective-permute-start.26) | collective-permute-done | bytes 393248 | tf_op jit(solution)/shard_map/ppermute | solution.py:464
  206.4 2.8 %collective-permute-done.27.refs_6_ = f32[2,2,24,1024]{3,2,1,0:T(8,128)} collective-permute-done((f32[2,2,24,1024]{3,2,1,0:T(8,128)}, f32[2,2,24,1024]{3,2,1,0:T(8,128)}, u32[]{:S(2)}, u32[]{:S(2)}) %collective-permute-start.27) | collective-permute-done | bytes 393248 | tf_op jit(solution)/shard_map/ppermute | solution.py:464
  209.2 2.6 %shard_map.326 = (f32[2,24,1024]{2,1,0:T(8,128)}, f32[2,24,1024]{2,1,0:T(8,128)}, f32[2,24,1024]{2,1,0:T(8,128)}, f32[2,24,1024]{2,1,0:T(8,128)}, f32[2,24,1024]{2,1,0:T(8,128)}, /*index=5*/f32[2,24,1024]{2,1,0:T(8,128)}) custom-call(s32[5]{0:T(128)} %stack.23.refs_2_.refs_0_.refs_1_, f32[2,2,24,1024]{3,2,1,0:T(8,128)} %get-tuple-element.159.refs_3_.refs_1_, ...), custom_call_target="tpu_custom_call" | custom-call | tf_op jit(solution)/shard_map/pallas_call | solution.py:583
  211.9 1.1 collective-permute-start.30
  213.1 0.9 collective-permute-start.31
  213.9 2.1 shard_map.327
  216.0 1.8 collective-permute-start.28
  217.8 1.8 shard_map.328.refs_7_.refs_1_
  219.6 2.2 shard_map.329
  221.9 3.5 %collective-permute-start.36 = (f32[24,3072]{1,0:T(8,128)}, f32[24,3072]{1,0:T(8,128)}, u32[]{:S(2)}, u32[]{:S(2)}) collective-permute-start(f32[24,3072]{1,0:T(8,128)} %get-tuple-element.172.refs_2_), channel_id=1, source_target_pairs={{0,16},{2,18},{4,20},{6,22},{8,24},{10,26},{12,28},{14,30},{16,0},... | collective-permute-start | bytes 884744 | tf_op jit(solution)/shard_map/ppermute | solution.py:464
  225.4 0.7 copy-done
  226.1 1.7 shard_map.330.refs_0_.refs_2_
  228.0 1.3 collective-permute-start.35
  229.3 7.8 %collective-permute-done.33.refs_1_ = f32[192,256]{1,0:T(8,128)S(1)} collective-permute-done((f32[192,256]{1,0:T(8,128)}, f32[192,256]{1,0:T(8,128)S(1)}, u32[]{:S(2)}, u32[]{:S(2)}) %collective-permute-start.33) | collective-permute-done | bytes 196640 | tf_op jit(solution)/shard_map/ppermute | solution.py:464
  237.8 1.7 shard_map.331.refs_2_.refs_0_
  239.5 1.8 shard_map.332.refs_3_.refs_1_
  241.3 0.7 collective-permute-start.37
  242.1 1.9 shard_map.333.refs_2_
  244.0 0.7 copy-done.2
  244.7 1.7 shard_map.334
  246.4 2.0 collective-permute-done.37.refs_2_
  248.4 1.9 shard_map.335
  (62 shorter events, 8.0 us)
Async XLA Ops:
  2.0 1.3 collective-permute-start
  3.4 4.4 %copy-start.5 = (f32[40]{0:T(128)}, f32[40]{0:T(128)S(1)}, u32[]{:S(2)}) copy-start(f32[40]{0:T(128)S(1)} %add.21.refs_8_) | copy-start | bytes 484
  3.4 13.1 %collective-permute-start.3 = (f32[40]{0:T(128)S(1)}, f32[40]{0:T(128)S(1)}, u32[]{:S(2)}, u32[]{:S(2)}) collective-permute-start(f32[40]{0:T(128)S(1)} %add.21.refs_8_), channel_id=1, source_target_pairs={{0,12},{1,13},{2,14},{3,15},{4,8},{5,9},{6,10},{7,11},{8,4},{9,5},... | collective-permute-start | bytes 488 | tf_op jit(solution)/shard_map/ppermute | solution.py:479
  7.2 9.3 %collective-permute-start.2 = (f32[40]{0:T(128)S(1)}, f32[40]{0:T(128)S(1)}, u32[]{:S(2)}, u32[]{:S(2)}) collective-permute-start(f32[40]{0:T(128)S(1)} %add.21.refs_8_), channel_id=1, source_target_pairs={{0,8},{1,9},{2,10},{3,11},{4,12},{5,13},{6,14},{7,15},{8,0},{9,1},... | collective-permute-start | bytes 488 | tf_op jit(solution)/shard_map/ppermute | solution.py:479
  7.6 8.9 %collective-permute-start.1 = (f32[40]{0:T(128)S(1)}, f32[40]{0:T(128)S(1)}, u32[]{:S(2)}, u32[]{:S(2)}) collective-permute-start(f32[40]{0:T(128)S(1)} %add.21.refs_8_), channel_id=1, source_target_pairs={{0,4},{1,5},{2,6},{3,7},{4,0},{5,1},{6,2},{7,3},{8,12},{9,13},{10,... | collective-permute-start | bytes 488 | tf_op jit(solution)/shard_map/ppermute | solution.py:479
  17.2 4.5 %copy-start.3 = (f32[40]{0:T(128)}, f32[40]{0:T(128)S(1)}, u32[]{:S(2)}) copy-start(f32[40]{0:T(128)S(1)} %add_add_fusion.1.refs_7_) | copy-start | bytes 484
  17.2 16.3 %collective-permute-start.6 = (f32[40]{0:T(128)S(1)}, f32[40]{0:T(128)S(1)}, u32[]{:S(2)}, u32[]{:S(2)}) collective-permute-start(f32[40]{0:T(128)S(1)} %add_add_fusion.1.refs_7_), channel_id=1, source_target_pairs={{0,17},{1,16},{2,19},{3,18},{4,21},{5,20},{6,23},{7,22},{8,25},{9,... | collective-permute-start | bytes 488 | tf_op jit(solution)/shard_map/ppermute | solution.py:479
  21.1 12.4 %collective-permute-start.5 = (f32[40]{0:T(128)S(1)}, f32[40]{0:T(128)S(1)}, u32[]{:S(2)}, u32[]{:S(2)}) collective-permute-start(f32[40]{0:T(128)S(1)} %add_add_fusion.1.refs_7_), channel_id=1, source_target_pairs={{0,1},{1,0},{2,3},{3,2},{4,5},{5,4},{6,7},{7,6},{8,9},{9,8},{10,11... | collective-permute-start | bytes 488 | tf_op jit(solution)/shard_map/ppermute | solution.py:479
  21.6 11.9 %collective-permute-start.4 = (f32[40]{0:T(128)S(1)}, f32[40]{0:T(128)S(1)}, u32[]{:S(2)}, u32[]{:S(2)}) collective-permute-start(f32[40]{0:T(128)S(1)} %add_add_fusion.1.refs_7_), channel_id=1, source_target_pairs={{0,16},{1,17},{2,18},{3,19},{4,20},{5,21},{6,22},{7,23},{8,24},{9,... | collective-permute-start | bytes 488 | tf_op jit(solution)/shard_map/ppermute | solution.py:479
  21.7 12.5 %copy-start.4 = (s32[4]{0:T(128)S(1)}, s32[4]{0:T(128)}, u32[]{:S(2)}) copy-start(s32[4]{0:T(128)} %refs_0_.13) | copy-start | bytes 52
  52.9 21.7 %collective-permute-start.7 = (f32[8,192,768]{2,1,0:T(8,128)}, f32[8,192,768]{2,1,0:T(8,128)}, u32[]{:S(2)}, u32[]{:S(2)}) collective-permute-start(f32[8,192,768]{2,1,0:T(8,128)} %get-tuple-element.106), channel_id=1, source_target_pairs={{0,2},{2,0},{4,6},{6,4},{8,10},{10,8},{12,14},{14,12},{16,18},{18,... | collective-permute-start | bytes 14155784 | tf_op jit(solution)/shard_map/ppermute | solution.py:464
  74.1 19.3 %collective-permute-start.10 = (f32[8,48,3072]{2,1,0:T(8,128)}, f32[8,48,3072]{2,1,0:T(8,128)}, u32[]{:S(2)}, u32[]{:S(2)}) collective-permute-start(f32[8,48,3072]{2,1,0:T(8,128)} %get-tuple-element.120), channel_id=1, source_target_pairs={{0,2},{2,0},{4,6},{6,4},{8,10},{10,8},{12,14},{14,12},{16,18},{18,... | collective-permute-start | bytes 14155784 | tf_op jit(solution)/shard_map/ppermute | solution.py:464
  80.4 29.1 %collective-permute-start.8 = (f32[2,2,2,96,384]{4,3,2,1,0:T(8,128)}, f32[2,2,2,96,384]{4,3,2,1,0:T(8,128)}, u32[]{:S(2)}, u32[]{:S(2)}) collective-permute-start(f32[2,2,2,96,384]{4,3,2,1,0:T(8,128)} %get-tuple-element.112.refs_9_), channel_id=1, source_target_pairs={{0,4},{2,6},{4,0},{6,2},{8,12},{10,14},{12,8},{14,10},{16,20},{18,... | collective-permute-start | bytes 3538952 | tf_op jit(solution)/shard_map/ppermute | solution.py:464
  82.1 27.9 %collective-permute-start.9 = (f32[2,2,2,96,384]{4,3,2,1,0:T(8,128)}, f32[2,2,2,96,384]{4,3,2,1,0:T(8,128)}, u32[]{:S(2)}, u32[]{:S(2)}) collective-permute-start(f32[2,2,2,96,384]{4,3,2,1,0:T(8,128)} %get-tuple-element.114.refs_11_), channel_id=1, source_target_pairs={{0,1},{1,0},{2,3},{3,2},{4,5},{5,4},{6,7},{7,6},{8,9},{9,8},{10,11... | collective-permute-start | bytes 3538952 | tf_op jit(solution)/shard_map/ppermute | solution.py:464
  99.4 34.6 %collective-permute-start.13 = (f32[2,2,2,24,1920]{4,3,2,1,0:T(8,128)}, f32[2,2,2,24,1920]{4,3,2,1,0:T(8,128)}, u32[]{:S(2)}, u32[]{:S(2)}) collective-permute-start(f32[2,2,2,24,1920]{4,3,2,1,0:T(8,128)} %get-tuple-element.122.refs_7_), channel_id=1, source_target_pairs={{0,8},{2,10},{4,12},{6,14},{8,0},{10,2},{12,4},{14,6},{16,24},{18,... | collective-permute-start | bytes 4423688 | tf_op jit(solution)/shard_map/ppermute | solution.py:464
  101.0 33.0 %collective-permute-start.14 = (f32[2,2,2,24,1152]{4,3,2,1,0:T(8,128)}, f32[2,2,2,24,1152]{4,3,2,1,0:T(8,128)}, u32[]{:S(2)}, u32[]{:S(2)}) collective-permute-start(f32[2,2,2,24,1152]{4,3,2,1,0:T(8,128)} %get-tuple-element.124.refs_9_), channel_id=1, source_target_pairs={{0,4},{2,6},{4,0},{6,2},{8,12},{10,14},{12,8},{14,10},{16,20},{18,... | collective-permute-start | bytes 2654216 | tf_op jit(solution)/shard_map/ppermute | solution.py:464
  113.5 26.3 %collective-permute-start.11 = (f32[2,2,96,384]{3,2,1,0:T(8,128)}, f32[2,2,96,384]{3,2,1,0:T(8,128)}, u32[]{:S(2)}, u32[]{:S(2)}) collective-permute-start(f32[2,2,96,384]{3,2,1,0:T(8,128)} %get-tuple-element.127.refs_12_), channel_id=1, source_target_pairs={{0,1},{1,0},{2,3},{3,2},{4,5},{5,4},{6,7},{7,6},{8,9},{9,8},{10,11... | collective-permute-start | bytes 1769480 | tf_op jit(solution)/shard_map/ppermute | solution.py:464
  115.1 25.2 %collective-permute-start.12 = (f32[2,2,96,384]{3,2,1,0:T(8,128)}, f32[2,2,96,384]{3,2,1,0:T(8,128)}, u32[]{:S(2)}, u32[]{:S(2)}) collective-permute-start(f32[2,2,96,384]{3,2,1,0:T(8,128)} %get-tuple-element.129.refs_14_), channel_id=1, source_target_pairs={{0,4},{2,6},{4,0},{6,2},{8,12},{10,14},{12,8},{14,10},{16,20},{18,... | collective-permute-start | bytes 1769480 | tf_op jit(solution)/shard_map/ppermute | solution.py:464
  133.9 10.6 %collective-permute-start.18 = (f32[8,48,3072]{2,1,0:T(8,128)}, f32[8,48,3072]{2,1,0:T(8,128)}, u32[]{:S(2)}, u32[]{:S(2)}) collective-permute-start(f32[8,48,3072]{2,1,0:T(8,128)} %get-tuple-element.143), channel_id=1, source_target_pairs={{0,2},{2,0},{4,6},{6,4},{8,10},{10,8},{12,14},{14,12},{16,18},{18,... | collective-permute-start | bytes 14155784 | tf_op jit(solution)/shard_map/ppermute | solution.py:464
  137.5 16.8 %collective-permute-start.17 = (f32[2,2,24,1152]{3,2,1,0:T(8,128)}, f32[2,2,24,1152]{3,2,1,0:T(8,128)}, u32[]{:S(2)}, u32[]{:S(2)}) collective-permute-start(f32[2,2,24,1152]{3,2,1,0:T(8,128)} %get-tuple-element.135.refs_7_), channel_id=1, source_target_pairs={{0,8},{2,10},{4,12},{6,14},{8,0},{10,2},{12,4},{14,6},{16,24},{18,... | collective-permute-start | bytes 1327112 | tf_op jit(solution)/shard_map/ppermute | solution.py:464
  139.0 19.6 %collective-permute-start.16 = (f32[2,2,24,1920]{3,2,1,0:T(8,128)}, f32[2,2,24,1920]{3,2,1,0:T(8,128)}, u32[]{:S(2)}, u32[]{:S(2)}) collective-permute-start(f32[2,2,24,1920]{3,2,1,0:T(8,128)} %get-tuple-element.133.refs_5_), channel_id=1, source_target_pairs={{0,4},{2,6},{4,0},{6,2},{8,12},{10,14},{12,8},{14,10},{16,20},{18,... | collective-permute-start | bytes 2211848 | tf_op jit(solution)/shard_map/ppermute | solution.py:464
  142.7 28.8 %collective-permute-start.15 = (f32[2,96,768]{2,1,0:T(8,128)}, f32[2,96,768]{2,1,0:T(8,128)}, u32[]{:S(2)}, u32[]{:S(2)}) collective-permute-start(f32[2,96,768]{2,1,0:T(8,128)} %get-tuple-element.138.refs_3_), channel_id=1, source_target_pairs={{0,8},{2,10},{4,12},{6,14},{8,0},{10,2},{12,4},{14,6},{16,24},{18,... | collective-permute-start | bytes 1769480 | tf_op jit(solution)/shard_map/ppermute | solution.py:464
  150.3 38.2 %collective-permute-start.20 = (f32[2,2,2,24,1024]{4,3,2,1,0:T(8,128)}, f32[2,2,2,24,1024]{4,3,2,1,0:T(8,128)}, u32[]{:S(2)}, u32[]{:S(2)}) collective-permute-start(f32[2,2,2,24,1024]{4,3,2,1,0:T(8,128)} %get-tuple-element.144.refs_5_), channel_id=1, source_target_pairs={{0,4},{2,6},{4,0},{6,2},{8,12},{10,14},{12,8},{14,10},{16,20},{18,... | collective-permute-start | bytes 2359304 | tf_op jit(solution)/shard_map/ppermute | solution.py:464
  151.8 36.7 %collective-permute-start.21 = (f32[2,2,2,24,1024]{4,3,2,1,0:T(8,128)}, f32[2,2,2,24,1024]{4,3,2,1,0:T(8,128)}, u32[]{:S(2)}, u32[]{:S(2)}) collective-permute-start(f32[2,2,2,24,1024]{4,3,2,1,0:T(8,128)} %get-tuple-element.146.refs_7_), channel_id=1, source_target_pairs={{0,1},{1,0},{2,3},{3,2},{4,5},{5,4},{6,7},{7,6},{8,9},{9,8},{10,11... | collective-permute-start | bytes 2359304 | tf_op jit(solution)/shard_map/ppermute | solution.py:464
  154.2 34.3 %collective-permute-start.22 = (f32[2,2,2,24,1024]{4,3,2,1,0:T(8,128)}, f32[2,2,2,24,1024]{4,3,2,1,0:T(8,128)}, u32[]{:S(2)}, u32[]{:S(2)}) collective-permute-start(f32[2,2,2,24,1024]{4,3,2,1,0:T(8,128)} %get-tuple-element.148.refs_9_), channel_id=1, source_target_pairs={{0,8},{2,10},{4,12},{6,14},{8,0},{10,2},{12,4},{14,6},{16,24},{18,... | collective-permute-start | bytes 2359304 | tf_op jit(solution)/shard_map/ppermute | solution.py:464
  161.2 25.2 %collective-permute-start.23 = (f32[2,24,3072]{2,1,0:T(8,128)}, f32[2,24,3072]{2,1,0:T(8,128)}, u32[]{:S(2)}, u32[]{:S(2)}) collective-permute-start(f32[2,24,3072]{2,1,0:T(8,128)} %get-tuple-element.150.refs_9_), channel_id=1, source_target_pairs={{0,1},{1,0},{2,3},{3,2},{4,5},{5,4},{6,7},{7,6},{8,9},{9,8},{10,11... | collective-permute-start | bytes 1769480 | tf_op jit(solution)/shard_map/ppermute | solution.py:464
  173.9 23.4 %collective-permute-start.19 = (f32[96,1280]{1,0:T(8,128)}, f32[96,1280]{1,0:T(8,128)}, u32[]{:S(2)}, u32[]{:S(2)}) collective-permute-start(f32[96,1280]{1,0:T(8,128)} %get-tuple-element.154.refs_4_), channel_id=1, source_target_pairs={{0,16},{2,18},{4,20},{6,22},{8,24},{10,26},{12,28},{14,30},{16,0},... | collective-permute-start | bytes 1474568 | tf_op jit(solution)/shard_map/ppermute | solution.py:464
  192.0 11.3 %collective-permute-start.25 = (f32[2,2,24,1024]{3,2,1,0:T(8,128)}, f32[2,2,24,1024]{3,2,1,0:T(8,128)}, u32[]{:S(2)}, u32[]{:S(2)}) collective-permute-start(f32[2,2,24,1024]{3,2,1,0:T(8,128)} %get-tuple-element.158.refs_2_), channel_id=1, source_target_pairs={{0,1},{1,0},{2,3},{3,2},{4,5},{5,4},{6,7},{7,6},{8,9},{9,8},{10,11... | collective-permute-start | bytes 1179656 | tf_op jit(solution)/shard_map/ppermute | solution.py:464
  193.6 12.9 %collective-permute-start.26 = (f32[2,2,24,1024]{3,2,1,0:T(8,128)}, f32[2,2,24,1024]{3,2,1,0:T(8,128)}, u32[]{:S(2)}, u32[]{:S(2)}) collective-permute-start(f32[2,2,24,1024]{3,2,1,0:T(8,128)} %get-tuple-element.160.refs_4_), channel_id=1, source_target_pairs={{0,8},{2,10},{4,12},{6,14},{8,0},{10,2},{12,4},{14,6},{16,24},{18,... | collective-permute-start | bytes 1179656 | tf_op jit(solution)/shard_map/ppermute | solution.py:464
  199.3 14.7 %collective-permute-start.24 = (f32[96,1280]{1,0:T(8,128)}, f32[96,1280]{1,0:T(8,128)}, u32[]{:S(2)}, u32[]{:S(2)}) collective-permute-start(f32[96,1280]{1,0:T(8,128)} %shard_map.325.refs_7_.refs_1_), channel_id=1, source_target_pairs={{0,1},{1,0},{2,3},{3,2},{4,5},{5,4},{6,7},{7,6},{8,9},{9,8},{10,11... | collective-permute-start | bytes 1474568 | tf_op jit(solution)/shard_map/ppermute | solution.py:464
  200.8 8.4 %collective-permute-start.27 = (f32[2,2,24,1024]{3,2,1,0:T(8,128)}, f32[2,2,24,1024]{3,2,1,0:T(8,128)}, u32[]{:S(2)}, u32[]{:S(2)}) collective-permute-start(f32[2,2,24,1024]{3,2,1,0:T(8,128)} %get-tuple-element.162.refs_6_), channel_id=1, source_target_pairs={{0,4},{2,6},{4,0},{6,2},{8,12},{10,14},{12,8},{14,10},{16,20},{18,... | collective-permute-start | bytes 1179656 | tf_op jit(solution)/shard_map/ppermute | solution.py:464
  201.6 16.2 %collective-permute-start.32 = (f32[24,3072]{1,0:T(8,128)}, f32[24,3072]{1,0:T(8,128)}, u32[]{:S(2)}, u32[]{:S(2)}) collective-permute-start(f32[24,3072]{1,0:T(8,128)} %get-tuple-element.156.refs_7_), channel_id=1, source_target_pairs={{0,16},{2,18},{4,20},{6,22},{8,24},{10,26},{12,28},{14,30},{16,0},... | collective-permute-start | bytes 884744 | tf_op jit(solution)/shard_map/ppermute | solution.py:464
  211.8 7.8 %collective-permute-start.29 = (f32[2,24,1024]{2,1,0:T(8,128)}, f32[2,24,1024]{2,1,0:T(8,128)}, u32[]{:S(2)}, u32[]{:S(2)}) collective-permute-start(f32[2,24,1024]{2,1,0:T(8,128)} %get-tuple-element.164.refs_3_), channel_id=1, source_target_pairs={{0,8},{2,10},{4,12},{6,14},{8,0},{10,2},{12,4},{14,6},{16,24},{18,... | collective-permute-start | bytes 589832 | tf_op jit(solution)/shard_map/ppermute | solution.py:464
  211.9 7.7 %collective-permute-start.30 = (f32[2,24,1024]{2,1,0:T(8,128)}, f32[2,24,1024]{2,1,0:T(8,128)}, u32[]{:S(2)}, u32[]{:S(2)}) collective-permute-start(f32[2,24,1024]{2,1,0:T(8,128)} %get-tuple-element.166.refs_5_), channel_id=1, source_target_pairs={{0,4},{2,6},{4,0},{6,2},{8,12},{10,14},{12,8},{14,10},{16,20},{18,... | collective-permute-start | bytes 589832 | tf_op jit(solution)/shard_map/ppermute | solution.py:464
  213.1 6.6 %collective-permute-start.31 = (f32[2,24,1024]{2,1,0:T(8,128)}, f32[2,24,1024]{2,1,0:T(8,128)}, u32[]{:S(2)}, u32[]{:S(2)}) collective-permute-start(f32[2,24,1024]{2,1,0:T(8,128)} %get-tuple-element.168.refs_7_), channel_id=1, source_target_pairs={{0,1},{1,0},{2,3},{3,2},{4,5},{5,4},{6,7},{7,6},{8,9},{9,8},{10,11... | collective-permute-start | bytes 589832 | tf_op jit(solution)/shard_map/ppermute | solution.py:464
  216.0 9.4 %collective-permute-start.28 = (f32[192,256]{1,0:T(8,128)}, f32[192,256]{1,0:T(8,128)S(1)}, u32[]{:S(2)}, u32[]{:S(2)}) collective-permute-start(f32[192,256]{1,0:T(8,128)} %get-tuple-element.170.refs_0_), channel_id=1, source_target_pairs={{0,4},{2,6},{4,0},{6,2},{8,12},{10,14},{12,8},{14,10},{16,20},{18,... | collective-permute-start | bytes 589832 | tf_op jit(solution)/shard_map/ppermute | solution.py:464
  221.9 17.7 %collective-permute-start.36 = (f32[24,3072]{1,0:T(8,128)}, f32[24,3072]{1,0:T(8,128)}, u32[]{:S(2)}, u32[]{:S(2)}) collective-permute-start(f32[24,3072]{1,0:T(8,128)} %get-tuple-element.172.refs_2_), channel_id=1, source_target_pairs={{0,16},{2,18},{4,20},{6,22},{8,24},{10,26},{12,28},{14,30},{16,0},... | collective-permute-start | bytes 884744 | tf_op jit(solution)/shard_map/ppermute | solution.py:464
  225.4 0.7 copy-start
  227.8 9.3 %collective-permute-start.33 = (f32[192,256]{1,0:T(8,128)}, f32[192,256]{1,0:T(8,128)S(1)}, u32[]{:S(2)}, u32[]{:S(2)}) collective-permute-start(f32[192,256]{1,0:T(8,128)} %shard_map.330.refs_0_.refs_2_), channel_id=1, source_target_pairs={{0,8},{2,10},{4,12},{6,14},{8,0},{10,2},{12,4},{14,6},{16,24},{18,... | collective-permute-start | bytes 589832 | tf_op jit(solution)/shard_map/ppermute | solution.py:464
  228.0 14.0 %collective-permute-start.35 = (f32[24,3072]{1,0:T(8,128)}, f32[24,3072]{1,0:T(8,128)}, u32[]{:S(2)}, u32[]{:S(2)}) collective-permute-start(f32[24,3072]{1,0:T(8,128)} %shard_map.328.refs_7_.refs_1_), channel_id=1, source_target_pairs={{0,1},{1,0},{2,3},{3,2},{4,5},{5,4},{6,7},{7,6},{8,9},{9,8},{10,11... | collective-permute-start | bytes 884744 | tf_op jit(solution)/shard_map/ppermute | solution.py:464
  237.1 0.7 copy-start.1
  241.3 7.0 %collective-permute-start.37 = (f32[24,3072]{1,0:T(8,128)}, f32[24,3072]{1,0:T(8,128)}, u32[]{:S(2)}, u32[]{:S(2)}) collective-permute-start(f32[24,3072]{1,0:T(8,128)} %shard_map.332.refs_3_.refs_1_), channel_id=1, source_target_pairs={{0,1},{1,0},{2,3},{3,2},{4,5},{5,4},{6,7},{7,6},{8,9},{9,8},{10,11... | collective-permute-start | bytes 884744 | tf_op jit(solution)/shard_map/ppermute | solution.py:464
  242.1 1.9 collective-permute-start.34
  244.0 0.7 copy-start.2
